TPU v7x, 32 devices: a whole 2x2x4 slice. The times are simulated.
32 devices in a mesh: dp: 8 (over z, x), mp: 4 (over y, core).
Axes of the slice: x: 2, y: 2, z: 4, core: 2. Of those that a mesh axis runs over, the one named last changes fastest.
Arguments:
- tokens: bfloat16 [16384, 768], P('dp'), may hold values from -6 to 6
- out_grad: bfloat16 [16384, 768], P('dp'), may hold values from -6 to 6
- w_qkv: bfloat16 [768, 3, 768], P('dp', None, 'mp'), may hold values from -0.21875 to 0.21875
- w_out: bfloat16 [768, 768], P('mp', 'dp'), may hold values from -3.5 to 3.5
- w_gu: bfloat16 [768, 2, 1152], P('dp', None, 'mp'), may hold values from -0.21875 to 0.21875
- w_down: bfloat16 [1152, 768], P('mp', 'dp'), may hold values from -0.1875 to 0.1875
- gain_attn: bfloat16 [768], P('dp'), may hold values from 0.25 to 1.75
- gain_mlp: bfloat16 [768], P('dp'), may hold values from 0.25 to 1.75
- doc_lengths: int32 [8, 8], P('dp'), may hold values from 0 to 2048, as said below
Outputs:
- layer_out: bfloat16 [16384, 768], P('dp')
- input_grad: float32 [16384, 768], P('dp')
- grad_w_qkv: float32 [768, 3, 768], P('dp', None, 'mp')
- grad_w_out: float32 [768, 768], P('mp', 'dp')
- grad_w_gu: float32 [768, 2, 1152], P('dp', None, 'mp')
- grad_w_down: float32 [1152, 768], P('mp', 'dp')
- grad_gain_attn: float32 [768], P('dp')
- grad_gain_mlp: float32 [768], P('dp')
Inputs may be any that keep to these rules, and one draw needn't show every extreme that they name: `doc_lengths`: each row of a group's lengths sums to between 1024 and 2048; the token slots after that sum are padding. Lengths may be zero. In every draw one group holds a single document of exactly 2048 tokens.
All inputs are finite; a program needn't handle non-finite values.
Results may differ from a plain program's by a relative error of at most 0.022.
Values may be sent and summed in bfloat16 or wider, within the bound.
A program may use at most 128 MiB of HBM per device.

v0:
```python
import jax
import jax.numpy as jnp
from jax import lax
from jax.sharding import PartitionSpec as P

HDIM = 64
QBLK = 512


epsilon = 1e-05
rope_base = 160000.0


def layout(lengths, tok_rows):
    doc_ends = jnp.cumsum(lengths, dtype=jnp.int32)
    row_index = jnp.arange(tok_rows, dtype=jnp.int32)
    past_end = row_index[:, None] >= doc_ends[None, :]
    segment = jnp.sum(past_end.astype(jnp.int32), axis=1, dtype=jnp.int32)
    doc_start = jnp.max(jnp.where(past_end, doc_ends[None, :], 0), axis=1)
    return (segment, row_index - doc_start, row_index < doc_ends[-1])


def tables(position):
    half_dim = HDIM // 2
    frequency = rope_base ** (-(jnp.arange(half_dim, dtype=jnp.float32) * (2.0 / HDIM)))
    angles = position.astype(jnp.float32)[:, None] * frequency[None, :]
    cosine_table = jnp.concatenate([jnp.cos(angles), jnp.cos(angles)], axis=1)
    sine_table = jnp.concatenate([jnp.sin(angles), jnp.sin(angles)], axis=1)
    return (cosine_table, sine_table)


def rotate(vectors, cosine_table, sine_table):
    half_dim = vectors.shape[-1] // 2
    turned = jnp.concatenate([-vectors[..., half_dim:], vectors[..., :half_dim]], axis=-1)
    return vectors * cosine_table[:, None, :] + turned * sine_table[:, None, :]


def rotate_back(vectors, cosine_table, sine_table):
    half_dim = vectors.shape[-1] // 2
    scaled = vectors * sine_table[:, None, :]
    turned = jnp.concatenate([scaled[..., half_dim:], -scaled[..., :half_dim]], axis=-1)
    return vectors * cosine_table[:, None, :] + turned


def layer_norm(vectors, gain):
    row_mean = jnp.mean(vectors, axis=-1, keepdims=True)
    centered = vectors - row_mean
    row_var = jnp.mean(centered * centered, axis=-1, keepdims=True)
    return centered * lax.rsqrt(row_var + epsilon) * gain


def geglu(gate_up):
    return jax.nn.gelu(gate_up[:, 0], approximate=False) * gate_up[:, 1]


def per_device(tokens, out_grad, w_qkv, w_out, w_gu, w_down, gain_attn, gain_mlp, doc_lengths):
    tok_rows = tokens.shape[0]
    score_scale = HDIM ** (-0.5)
    full_qkv, full_out, full_gu, full_down, attn_gain, mlp_gain = (
        lax.all_gather(w_qkv, "dp", axis=0, tiled=True),
        lax.all_gather(w_out, "dp", axis=1, tiled=True),
        lax.all_gather(w_gu, "dp", axis=0, tiled=True),
        lax.all_gather(w_down, "dp", axis=1, tiled=True),
        lax.all_gather(gain_attn, "dp", axis=0, tiled=True),
        lax.all_gather(gain_mlp, "dp", axis=0, tiled=True),
    )
    segment, position, live_rows = layout(doc_lengths[0], tok_rows)
    cosine_table, sine_table = tables(position)
    local_heads = full_qkv.shape[2] // HDIM
    block_count = tok_rows // QBLK
    inputs = tokens.astype(jnp.float32)
    gain_first = attn_gain.astype(jnp.float32)
    normed_one = layer_norm(inputs, gain_first).astype(jnp.bfloat16)
    proj_qkv = jnp.einsum("td,dcf->tcf", normed_one, full_qkv, preferred_element_type=jnp.float32)
    shaped = proj_qkv.reshape(tok_rows, 3, local_heads, HDIM)
    queries = rotate(shaped[:, 0], cosine_table, sine_table).astype(jnp.bfloat16)
    keys_rot = rotate(shaped[:, 1], cosine_table, sine_table).astype(jnp.bfloat16)
    values = shaped[:, 2].astype(jnp.bfloat16)

    def block_scores(block_id):
        first_row = block_id * QBLK
        q_block = lax.dynamic_slice_in_dim(queries, first_row, QBLK, 0)
        seg_block = lax.dynamic_slice_in_dim(segment, first_row, QBLK, 0)
        scores = (
            jnp.einsum("qhe,khe->hqk", q_block, keys_rot, preferred_element_type=jnp.float32)
            * score_scale
        )
        masked = jnp.where((seg_block[:, None] == segment[None, :])[None], scores, -jnp.inf)
        return (q_block, masked)

    def attend(block_id):
        q_block, masked = block_scores(block_id)
        row_top = jnp.max(masked, axis=2, keepdims=True)
        exp_terms = jnp.exp(masked - row_top)
        row_total = jnp.sum(exp_terms, axis=2, keepdims=True)
        prob_rows = (exp_terms / row_total).astype(jnp.bfloat16)
        head_out = jnp.einsum("hqk,khe->qhe", prob_rows, values, preferred_element_type=jnp.float32)
        return (head_out.astype(jnp.bfloat16), (row_top + jnp.log(row_total))[:, :, 0])

    head_blocks, log_blocks = lax.map(attend, jnp.arange(block_count, dtype=jnp.int32))
    attn_rows = head_blocks.reshape(tok_rows, local_heads * HDIM)
    attn_part = jnp.dot(attn_rows, full_out, preferred_element_type=jnp.float32)
    attn_sum = lax.psum(attn_part.astype(jnp.bfloat16), "mp").astype(jnp.float32)
    middle = inputs + attn_sum
    gain_second = mlp_gain.astype(jnp.float32)
    normed_two = layer_norm(middle, gain_second).astype(jnp.bfloat16)
    gate_up = jnp.einsum("td,dcf->tcf", normed_two, full_gu, preferred_element_type=jnp.float32)
    hidden = geglu(gate_up).astype(jnp.bfloat16)
    mlp_part = jnp.dot(hidden, full_down, preferred_element_type=jnp.float32)
    mlp_sum = lax.psum(mlp_part.astype(jnp.bfloat16), "mp").astype(jnp.float32)
    layer_out = (middle + mlp_sum).astype(jnp.bfloat16)
    out_cot = out_grad.astype(jnp.float32) * live_rows[:, None].astype(jnp.float32)
    branch_cot = out_cot.astype(jnp.bfloat16)
    grad_down = jnp.einsum("tf,td->fd", hidden, branch_cot, preferred_element_type=jnp.float32)
    hidden_cot = jnp.einsum("td,fd->tf", branch_cot, full_down, preferred_element_type=jnp.float32)
    gate_up_cot = jax.vjp(geglu, gate_up)[1](hidden_cot)[0].astype(jnp.bfloat16)
    grad_gu = jnp.einsum("td,tcf->dcf", normed_two, gate_up_cot, preferred_element_type=jnp.float32)
    normed_two_part = jnp.einsum(
        "tcf,dcf->td", gate_up_cot, full_gu, preferred_element_type=jnp.float32
    )
    normed_two_cot = lax.psum(normed_two_part.astype(jnp.bfloat16), "mp").astype(jnp.float32)
    middle_back, gain_second_grad = jax.vjp(layer_norm, middle, gain_second)[1](normed_two_cot)
    middle_cot = out_cot + middle_back
    attn_cot = middle_cot.astype(jnp.bfloat16)
    grad_out = jnp.einsum("tf,td->fd", attn_rows, attn_cot, preferred_element_type=jnp.float32)
    rows_cot = jnp.einsum("td,fd->tf", attn_cot, full_out, preferred_element_type=jnp.float32)
    rows_cot = rows_cot.astype(jnp.bfloat16).reshape(tok_rows, local_heads, HDIM)

    def attend_back(carried, block_id):
        key_cot, value_cot = carried
        q_block, masked = block_scores(block_id)
        cot_block = lax.dynamic_slice_in_dim(rows_cot, block_id * QBLK, QBLK, 0)
        prob_rows = jnp.exp(masked - log_blocks[block_id][:, :, None])
        prob_cot = jnp.einsum("qhe,khe->hqk", cot_block, values, preferred_element_type=jnp.float32)
        row_inner = jnp.sum(prob_rows * prob_cot, axis=2, keepdims=True)
        score_cot = (prob_rows * (prob_cot - row_inner)).astype(jnp.bfloat16)
        query_cot = (
            jnp.einsum("hqk,khe->qhe", score_cot, keys_rot, preferred_element_type=jnp.float32)
            * score_scale
        )
        key_cot = (
            key_cot
            + jnp.einsum("hqk,qhe->khe", score_cot, q_block, preferred_element_type=jnp.float32)
            * score_scale
        )
        value_cot = value_cot + jnp.einsum(
            "hqk,qhe->khe",
            prob_rows.astype(jnp.bfloat16),
            cot_block,
            preferred_element_type=jnp.float32,
        )
        return ((key_cot, value_cot), query_cot)

    zero_rows = jnp.zeros((tok_rows, local_heads, HDIM), jnp.float32)
    (key_cot, value_cot), query_blocks = lax.scan(
        attend_back, (zero_rows, zero_rows), jnp.arange(block_count, dtype=jnp.int32)
    )
    query_cot = query_blocks.reshape(tok_rows, local_heads, HDIM)
    qkv_cot = jnp.stack(
        [
            rotate_back(query_cot, cosine_table, sine_table),
            rotate_back(key_cot, cosine_table, sine_table),
            value_cot,
        ],
        axis=1,
    )
    qkv_cot = qkv_cot.reshape(tok_rows, 3, local_heads * HDIM).astype(jnp.bfloat16)
    grad_qkv = jnp.einsum("td,tcf->dcf", normed_one, qkv_cot, preferred_element_type=jnp.float32)
    normed_one_part = jnp.einsum(
        "tcf,dcf->td", qkv_cot, full_qkv, preferred_element_type=jnp.float32
    )
    normed_one_cot = lax.psum(normed_one_part.astype(jnp.bfloat16), "mp").astype(jnp.float32)
    input_back, gain_first_grad = jax.vjp(layer_norm, inputs, gain_first)[1](normed_one_cot)
    input_cot = middle_cot + input_back
    grad_qkv_part, grad_out_part, grad_gu_part, grad_down_part, attn_gain_part, mlp_gain_part = (
        lax.psum_scatter(grad_qkv, "dp", scatter_dimension=0, tiled=True),
        lax.psum_scatter(grad_out, "dp", scatter_dimension=1, tiled=True),
        lax.psum_scatter(grad_gu, "dp", scatter_dimension=0, tiled=True),
        lax.psum_scatter(grad_down, "dp", scatter_dimension=1, tiled=True),
        lax.psum_scatter(gain_first_grad, "dp", scatter_dimension=0, tiled=True),
        lax.psum_scatter(gain_second_grad, "dp", scatter_dimension=0, tiled=True),
    )
    return (
        layer_out,
        input_cot,
        grad_qkv_part,
        grad_out_part,
        grad_gu_part,
        grad_down_part,
        attn_gain_part,
        mlp_gain_part,
    )


def solution(mesh):
    return jax.shard_map(
        per_device,
        mesh=mesh,
        in_specs=(
            P("dp", None),
            P("dp", None),
            P("dp", None, "mp"),
            P("mp", "dp"),
            P("dp", None, "mp"),
            P("mp", "dp"),
            P("dp"),
            P("dp"),
            P("dp", None),
        ),
        out_specs=(
            P("dp", None),
            P("dp", None),
            P("dp", None, "mp"),
            P("mp", "dp"),
            P("dp", None, "mp"),
            P("mp", "dp"),
            P("dp"),
            P("dp"),
        ),
        check_vma=False,
    )
```

profile of v0, /device:TPU:0, one launch (start us, length us, event | category | flops | bytes accessed | tf_op | source)
XLA Modules:
  0.0 821.5 jit_solution(606801633420478469)
XLA Ops:
  11.7 23.7 %all-reduce.7 = (bf16[768]{0:T(1024)(128)(2,1)S(1)}, bf16[768]{0:T(1024)(128)(2,1)}) all-reduce(bf16[768]{0:T(1024)(128)(2,1)S(1)} %dynamic-update-slice, bf16[768]{0:T(1024)(128)(2,1)S(1)} %dynamic-update-slice.1), channel_id=1, replica_groups=mesh['dp'=8,'mp'=4] {'dp'}, use_global_device_ids=true, to_apply=%add.2 | all-reduce | flops 1536 | bytes 6144
  39.5 36.5 %all_gather.19 = bf16[768,3,192]{2,1,0:T(4,128)(2,1)} all-gather(bf16[96,3,192]{2,1,0:T(4,128)(2,1)S(1)} %copy.48), channel_id=1, replica_groups=mesh['dp'=8,'mp'=4] {'dp'}, dimensions={0}, use_global_device_ids=true | all-gather | bytes 995328 | tf_op jit(solution)/shard_map/all_gather | solution.py:60
  88.7 32.0 %all_gather.20 = bf16[192,768]{0,1:T(8,128)(2,1)S(1)} all-gather(bf16[192,96]{0,1:T(8,128)(2,1)} %copy.51), channel_id=1, replica_groups=mesh['dp'=8,'mp'=4] {'dp'}, dimensions={1}, use_global_device_ids=true | all-gather | bytes 331776 | tf_op jit(solution)/shard_map/all_gather | solution.py:61
  127.7 99.7 %while.27 = (s32[]{:T(128)}, bf16[4,512,3,64]{1,3,2,0:T(8,128)(2,1)}, f32[4,3,512]{2,1,0:T(4,128)}, s32[4]{0:T(128)S(1)}, s32[2048]{0:T(1024)S(1)}, /*index=5*/b...) while((s32[]{:T(128)}, ...), condition=%wide.region_8.9_spmd, body=%wide.region_5.8_spmd.sunk | while | flops 844200448 | bytes 47120612 | solution.py:100
  129.7 8.1 fusion.148
  137.8 6.8 fusion.149
  144.7 7.4 fusion.150
  154.6 8.1 fusion.148
  162.7 6.8 fusion.149
  169.6 7.4 fusion.150
  179.5 8.1 fusion.148
  187.7 6.8 fusion.149
  194.5 7.4 fusion.150
  204.4 8.1 fusion.148
  212.6 6.8 fusion.149
  219.4 7.4 fusion.150
  236.5 32.0 %all_gather.23 = bf16[288,768]{0,1:T(8,128)(2,1)S(1)} all-gather(bf16[288,96]{0,1:T(8,128)(2,1)} %copy.53), channel_id=1, replica_groups=mesh['dp'=8,'mp'=4] {'dp'}, dimensions={1}, use_global_device_ids=true | all-gather | bytes 497664 | tf_op jit(solution)/shard_map/all_gather | solution.py:63
  274.0 34.7 %all_gather.22 = bf16[768,2,288]{2,1,0:T(2,128)(2,1)} all-gather(bf16[96,2,288]{2,1,0:T(2,128)(2,1)S(1)} %copy-done.41), channel_id=1, replica_groups=mesh['dp'=8,'mp'=4] {'dp'}, dimensions={0}, use_global_device_ids=true | all-gather | bytes 995328 | tf_op jit(solution)/shard_map/all_gather | solution.py:62
  335.1 61.7 %all-reduce.15.cloned.1.call-done = bf16[2048,768]{1,0:T(8,128)(2,1)} async-done(((bf16[2048,768]{1,0:T(8,128)(2,1)}), bf16[2048,768]{1,0:T(8,128)(2,1)}) %all-reduce.15.cloned.1.call-update) | async-done | bytes 3145744 | tf_op jit(solution)/shard_map/psum | solution.py:121
  396.8 6.5 fusion.46
  427.8 175.6 %while.28 = (s32[]{:T(128)}, f32[2048,3,64]{0,2,1:T(8,128)}, f32[2048,3,64]{0,2,1:T(8,128)}, f32[4,512,3,64]{1,0,3,2:T(4,128)}, s32[4]{0:T(128)S(1)}, /*index=5*...) while((s32[]{:T(128)}, f32[2048,3,64]{0,2,1:T(8,128)}, ...), condition=%wide.region_18.19_spmd.clone, body=%wide.region_16.18_spmd.clone.sunk | while | flops 2063563264 | bytes 142532976 | solution.py:155
  462.4 8.6 %dynamic_update_slice.20 = f32[4,512,3,64]{1,0,3,2:T(4,128)} dynamic-update-slice(f32[4,512,3,64]{1,0,3,2:T(4,128)} %get-tuple-element.446, f32[1,512,3,64]{1,0,3,2:T(1,128)S(1)} %copy.89, s32[]{:T(128)S(6)} %copy.110, s32[]{:T(128)} %constant.73.clone.1..sunk.1, s32[]{:T(128)} %constant.73.clone.1..sunk.1, s32[]{:T(128)} %constant.73.clone.1..sunk.1) | dynamic-update-slice | bytes 786436 | tf_op jit(solution)/shard_map/while/body/jit(dynamic_update_index_in_dim)/dynamic_update_slice | solution.py:155
  478.7 6.3 fusion.162
  506.4 8.6 %dynamic_update_slice.20 = f32[4,512,3,64]{1,0,3,2:T(4,128)} dynamic-update-slice(f32[4,512,3,64]{1,0,3,2:T(4,128)} %get-tuple-element.446, f32[1,512,3,64]{1,0,3,2:T(1,128)S(1)} %copy.89, s32[]{:T(128)S(6)} %copy.110, s32[]{:T(128)} %constant.73.clone.1..sunk.1, s32[]{:T(128)} %constant.73.clone.1..sunk.1, s32[]{:T(128)} %constant.73.clone.1..sunk.1) | dynamic-update-slice | bytes 786436 | tf_op jit(solution)/shard_map/while/body/jit(dynamic_update_index_in_dim)/dynamic_update_slice | solution.py:155
  522.7 6.3 fusion.162
  550.4 8.6 %dynamic_update_slice.20 = f32[4,512,3,64]{1,0,3,2:T(4,128)} dynamic-update-slice(f32[4,512,3,64]{1,0,3,2:T(4,128)} %get-tuple-element.446, f32[1,512,3,64]{1,0,3,2:T(1,128)S(1)} %copy.89, s32[]{:T(128)S(6)} %copy.110, s32[]{:T(128)} %constant.73.clone.1..sunk.1, s32[]{:T(128)} %constant.73.clone.1..sunk.1, s32[]{:T(128)} %constant.73.clone.1..sunk.1) | dynamic-update-slice | bytes 786436 | tf_op jit(solution)/shard_map/while/body/jit(dynamic_update_index_in_dim)/dynamic_update_slice | solution.py:155
  594.6 8.6 %dynamic_update_slice.20 = f32[4,512,3,64]{1,0,3,2:T(4,128)} dynamic-update-slice(f32[4,512,3,64]{1,0,3,2:T(4,128)} %get-tuple-element.446, f32[1,512,3,64]{1,0,3,2:T(1,128)S(1)} %copy.89, s32[]{:T(128)S(6)} %copy.110, s32[]{:T(128)} %constant.73.clone.1..sunk.1, s32[]{:T(128)} %constant.73.clone.1..sunk.1, s32[]{:T(128)} %constant.73.clone.1..sunk.1) | dynamic-update-slice | bytes 786436 | tf_op jit(solution)/shard_map/while/body/jit(dynamic_update_index_in_dim)/dynamic_update_slice | solution.py:155
  622.4 6.3 fusion.56
  634.6 106.0 %all-reduce.17.cloned.1.call-done = (bf16[2048,768]{1,0:T(8,128)(2,1)}, bf16[2048,768]{1,0:T(8,128)(2,1)}) async-done(((bf16[2048,768]{1,0:T(8,128)(2,1)}, bf16[2048,768]{1,0:T(8,128)(2,1)}), (bf16[2048,768]{1,0:T(8,128)(2,1)}, bf16[2048,768]{1,0:T(8,128)(2,1)})) %all-reduce.17.cloned.1.call-update) | async-done | bytes 6291472 | tf_op jit(solution)/shard_map/psum | solution.py:110
  747.7 21.9 %all-reduce.6 = (f32[768]{0:T(1024)S(1)}, f32[768]{0:T(1024)S(1)}) all-reduce(f32[768]{0:T(1024)S(1)} %get-tuple-element.185, f32[768]{0:T(1024)S(1)} %copy-done.64), channel_id=6, replica_groups=mesh['dp'=8,'mp'=4] {'dp'}, use_global_device_ids=true, to_apply=%region_27.28.clone | all-reduce | flops 1536 | bytes 12288
  770.8 12.6 %add_add_fusion.2 = (f32[2048,768]{1,0:T(8,128)}, bf16[2048,768]{1,0:T(8,128)(2,1)}) fusion(bf16[2048,768]{1,0:T(8,128)(2,1)S(1)} %copy-done.3, bf16[2048,768]{1,0:T(8,128)(2,1)} %get-tuple-element.232, f32[2048,768]{1,0:T(8,128)} %copy-done.10, bf16[2048,768]{1,0:T(8,128)(2,1)} %param.14, f32[2048]{0:T(1024)S(1)} %negate_multiply_fusion.1, ...), kind=kLoop, calls=%fused_computation.68 | loop fusion | flops 29884416 | bytes 31509504 | tf_op jit(solution)/shard_map/add | solution.py:174
  783.5 31.0 %reduce-scatter.9.cloned.1.call-done = f32[96,3,192]{2,0,1:T(8,128)} async-done(((f32[768,3,192]{2,0,1:T(8,128)}), f32[96,3,192]{2,0,1:T(8,128)}) %reduce-scatter.9.cloned.1.call-update) | async-done | bytes 221200 | tf_op jit(solution)/shard_map/reduce_scatter | solution.py:176
  (314 shorter events, 249.9 us)
Async XLA Ops:
  7.2 30.7 %copy-start.2 = (bf16[2048,768]{1,0:T(8,128)(2,1)S(1)}, bf16[2048,768]{1,0:T(8,128)(2,1)}, u32[]{:S(2)}) copy-start(bf16[2048,768]{1,0:T(8,128)(2,1)} %param.13) | copy-start | bytes 9437188
  7.2 301.5 %all-reduce.13.cloned.1.call-start = ((), (), s32[]{:S(2)}) async-start(), calls=%async_computation.4 | async-start | bytes 6291456 | tf_op jit(solution)/shard_map/psum | solution.py:103
  35.4 44.0 %copy-start.58 = (f32[768]{0:T(1024)}, f32[768]{0:T(1024)S(1)}, u32[]{:S(2)}) copy-start(f32[768]{0:T(1024)S(1)} %convert_element_type.106) | copy-start | bytes 9220
  37.8 41.5 %copy-start.38 = (f32[2048]{0:T(1024)}, f32[2048]{0:T(1024)S(1)}, u32[]{:S(2)}) copy-start(f32[2048]{0:T(1024)S(1)} %broadcast_multiply_fusion.3) | copy-start | bytes 24580
  38.9 43.8 %copy-start.47 = (f32[2048]{0:T(1024)}, f32[2048]{0:T(1024)S(1)}, u32[]{:S(2)}) copy-start(f32[2048]{0:T(1024)S(1)} %fusion.94) | copy-start | bytes 24580
  88.7 33.8 %copy-start.23 = (f32[2048,3,64]{0,2,1:T(8,128)S(1)}, f32[2048,3,64]{0,2,1:T(8,128)}, u32[]{:S(2)}) copy-start(f32[2048,3,64]{0,2,1:T(8,128)} %get-tuple-element.245) | copy-start | bytes 4718596
  137.8 6.8 copy-start.11
  162.7 6.8 copy-start.11
  187.7 6.8 copy-start.11
  212.6 6.8 copy-start.11
  233.0 163.8 %all-reduce.15.cloned.1.call-start = ((), (), s32[]{:S(2)}) async-start(), calls=%async_computation.5 | async-start | bytes 6291456 | tf_op jit(solution)/shard_map/psum | solution.py:121
  236.5 170.2 %copy-start.42 = (f32[2048]{0:T(1024)}, f32[2048]{0:T(1024)S(1)}, u32[]{:S(2)}) copy-start(f32[2048]{0:T(1024)S(1)} %fusion.93) | copy-start | bytes 24580
  329.4 300.0 %reduce-scatter.15.cloned.1.call-start = ((), (), s32[]{:S(2)}) async-start(), calls=%async_computation.9 | async-start | bytes 1327104
  334.8 296.3 %reduce-scatter.13.cloned.1.call-start = ((), (), s32[]{:S(2)}) async-start(), calls=%async_computation.8 | async-start | bytes 884736
  396.8 6.5 copy-start.57
  396.8 6.5 copy-start.7
  396.8 6.6 copy-start.15
  396.8 6.6 copy-start.45
  396.8 6.6 copy-start.52
  396.8 6.6 copy-start.62
  413.2 5.2 copy-start.46
  413.2 219.5 %reduce-scatter.11.cloned.1.call-start = ((), (), s32[]{:S(2)}) async-start(), calls=%async_computation.7 | async-start | bytes 2654208 | tf_op jit(solution)/shard_map/reduce_scatter | solution.py:178
  413.3 5.1 copy-start.8
  423.6 317.0 %all-reduce.17.cloned.1.call-start = ((), (), s32[]{:S(2)}) async-start(), calls=%async_computation.10 | async-start | bytes 12582912 | tf_op jit(solution)/shard_map/psum | solution.py:110
  458.5 12.5 %copy-start.5 = (bf16[2048,3,64]{0,2,1:T(8,128)(2,1)S(1)}, bf16[2048,3,64]{0,2,1:T(8,128)(2,1)}, u32[]{:S(2)}) copy-start(bf16[2048,3,64]{0,2,1:T(8,128)(2,1)} %get-tuple-element.502) | copy-start | bytes 2359300 | tf_op jit(solution)/shard_map/while
  502.0 13.1 %copy-start.5 = (bf16[2048,3,64]{0,2,1:T(8,128)(2,1)S(1)}, bf16[2048,3,64]{0,2,1:T(8,128)(2,1)}, u32[]{:S(2)}) copy-start(bf16[2048,3,64]{0,2,1:T(8,128)(2,1)} %get-tuple-element.502) | copy-start | bytes 2359300 | tf_op jit(solution)/shard_map/while
  545.9 13.1 %copy-start.5 = (bf16[2048,3,64]{0,2,1:T(8,128)(2,1)S(1)}, bf16[2048,3,64]{0,2,1:T(8,128)(2,1)}, u32[]{:S(2)}) copy-start(bf16[2048,3,64]{0,2,1:T(8,128)(2,1)} %get-tuple-element.502) | copy-start | bytes 2359300 | tf_op jit(solution)/shard_map/while
  584.9 5.3 copy-start
  590.2 13.1 %copy-start.5 = (bf16[2048,3,64]{0,2,1:T(8,128)(2,1)S(1)}, bf16[2048,3,64]{0,2,1:T(8,128)(2,1)}, u32[]{:S(2)}) copy-start(bf16[2048,3,64]{0,2,1:T(8,128)(2,1)} %get-tuple-element.502) | copy-start | bytes 2359300 | tf_op jit(solution)/shard_map/while
  620.6 193.9 %reduce-scatter.9.cloned.1.call-start = ((), (), s32[]{:S(2)}) async-start(), calls=%async_computation.6 | async-start | bytes 2654208 | tf_op jit(solution)/shard_map/reduce_scatter | solution.py:176
  744.0 26.9 %copy-start.43 = (f32[2048]{0:T(1024)S(1)}, f32[2048]{0:T(1024)}, u32[]{:S(2)}) copy-start(f32[2048]{0:T(1024)} %copy-done.42) | copy-start | bytes 24580
  744.0 26.9 %copy-start.50 = (f32[2048]{0:T(1024)S(1)}, f32[2048]{0:T(1024)}, u32[]{:S(2)}) copy-start(f32[2048]{0:T(1024)} %copy-done.49) | copy-start | bytes 24580
  (56 other events, 158.9 us)
Sparse Core Ops, SparseCore 0:
  233.1 67.4 all-reduce.12
  329.5 67.2 all-reduce.14
  400.2 64.1 reduce-scatter.14
  467.5 61.4 reduce-scatter.12
  532.8 67.9 reduce-scatter.10
  620.7 119.8 all-reduce.16
  745.1 69.3 reduce-scatter.8
where the time goes:
time: 828 us; the launch traced here: 822 us
  matrix products  208 us (25%)
  waiting for transfers between devices  199 us (24%)
  blocking collectives  181 us (22%)
  other arithmetic  118 us (14%)
  local copies, waits for them, and re-layouts  85.7 us (10%)
  between operations  16.5 us (2%)
  loops' own time  13.9 us (2%)
    psum x1, waiting for transfers between devices, per_device(): mlp_sum = lax.psum(mlp_part.astype(jnp.bfloat16), 'mp').astype(jnp.float32)  106 us
    psum x1, waiting for transfers between devices, per_device(): lax.psum(normed_two_part.astype(jnp.bfloat16), 'mp').astype(jnp.float32)  61.7 us
    unnamed x2, blocking collectives  45.6 us
    dot_general x8, matrix products, block_scores(): jnp.einsum('qhe,khe->hqk', q_block, keys_rot, preferred_element_type=jnp....  44.5 us
    all_gather x1, blocking collectives, per_device(): lax.all_gather(w_qkv, 'dp', axis=0, tiled=True)  36.5 us
    dynamic_update_slice x8, local copies, waits for them, and re-layouts, per_device(): lax.scan(attend_back, (zero_rows, zero_rows), jnp.arange(block_count, dty...  36.1 us
    all_gather x1, blocking collectives, per_device(): lax.all_gather(w_gu, 'dp', axis=0, tiled=True)  34.7 us
    all_gather x1, blocking collectives, per_device(): lax.all_gather(w_down, 'dp', axis=1, tiled=True)  32 us
  transfers between devices with their start and end apart: 7, of which 3 were waited for; matrix products, arithmetic and copies ran while one was open for 31% of the time, Pallas kernels for 0%

commit v1 on v0

v1 whole, which is shorter than its diff:
```python
import functools
import math

import jax
import jax.numpy as jnp
from jax import lax
from jax.experimental import pallas as pl
from jax.experimental.pallas import tpu as pltpu
from jax.sharding import PartitionSpec as P

HDIM = 64
HALF = HDIM // 2
AUG = HDIM + 16
EPS = 1e-05
ROPE_BASE = 160000.0
LOG2E = math.log2(math.e)
LN2 = math.log(2.0)
SCALE = HDIM ** (-0.5)
FAR = -1e30
BF16 = jnp.bfloat16
F32 = jnp.float32
VMEM_BYTES = 60 << 20
NN = (((1,), (0,)), ((), ()))
NT = (((1,), (1,)), ((), ()))
TN = (((0,), (0,)), ((), ()))


def dot(a, b, dims):
    return lax.dot_general(a, b, dims, preferred_element_type=F32)


def params(*semantics):
    return pltpu.CompilerParams(
        dimension_semantics=semantics or None, vmem_limit_bytes=VMEM_BYTES
    )


def whole(*shape):
    return pl.BlockSpec(shape, lambda *i: (0,) * len(shape))


def layout_rows(len_ref, docs, first, rows):
    index = first + lax.broadcasted_iota(jnp.int32, (1, rows), 1)
    segment = jnp.zeros((1, rows), jnp.int32)
    start = jnp.zeros((1, rows), jnp.int32)
    end = jnp.int32(0)
    for j in range(docs):
        end = end + len_ref[0, j]
        past = index >= end
        segment = segment + jnp.where(past, 1, 0)
        start = jnp.where(past, jnp.maximum(start, end), start)
    return segment, index - start, index < end


def normalize(columns):
    mean = jnp.mean(columns, axis=0, keepdims=True)
    centered = columns - mean
    var = jnp.mean(centered * centered, axis=0, keepdims=True)
    inv = lax.rsqrt(var + EPS)
    return centered * inv, inv


def turn(block, cos, sin, heads, back=False):
    out = []
    for h in range(heads):
        one = block[h * HDIM : h * HDIM + HALF]
        two = block[h * HDIM + HALF : (h + 1) * HDIM]
        if back:
            out += [one * cos + two * sin, two * cos - one * sin]
        else:
            out += [one * cos - two * sin, two * cos + one * sin]
    return jnp.concatenate(out, axis=0)


def prep_kernel(own_axis, own, len_ref, tok_ref, gain_ref, w_ref, n1_ref, q_ref, k_ref, v_ref, cos_ref, sin_ref):
    features, rows = n1_ref.shape
    width = w_ref.shape[2] // 3
    heads = width // HDIM
    chunk = own

    @pl.when(pl.program_id(0) == 0)
    def _():
        gain = gain_ref[...]

        def norm(i, carry):
            at = pl.ds(pl.multiple_of(i * chunk, chunk), chunk)
            hat, _ = normalize(tok_ref[at, :].T.astype(F32))
            n1_ref[:, at] = (hat * gain).astype(BF16)
            return carry

        lax.fori_loop(0, rows // chunk, norm, 0)
        _, position, _ = layout_rows(len_ref, len_ref.shape[1], 0, rows)
        power = lax.broadcasted_iota(jnp.int32, (HALF, 1), 0).astype(F32) * (-2.0 / HDIM * math.log2(ROPE_BASE))
        angle = position.astype(F32) * jnp.exp2(power)
        cos_ref[...] = jnp.cos(angle)
        sin_ref[...] = jnp.sin(angle)

    def project(i, carry):
        at = pl.ds(pl.multiple_of(i * chunk, chunk), chunk)
        made = dot(w_ref[0, :, width:], n1_ref[:, at], TN)
        k_ref[:, at] = turn(made[:width], cos_ref[:, at], sin_ref[:, at], heads).astype(BF16)
        v_ref[:, at] = made[width:].astype(BF16)
        return carry

    lax.fori_loop(0, rows // chunk, project, 0)
    mine = pl.ds(pl.multiple_of(lax.axis_index(own_axis) * own, own), own)
    made = dot(w_ref[0, :, :width], n1_ref[:, mine], TN) * (SCALE * LOG2E)
    q_ref[...] = turn(made, cos_ref[:, mine], sin_ref[:, mine], heads).astype(BF16)


def prep(lengths, tokens, gain, w_qkv, n_mp, own_axis="mp"):
    rows, features = tokens.shape
    own = rows // n_mp
    width = w_qkv.shape[2] // 3
    return pl.pallas_call(
        functools.partial(prep_kernel, own_axis, own),
        grid=(n_mp,),
        in_specs=[
            pl.BlockSpec(memory_space=pltpu.SMEM),
            whole(rows, features),
            whole(features, 1),
            pl.BlockSpec((1,) + w_qkv.shape[1:], lambda m: (m, 0, 0)),
        ],
        out_specs=[
            whole(features, rows),
            pl.BlockSpec((width, own), lambda m: (m, 0)),
            pl.BlockSpec((width, rows), lambda m: (m, 0)),
            pl.BlockSpec((width, rows), lambda m: (m, 0)),
            whole(HALF, rows),
            whole(HALF, rows),
        ],
        out_shape=[
            jax.ShapeDtypeStruct((features, rows), BF16),
            jax.ShapeDtypeStruct((features, own), BF16),
            jax.ShapeDtypeStruct((features, rows), BF16),
            jax.ShapeDtypeStruct((features, rows), BF16),
            jax.ShapeDtypeStruct((HALF, rows), F32),
            jax.ShapeDtypeStruct((HALF, rows), F32),
        ],
        compiler_params=params("arbitrary"),
        name="prep",
    )(lengths, tokens, gain, w_qkv)


def attend_kernel(own_axis, len_ref, q_ref, k_ref, v_ref, o_ref, p_ref, inv_ref, ka_ref, qa_ref, va_ref):
    rows, own = k_ref.shape[1], q_ref.shape[1]
    docs = len_ref.shape[1]

    @pl.when(pl.program_id(0) == 0)
    def _():
        keys, _, _ = layout_rows(len_ref, docs, 0, rows)
        queries, _, _ = layout_rows(len_ref, docs, lax.axis_index(own_axis) * own, own)
        kind = lax.broadcasted_iota(jnp.int32, (AUG - HDIM, 1), 0)
        ka_ref[HDIM:] = jnp.where(kind == keys, 1.0, 0.0).astype(BF16)
        qa_ref[HDIM:] = jnp.where(kind == queries, 0.0, FAR).astype(BF16)
        va_ref[HDIM:] = jnp.ones((AUG - HDIM, rows), BF16)

    ka_ref[:HDIM] = k_ref[...]
    qa_ref[:HDIM] = q_ref[...]
    va_ref[:HDIM] = v_ref[...]
    step = 256
    for c in range(own // step):
        at = slice(c * step, (c + 1) * step)
        scores = dot(ka_ref[...], qa_ref[:, at], TN)
        top = jnp.max(scores, axis=0, keepdims=True)
        probs = jnp.exp2(scores - top).astype(BF16)
        p_ref[0, :, at] = probs
        out = dot(va_ref[...], probs, NN)
        inv = 1.0 / out[HDIM : HDIM + 1]
        o_ref[:, at] = (out[:HDIM] * inv).astype(BF16)
        inv_ref[0, :, at] = inv


def attend(lengths, q, k, v, own_axis="mp"):
    (features, own), rows = q.shape, k.shape[1]
    heads = features // HDIM
    return pl.pallas_call(
        functools.partial(attend_kernel, own_axis),
        grid=(heads,),
        in_specs=[
            pl.BlockSpec(memory_space=pltpu.SMEM),
            pl.BlockSpec((HDIM, own), lambda h: (h, 0)),
            pl.BlockSpec((HDIM, rows), lambda h: (h, 0)),
            pl.BlockSpec((HDIM, rows), lambda h: (h, 0)),
        ],
        out_specs=[
            pl.BlockSpec((HDIM, own), lambda h: (h, 0)),
            pl.BlockSpec((1, rows, own), lambda h: (h, 0, 0)),
            pl.BlockSpec((1, 1, own), lambda h: (h, 0, 0)),
        ],
        out_shape=[
            jax.ShapeDtypeStruct((features, own), BF16),
            jax.ShapeDtypeStruct((heads, rows, own), BF16),
            jax.ShapeDtypeStruct((heads, 1, own), F32),
        ],
        scratch_shapes=[
            pltpu.VMEM((AUG, rows), BF16),
            pltpu.VMEM((AUG, own), BF16),
            pltpu.VMEM((AUG, rows), BF16),
        ],
        compiler_params=params("arbitrary"),
        name="attend",
    )(lengths, q, k, v)


def gelu_parts(gate):
    phi = 0.5 * (1.0 + lax.erf(gate * math.sqrt(0.5)))
    density = jnp.exp2(gate * gate * (-0.5 * LOG2E)) * (1.0 / math.sqrt(2.0 * math.pi))
    return phi, gate * density


def mid_kernel(
    own_axis, len_ref, tok_ref, cot_ref, gain_ref, heads_ref, inv_ref, wo_ref, wg_ref, wd_ref,
    out_ref, mcot_ref, do_ref, go_ref, gg_ref, gd_ref, gain_cot_ref,
    up_ref, hid_ref,
):
    own, features = tok_ref.shape
    parts, _, width = wo_ref.shape
    units = wd_ref.shape[2]
    heads = width // HDIM
    _, _, live = layout_rows(len_ref, len_ref.shape[1], lax.axis_index(own_axis) * own, own)
    total = dot(wo_ref[0], heads_ref[:width], NN)
    for m in range(1, parts):
        total += dot(wo_ref[m], heads_ref[m * width : (m + 1) * width], NN)
    middle = tok_ref[...].T.astype(F32) + total
    gain = gain_ref[...]
    hat, inv_sigma = normalize(middle)
    normed = (hat * gain).astype(BF16)
    branch = jnp.where(live, cot_ref[...].T.astype(F32), 0.0).astype(BF16)
    total = middle
    back = jnp.zeros((features, own), F32)
    for m in range(parts):
        gate_up = dot(wg_ref[m], normed, TN)
        gate, up = gate_up[:units], gate_up[units:]
        phi, slope = gelu_parts(gate)
        act = gate * phi
        hidden = (act * up).astype(BF16)
        total += dot(wd_ref[m], hidden, NN)
        hidden_cot = dot(wd_ref[m], branch, TN)
        gd_ref[m] = dot(branch, hidden, NT).astype(BF16)
        cots = jnp.concatenate([hidden_cot * up * (phi + slope), hidden_cot * act], axis=0).astype(BF16)
        gg_ref[m] = dot(normed, cots, NT).astype(BF16)
        back += dot(wg_ref[m], cots, NN)
    out_ref[...] = total.astype(BF16).T
    gain_cot_ref[...] = jnp.sum(back * hat, axis=1, keepdims=True)
    d = back * gain
    middle_cot = branch.astype(F32) + inv_sigma * (
        d - jnp.mean(d, axis=0, keepdims=True) - hat * jnp.mean(d * hat, axis=0, keepdims=True)
    )
    mcot_ref[...] = middle_cot
    attn_cot = middle_cot.astype(BF16)
    for m in range(parts):
        part = heads_ref[m * width : (m + 1) * width]
        go_ref[m] = dot(attn_cot, part, NT).astype(BF16)
        back_heads = dot(wo_ref[m], attn_cot, TN)
        for h in range(heads):
            head = m * heads + h
            rows = slice(h * HDIM, (h + 1) * HDIM)
            inv = inv_ref[head]
            cot = back_heads[rows] * inv
            inner = jnp.sum(cot * part[rows].astype(F32), axis=0, keepdims=True)
            high = inner.astype(BF16).astype(F32)
            pad = jnp.zeros((AUG - HDIM - 2, own), F32)
            do_ref[head] = jnp.concatenate([cot, high, inner - high, pad], axis=0).astype(BF16)


def mid(lengths, tokens, out_grad, gain, heads_out, inv, w_out, w_gu, w_down, own_axis="mp"):
    features, own = heads_out.shape
    heads = inv.shape[0]
    mine = lambda: (lax.axis_index(own_axis), 0)
    args = (tokens, out_grad, gain, heads_out, inv, w_out, w_gu, w_down)
    tok = lax.dynamic_slice_in_dim(tokens, lax.axis_index(own_axis) * own, own, 0)
    cot = lax.dynamic_slice_in_dim(out_grad, lax.axis_index(own_axis) * own, own, 0)
    vm = pl.BlockSpec(memory_space=pltpu.VMEM)
    units = w_down.shape[2]
    return pl.pallas_call(
        functools.partial(mid_kernel, own_axis),
        in_specs=[pl.BlockSpec(memory_space=pltpu.SMEM)] + [vm] * 8,
        out_specs=[vm] * 7,
        out_shape=[
            jax.ShapeDtypeStruct((own, features), BF16),
            jax.ShapeDtypeStruct((features, own), F32),
            jax.ShapeDtypeStruct((heads, AUG, own), BF16),
            jax.ShapeDtypeStruct(w_out.shape, BF16),
            jax.ShapeDtypeStruct(w_gu.shape, BF16),
            jax.ShapeDtypeStruct(w_down.shape, BF16),
            jax.ShapeDtypeStruct((features, 1), F32),
        ],
        scratch_shapes=[
            pltpu.VMEM((8, 128), F32),
            pltpu.VMEM((8, 128), F32),
        ],
        compiler_params=params(),
        name="mid",
    )(lengths, tok, cot, gain, heads_out, inv, w_out, w_gu, w_down)


def attend_back_kernel(q_ref, k_ref, v_ref, do_ref, p_ref, dq_ref, dk_ref, dv_ref, va_ref):
    rows, own = k_ref.shape[1], q_ref.shape[1]

    @pl.when(pl.program_id(0) == 0)
    def _():
        va_ref[HDIM:] = jnp.full((AUG - HDIM, rows), -1.0, BF16)

    va_ref[:HDIM] = v_ref[...]
    cot = dot(va_ref[...], do_ref[0], TN)
    probs = p_ref[0]
    score_cot = probs * cot.astype(BF16)
    dv_ref[...] = dot(do_ref[0, :HDIM], probs, NT)
    dk_ref[...] = dot(q_ref[...], score_cot, NT) * LN2
    dq_ref[...] = dot(k_ref[...], score_cot, NN) * SCALE


def last_kernel(own_axis, q_ref, k_ref, v_ref, do_ref, p_ref, cos_ref, sin_ref, n1_ref, w_ref, gq_ref, nc_ref, gc_ref, dq_ref, dk_ref, dv_ref, pc_ref, acc_ref, va_ref):
    step, head = pl.program_id(0), pl.program_id(1)
    per = pl.num_programs(1)
    features, rows = n1_ref.shape
    own = q_ref.shape[1]
    width = per * HDIM
    mine = pl.ds(pl.multiple_of(lax.axis_index(own_axis) * own, own), own)

    @pl.when((step == 0) & (head == 0))
    def _():
        va_ref[HDIM:] = jnp.full((AUG - HDIM, rows), -1.0, BF16)
        acc_ref[...] = jnp.zeros_like(acc_ref)
        gc_ref[...] = jnp.zeros_like(gc_ref)

    va_ref[:HDIM] = v_ref[...]
    cot = dot(va_ref[...], do_ref[0], TN)
    probs = p_ref[0]
    score_cot = probs * cot.astype(BF16)
    at = pl.ds(pl.multiple_of(head * HDIM, HDIM), HDIM)
    dv = dot(do_ref[0, :HDIM], probs, NT)
    dk = dot(q_ref[...], score_cot, NT) * LN2
    dq = dot(k_ref[...], score_cot, NN) * SCALE
    pc_ref[pl.ds(pl.multiple_of(width + head * HDIM, HDIM), HDIM)] = dv.astype(BF16)
    pc_ref[at] = turn(dk, cos_ref[...], sin_ref[...], 1, True).astype(BF16)
    dq_ref[at] = turn(dq, cos_ref[:, mine], sin_ref[:, mine], 1, True).astype(BF16)

    @pl.when(head == per - 1)
    def _():
        kv = dot(n1_ref[...], pc_ref[...], NT)
        q = dot(n1_ref[:, mine], dq_ref[...], NT)
        gq_ref[0, :, :width] = q.astype(BF16)
        gq_ref[0, :, width:] = kv.astype(BF16)
        gc_ref[...] += jnp.sum(q * w_ref[0, :, :width].astype(F32), axis=1, keepdims=True) + jnp.sum(
            kv * w_ref[0, :, width:].astype(F32), axis=1, keepdims=True
        )

        def spread(i, carry):
            cols = pl.ds(pl.multiple_of(i * own, own), own)
            acc_ref[:, cols] += dot(w_ref[0, :, width:], pc_ref[:, cols], NN)
            return carry

        lax.fori_loop(0, rows // own, spread, 0)
        acc_ref[:, mine] += dot(w_ref[0, :, :width], dq_ref[...], NN)

    @pl.when((step == pl.num_programs(0) - 1) & (head == per - 1))
    def _():
        nc_ref[...] = acc_ref[...].astype(BF16)


def last(q, k, v, do, p, cos, sin, n1, w_qkv, own_axis="mp"):
    (features, own), rows = q.shape, k.shape[1]
    parts = w_qkv.shape[0]
    per = features // parts // HDIM
    width = per * HDIM
    head = lambda m, h: (m * per + h, 0)
    return pl.pallas_call(
        functools.partial(last_kernel, own_axis),
        grid=(parts, per),
        in_specs=[
            pl.BlockSpec((HDIM, own), head),
            pl.BlockSpec((HDIM, rows), head),
            pl.BlockSpec((HDIM, rows), head),
            pl.BlockSpec((1, AUG, own), lambda m, h: (m * per + h, 0, 0)),
            pl.BlockSpec((1, rows, own), lambda m, h: (m * per + h, 0, 0)),
            whole(HALF, rows),
            whole(HALF, rows),
            whole(features, rows),
            pl.BlockSpec((1,) + w_qkv.shape[1:], lambda m, h: (m, 0, 0)),
        ],
        out_specs=[
            pl.BlockSpec((1,) + w_qkv.shape[1:], lambda m, h: (m, 0, 0)),
            whole(features, rows),
            whole(features, 1),
        ],
        out_shape=[
            jax.ShapeDtypeStruct(w_qkv.shape, BF16),
            jax.ShapeDtypeStruct((features, rows), BF16),
            jax.ShapeDtypeStruct((features, 1), F32),
        ],
        scratch_shapes=[
            pltpu.VMEM((width, own), BF16),
            pltpu.VMEM((8, 128), F32),
            pltpu.VMEM((8, 128), F32),
            pltpu.VMEM((2 * width, rows), BF16),
            pltpu.VMEM((features, rows), F32),
            pltpu.VMEM((AUG, rows), BF16),
        ],
        compiler_params=params("arbitrary", "arbitrary"),
        name="last",
    )(q, k, v, do, p, cos, sin, n1, w_qkv)


def finish_kernel(tok_ref, gain_ref, nc_ref, mcot_ref, out_ref):
    hat, inv_sigma = normalize(tok_ref[...].T.astype(F32))
    d = nc_ref[...].astype(F32) * gain_ref[...]
    made = mcot_ref[...] + inv_sigma * (
        d - jnp.mean(d, axis=0, keepdims=True) - hat * jnp.mean(d * hat, axis=0, keepdims=True)
    )
    out_ref[...] = made.T.astype(BF16)


def finish(tokens, gain, nc, middle_cot, own_axis="mp"):
    features, own = middle_cot.shape
    tok = lax.dynamic_slice_in_dim(tokens, lax.axis_index(own_axis) * own, own, 0)
    vm = pl.BlockSpec(memory_space=pltpu.VMEM)
    return pl.pallas_call(
        finish_kernel,
        in_specs=[vm] * 4,
        out_specs=vm,
        out_shape=jax.ShapeDtypeStruct((own, features), BF16),
        compiler_params=params(),
        name="finish",
    )(tok, gain, nc, middle_cot)


def per_device(n_dp, n_mp, tokens, out_grad, w_qkv, w_out, w_gu, w_down, gain_attn, gain_mlp, lengths):
    rows, features = tokens.shape
    depth = w_qkv.shape[0]
    everyone = ("mp", "dp")

    def gather(shard):
        full = lax.all_gather(shard, everyone, axis=0, tiled=True)
        return full.reshape(n_mp, features, shard.shape[1])

    full_qkv = gather(w_qkv.reshape(depth, -1))
    full_out = gather(w_out.T)
    full_gu = gather(w_gu.reshape(depth, -1))
    full_down = gather(w_down.T)
    gain_one = lax.all_gather(gain_attn, "dp", axis=0, tiled=True).astype(F32)[:, None]
    gain_two = lax.all_gather(gain_mlp, "dp", axis=0, tiled=True).astype(F32)[:, None]
    n1, q, k, v, cos, sin = prep(lengths, tokens, gain_one, full_qkv, n_mp)
    heads_out, probs, inv = attend(lengths, q, k, v)
    out_own, middle_cot, do, g_out, g_gu, g_down, gain_two_cot = mid(
        lengths, tokens, out_grad, gain_two, heads_out, inv, full_out, full_gu, full_down
    )
    g_qkv, nc, gain_one_cot = last(q, k, v, do, probs, cos, sin, n1, full_qkv)
    nc_own = lax.psum_scatter(nc, "mp", scatter_dimension=1, tiled=True)
    in_own = finish(tokens, gain_one, nc_own, middle_cot)
    layer_out = lax.all_gather(out_own, "mp", axis=0, tiled=True)
    input_grad = lax.all_gather(in_own, "mp", axis=0, tiled=True).astype(F32)

    def scatter(grad):
        flat = grad.reshape(n_mp * features, grad.shape[2])
        return lax.psum_scatter(flat, everyone, scatter_dimension=0, tiled=True).astype(F32)

    def gain_grad(partial):
        full = lax.psum(partial[:, 0], ("dp", "mp"))
        return lax.dynamic_slice_in_dim(full, lax.axis_index("dp") * depth, depth, 0)

    return (
        layer_out,
        input_grad,
        scatter(g_qkv).reshape(w_qkv.shape),
        scatter(g_out).T,
        scatter(g_gu).reshape(w_gu.shape),
        scatter(g_down).T,
        gain_grad(gain_one_cot / gain_one),
        gain_grad(gain_two_cot),
    )


def solution(mesh):
    n_dp, n_mp = mesh.shape["dp"], mesh.shape["mp"]
    return jax.shard_map(
        functools.partial(per_device, n_dp, n_mp),
        mesh=mesh,
        in_specs=(
            P("dp", None),
            P("dp", None),
            P("dp", None, "mp"),
            P("mp", "dp"),
            P("dp", None, "mp"),
            P("mp", "dp"),
            P("dp"),
            P("dp"),
            P("dp", None),
        ),
        out_specs=(
            P("dp", None),
            P("dp", None),
            P("dp", None, "mp"),
            P("mp", "dp"),
            P("dp", None, "mp"),
            P("mp", "dp"),
            P("dp"),
            P("dp"),
        ),
        check_vma=False,
    )
```

time: 828 us -> 873 us (1.054)
  waiting for transfers between devices: 199 us -> 620 us
  matrix products: 208 us -> 0 us
  Pallas kernels: 0 us -> 145 us
  blocking collectives: 181 us -> 62.6 us
  other arithmetic: 118 us -> 6.89 us
  local copies, waits for them, and re-layouts: 85.7 us -> 22.7 us
  loops' own time: 13.9 us -> 0 us
    unnamed x9 -> x14, waiting for transfers between devices: 0.14 us -> 270 us
    all_gather x0 -> x6, waiting for transfers between devices: none -> 207 us  [the longest x4 152 us: gather(): full = lax.all_gather(shard, everyone, axis=0, tiled=True)]
    dot_general x37 -> x0, matrix products: 197 us -> none  [the longest x8 44.5 us: block_scores(): jnp.einsum('qhe,khe->hqk', q_block, keys_rot, preferred_element_type=jnp....]
    psum x3 -> x0, waiting for transfers between devices: 168 us -> none  [the longest x1 106 us: per_device(): mlp_sum = lax.psum(mlp_part.astype(jnp.bfloat16), 'mp').astype(jnp.float32)]
    pallas_call x0 -> x5, Pallas kernels: none -> 145 us  [the longest x1 59.1 us: last(): pl.pallas_call(functools.partial(last_kernel, own_axis), grid=(parts, per...]
    all_gather x4 -> x0, blocking collectives: 135 us -> none  [the longest x1 36.5 us: per_device(): lax.all_gather(w_qkv, 'dp', axis=0, tiled=True)]
    reduce_scatter x2, waiting for transfers between devices: 31 us -> 143 us  [the longest x1 110 us: scatter(): lax.psum_scatter(flat, everyone, scatter_dimension=0, tiled=True)]
    reduce_sum x12 -> x0, other arithmetic: 52 us -> none  [the longest x4 27.3 us: attend(): row_total = jnp.sum(exp_terms, axis=2, keepdims=True)]
  transfers between devices with their start and end apart: 7 -> 11, of which waited for: 3 -> 10; matrix products, arithmetic and copies ran while one was open for 31% -> 2% of each run, Pallas kernels for 0% -> 7%
where the time goes in v1:
time: 873 us; the launch traced here: 872 us
  waiting for transfers between devices  620 us (71%)
  Pallas kernels  145 us (17%)
  blocking collectives  62.6 us (7%)
  local copies, waits for them, and re-layouts  22.7 us (3%)
  between operations  14.6 us (2%)
    unnamed x14, waiting for transfers between devices  270 us
    all_gather x4, waiting for transfers between devices, gather(): full = lax.all_gather(shard, everyone, axis=0, tiled=True)  152 us
    reduce_scatter x1, waiting for transfers between devices, scatter(): lax.psum_scatter(flat, everyone, scatter_dimension=0, tiled=True)  110 us
    pallas_call x1, Pallas kernels, last(): pl.pallas_call(functools.partial(last_kernel, own_axis), grid=(parts, per...  59.1 us
    psum x1, blocking collectives, gain_grad(): full = lax.psum(partial[:, 0], ('dp', 'mp'))  39.5 us
    pallas_call x1, Pallas kernels, attend(): pl.pallas_call(functools.partial(attend_kernel, own_axis), grid=(heads,),...  35.1 us
    reduce_scatter x1, waiting for transfers between devices, per_device(): nc_own = lax.psum_scatter(nc, 'mp', scatter_dimension=1, tiled=True)  33.3 us
    all_gather x1, waiting for transfers between devices, per_device(): input_grad = lax.all_gather(in_own, 'mp', axis=0, tiled=True).astype(F32)  27.9 us
  transfers between devices with their start and end apart: 11, of which 10 were waited for; matrix products, arithmetic and copies ran while one was open for 2% of the time, Pallas kernels for 7%

profile of v1, /device:TPU:0, one launch (start us, length us, event | category | flops | bytes accessed | tf_op | source)
XLA Modules:
  0.0 872.0 jit_solution(4596235660632134578)
XLA Ops:
  7.2 1.1 copy.33
  9.1 1.5 copy.36
  10.7 1.6 copy.37
  12.4 1.7 reshape.61
  14.2 1.2 dynamic-slice
  17.8 23.1 %all-reduce.3 = (bf16[768]{0:T(1024)(128)(2,1)S(1)}, bf16[768]{0:T(1024)(128)(2,1)S(1)}) all-reduce(bf16[768]{0:T(1024)(128)(2,1)S(1)} %dynamic-update-slice, bf16[768]{0:T(1024)(128)(2,1)S(1)} %dynamic-update-slice.1), channel_id=1, replica_groups=mesh['dp'=8,'mp'=4] {'dp'}, use_global_device_ids=true, to_apply=%add | all-reduce | flops 1536 | bytes 6144
  40.9 0.9 reshape.95.gain_ref
  41.9 0.9 reshape.94.gain_ref
  42.8 2.7 constant_dynamic-slice_fusion
  45.5 30.0 %all-gather.7.cloned.1.call-done = bf16[3072,576]{1,0:T(8,128)(2,1)} async-done(((bf16[96,576]{1,0:T(8,128)(2,1)}), bf16[3072,576]{1,0:T(8,128)(2,1)}) %all-gather.7.cloned.1.call-update) | async-done | bytes 3538960 | tf_op jit(solution)/shard_map/all_gather | solution.py:435
  75.5 23.3 %prep.1 = (bf16[768,2048]{1,0:T(8,128)(2,1)}, bf16[768,512]{1,0:T(8,128)(2,1)}, bf16[768,2048]{1,0:T(8,128)(2,1)}, bf16[768,2048]{1,0:T(8,128)(2,1)}, f32[32,2048]{1,0:T(8,128)}, /*index=5*/f32[32,2048]{1,0:T(8,128)}) custom-call(s32[1,8]{1,0:T(1,128)} %len_ref.5, bf16[2048,768]{1,0:T(8,128)(2,1)} %tok_ref.1, f32[768,1]{1,0:T(8,128)} %reshape.95.gain_ref, ...), custom_call_target="tpu_custom_call" | custom-call | tf_op jit(solution)/shard_map/prep/pallas_call | solution.py:115
  98.8 35.1 %attend.1 = (bf16[768,512]{1,0:T(8,128)(2,1)}, bf16[12,2048,512]{2,1,0:T(8,128)(2,1)}, f32[12,1,512]{2,1,0:T(1,128)}) custom-call(s32[1,8]{1,0:T(1,128)} %len_ref.5, bf16[768,512]{1,0:T(8,128)(2,1)} %get-tuple-element.27.q_ref, bf16[768,2048]{1,0:T(8,128)(2,1)} %get-tuple-element.28.k_ref, bf16[768,2048]{1,0:T(8,128)(2,1)} %get-tuple-element.29.v_ref), custom_call_target="tpu_custom_call" | custom-call | tf_op jit(solution)/shard_map/attend/pallas_call | solution.py:177
  134.0 58.3 %all-gather.13.cloned.1.call-done = bf16[3072,288]{1,0:T(8,128)(2,1)} async-done(((bf16[96,288]{1,0:T(8,128)(2,1)}), bf16[3072,288]{1,0:T(8,128)(2,1)}) %all-gather.13.cloned.1.call-update) | async-done | bytes 1769488 | tf_op jit(solution)/shard_map/all_gather | solution.py:435
  192.2 63.6 %all-gather.11.cloned.1.call-done = bf16[3072,576]{1,0:T(8,128)(2,1)} async-done(((bf16[96,576]{1,0:T(8,128)(2,1)}), bf16[3072,576]{1,0:T(8,128)(2,1)}) %all-gather.11.cloned.1.call-update) | async-done | bytes 3538960 | tf_op jit(solution)/shard_map/all_gather | solution.py:435
  255.8 22.8 %mid.1 = (bf16[512,768]{1,0:T(8,128)(2,1)}, f32[768,512]{1,0:T(8,128)}, bf16[12,80,512]{2,1,0:T(8,128)(2,1)}, bf16[4,768,192]{2,1,0:T(8,128)(2,1)}, bf16[4,768,5...) custom-call(s32[1,8]{1,0:T(1,128)} %len_ref.5, bf16[512,768]{1,0:T(8,128)(2,1)} %get-tuple-element.67.tok_ref, ...), custom_call_target="tpu_custom_call" | custom-call | tf_op jit(solution)/shard_map/mid/pallas_call | solution.py:276
  278.6 59.1 %last.1 = (bf16[4,768,576]{2,1,0:T(8,128)(2,1)}, bf16[768,2048]{1,0:T(8,128)(2,1)}, f32[768,1]{1,0:T(8,128)}) custom-call(bf16[768,512]{1,0:T(8,128)(2,1)} %get-tuple-element.27.q_ref, bf16[768,2048]{1,0:T(8,128)(2,1)} %get-tuple-element.28.k_ref, bf16[768,2048]{1,0:T(8,128)(2,1)} %get-tuple-element.29.v_ref, bf16[12,80,512]{2,1,0:T(8,128)(2,1)} %get-tuple-element.33.do_ref, ...), custom_call_target="tpu_custom_call" | custom-call | tf_op jit(solution)/shard_map/last/pallas_call | solution.py:369
  341.2 33.3 %reduce-scatter.12.cloned.1.call-done.nc_ref = bf16[768,512]{1,0:T(8,128)(2,1)} async-done(((bf16[768,2048]{1,0:T(8,128)(2,1)}), bf16[768,512]{1,0:T(8,128)(2,1)}) %reduce-scatter.12.cloned.1.call-update) | async-done | bytes 786448 | tf_op jit(solution)/shard_map/reduce_scatter | solution.py:450
  374.5 4.4 finish.1
  379.4 39.5 %all-reduce.2 = (f32[768]{0:T(1024)S(1)}, f32[768]{0:T(1024)S(1)}) all-reduce(f32[768]{0:T(1024)S(1)} %divide_reduce_fusion, f32[768]{0:T(1024)S(1)} %reduce.1), channel_id=1, replica_groups=mesh['dp'=8,'mp'=4] {'dp','mp'}, use_global_device_ids=true, to_apply=%region_5.0 | all-reduce | flops 1536 | bytes 12288 | tf_op jit(solution)/shard_map/psum | solution.py:460
  420.0 57.5 %reduce-scatter.18.cloned.1.call-done = bf16[96,192]{1,0:T(8,128)(2,1)} async-done(((bf16[3072,192]{1,0:T(8,128)(2,1)}), bf16[96,192]{1,0:T(8,128)(2,1)}) %reduce-scatter.18.cloned.1.call-update) | async-done | bytes 36880
  477.5 0.9 copy.48
  479.1 102.6 %reduce-scatter.20.cloned.1.call-done = bf16[96,288]{1,0:T(8,128)(2,1)} async-done(((bf16[3072,288]{1,0:T(8,128)(2,1)}), bf16[96,288]{1,0:T(8,128)(2,1)}) %reduce-scatter.20.cloned.1.call-update) | async-done | bytes 55312
  581.7 1.0 copy.50
  583.4 106.7 %reduce-scatter.16.cloned.1.call-done = bf16[96,576]{1,0:T(8,128)(2,1)} async-done(((bf16[3072,576]{1,0:T(8,128)(2,1)}), bf16[96,576]{1,0:T(8,128)(2,1)}) %reduce-scatter.16.cloned.1.call-update) | async-done | bytes 110608
  690.1 1.0 copy.46
  691.2 0.9 copy.44
  692.0 27.2 %all-gather.15.cloned.1.call-done = bf16[2048,768]{1,0:T(8,128)(2,1)} async-done(((bf16[512,768]{1,0:T(8,128)(2,1)}), bf16[2048,768]{1,0:T(8,128)(2,1)}) %all-gather.15.cloned.1.call-update) | async-done | bytes 3145744 | tf_op jit(solution)/shard_map/all_gather | solution.py:452
  719.2 109.8 %reduce-scatter.14.cloned.1.call-done = bf16[96,576]{1,0:T(8,128)(2,1)} async-done(((bf16[3072,576]{1,0:T(8,128)(2,1)}), bf16[96,576]{1,0:T(8,128)(2,1)}) %reduce-scatter.14.cloned.1.call-update) | async-done | bytes 110608 | tf_op jit(solution)/shard_map/reduce_scatter | solution.py:457
  828.9 1.9 reshape.77
  830.8 27.9 %all-gather.17.cloned.1.call-done = bf16[2048,768]{1,0:T(8,128)(2,1)} async-done(((bf16[512,768]{1,0:T(8,128)(2,1)}), bf16[2048,768]{1,0:T(8,128)(2,1)}) %all-gather.17.cloned.1.call-update) | async-done | bytes 3145744 | tf_op jit(solution)/shard_map/all_gather | solution.py:453
  858.7 5.1 convert_element_type.2
  863.8 1.7 copy.54
  (41 shorter events, 9.1 us)
Async XLA Ops:
  7.2 68.3 %all-gather.7.cloned.1.call-start = ((), (), s32[]{:S(2)}) async-start(), calls=%async_computation.5 | async-start | bytes 4055040 | tf_op jit(solution)/shard_map/all_gather | solution.py:435
  9.1 124.8 %all-gather.9.cloned.1.call-start = ((), (), s32[]{:S(2)}) async-start(), calls=%async_computation.6 | async-start | bytes 1622016 | tf_op jit(solution)/shard_map/all_gather | solution.py:435
  10.7 181.5 %all-gather.13.cloned.1.call-start = ((), (), s32[]{:S(2)}) async-start(), calls=%async_computation.8 | async-start | bytes 2433024 | tf_op jit(solution)/shard_map/all_gather | solution.py:435
  12.4 243.4 %all-gather.11.cloned.1.call-start = ((), (), s32[]{:S(2)}) async-start(), calls=%async_computation.7 | async-start | bytes 4055040 | tf_op jit(solution)/shard_map/all_gather | solution.py:435
  14.2 360.3 %reduce-scatter.12.cloned.1.call-start = ((), (), s32[]{:S(2)}) async-start(), calls=%async_computation.10 | async-start | bytes 3932160 | tf_op jit(solution)/shard_map/reduce_scatter | solution.py:450
  337.7 139.8 %reduce-scatter.18.cloned.1.call-start = ((), (), s32[]{:S(2)}) async-start(), calls=%async_computation.14 | async-start | bytes 1622016
  338.3 243.4 %reduce-scatter.20.cloned.1.call-start = ((), (), s32[]{:S(2)}) async-start(), calls=%async_computation.15 | async-start | bytes 2433024
  339.0 351.1 %reduce-scatter.16.cloned.1.call-start = ((), (), s32[]{:S(2)}) async-start(), calls=%async_computation.13 | async-start | bytes 4055040
  339.8 379.4 %all-gather.15.cloned.1.call-start = ((), (), s32[]{:S(2)}) async-start(), calls=%async_computation.9 | async-start | bytes 3932160 | tf_op jit(solution)/shard_map/all_gather | solution.py:452
  340.5 488.4 %reduce-scatter.14.cloned.1.call-start = ((), (), s32[]{:S(2)}) async-start(), calls=%async_computation.12 | async-start | bytes 4055040 | tf_op jit(solution)/shard_map/reduce_scatter | solution.py:457
  341.1 37.8 %copy-start.1 = (f32[768,1]{1,0:T(8,128)S(1)}, f32[768,1]{1,0:T(8,128)}, u32[]{:S(2)}) copy-start(f32[768,1]{1,0:T(8,128)} %get-tuple-element.45) | copy-start | bytes 9220
  341.1 37.9 %copy-start.2 = (f32[768,1]{1,0:T(8,128)S(1)}, f32[768,1]{1,0:T(8,128)}, u32[]{:S(2)}) copy-start(f32[768,1]{1,0:T(8,128)} %get-tuple-element.44) | copy-start | bytes 9220
  341.1 517.6 %all-gather.17.cloned.1.call-start = ((), (), s32[]{:S(2)}) async-start(), calls=%async_computation.11 | async-start | bytes 3932160 | tf_op jit(solution)/shard_map/all_gather | solution.py:453
  830.8 32.9 %copy-start = (bf16[2048,768]{1,0:T(8,128)(2,1)S(1)}, bf16[2048,768]{1,0:T(8,128)(2,1)}, u32[]{:S(2)}) copy-start(bf16[2048,768]{1,0:T(8,128)(2,1)} %all-gather.15.cloned.1.call-done) | copy-start | bytes 9437188
Sparse Core Ops, SparseCore 0:
  11.6 63.8 all-gather.6
  78.5 53.8 all-gather.8
  136.0 56.2 all-gather.12
  195.6 60.1 all-gather.10
  337.8 36.6 reduce-scatter.11
  380.4 97.0 reduce-scatter.17
  483.7 98.0 reduce-scatter.19
  587.1 102.9 reduce-scatter.15
  691.7 27.4 all-gather.14
  725.0 103.9 reduce-scatter.13
  831.1 27.5 all-gather.16

commit v2 on v1

--- a/solution.py
+++ b/solution.py
@@ -72,15 +72,15 @@
     return jnp.concatenate(out, axis=0)
 
 
-def prep_kernel(own_axis, own, len_ref, tok_ref, gain_ref, w_ref, n1_ref, q_ref, k_ref, v_ref, cos_ref, sin_ref):
+def prep_kernel(own_axis, own, len_ref, tok_ref, w_ref, n1_ref, q_ref, k_ref, v_ref, cos_ref, sin_ref):
     features, rows = n1_ref.shape
-    width = w_ref.shape[2] // 3
+    width = q_ref.shape[0]
     heads = width // HDIM
     chunk = own
 
     @pl.when(pl.program_id(0) == 0)
     def _():
-        gain = gain_ref[...]
+        gain = w_ref[0, :, 3 * width :].astype(F32)
 
         def norm(i, carry):
             at = pl.ds(pl.multiple_of(i * chunk, chunk), chunk)
@@ -97,7 +97,7 @@
 
     def project(i, carry):
         at = pl.ds(pl.multiple_of(i * chunk, chunk), chunk)
-        made = dot(w_ref[0, :, width:], n1_ref[:, at], TN)
+        made = dot(w_ref[0, :, width : 3 * width], n1_ref[:, at], TN)
         k_ref[:, at] = turn(made[:width], cos_ref[:, at], sin_ref[:, at], heads).astype(BF16)
         v_ref[:, at] = made[width:].astype(BF16)
         return carry
@@ -108,17 +108,16 @@
     q_ref[...] = turn(made, cos_ref[:, mine], sin_ref[:, mine], heads).astype(BF16)
 
 
-def prep(lengths, tokens, gain, w_qkv, n_mp, own_axis="mp"):
+def prep(lengths, tokens, w_qkv, n_mp, own_axis="mp"):
     rows, features = tokens.shape
     own = rows // n_mp
-    width = w_qkv.shape[2] // 3
+    width = features // n_mp
     return pl.pallas_call(
         functools.partial(prep_kernel, own_axis, own),
         grid=(n_mp,),
         in_specs=[
             pl.BlockSpec(memory_space=pltpu.SMEM),
             whole(rows, features),
-            whole(features, 1),
             pl.BlockSpec((1,) + w_qkv.shape[1:], lambda m: (m, 0, 0)),
         ],
         out_specs=[
@@ -139,7 +138,7 @@
         ],
         compiler_params=params("arbitrary"),
         name="prep",
-    )(lengths, tokens, gain, w_qkv)
+    )(lengths, tokens, w_qkv)
 
 
 def attend_kernel(own_axis, len_ref, q_ref, k_ref, v_ref, o_ref, p_ref, inv_ref, ka_ref, qa_ref, va_ref):
@@ -210,39 +209,49 @@
 
 
 def mid_kernel(
-    own_axis, len_ref, tok_ref, cot_ref, gain_ref, heads_ref, inv_ref, wo_ref, wg_ref, wd_ref,
-    out_ref, mcot_ref, do_ref, go_ref, gg_ref, gd_ref, gain_cot_ref,
-    up_ref, hid_ref,
+    own_axis, units, len_ref, tok_ref, cot_ref, heads_ref, inv_ref, w_ref,
+    out_ref, mcot_ref, do_ref, g_ref,
 ):
     own, features = tok_ref.shape
-    parts, _, width = wo_ref.shape
-    units = wd_ref.shape[2]
+    parts = w_ref.shape[0]
+    width = features // parts
     heads = width // HDIM
+    pair = 2 * units
     _, _, live = layout_rows(len_ref, len_ref.shape[1], lax.axis_index(own_axis) * own, own)
-    total = dot(wo_ref[0], heads_ref[:width], NN)
+
+    def w_gu(m):
+        return w_ref[m, :, :pair]
+
+    def w_out(m):
+        return w_ref[m, :, pair : pair + width]
+
+    def w_down(m):
+        return w_ref[m, :, pair + width : pair + width + units]
+
+    total = dot(w_out(0), heads_ref[:width], NN)
     for m in range(1, parts):
-        total += dot(wo_ref[m], heads_ref[m * width : (m + 1) * width], NN)
+        total += dot(w_out(m), heads_ref[m * width : (m + 1) * width], NN)
     middle = tok_ref[...].T.astype(F32) + total
-    gain = gain_ref[...]
+    gain = w_ref[0, :, pair + width + units :].astype(F32)
     hat, inv_sigma = normalize(middle)
     normed = (hat * gain).astype(BF16)
     branch = jnp.where(live, cot_ref[...].T.astype(F32), 0.0).astype(BF16)
     total = middle
     back = jnp.zeros((features, own), F32)
     for m in range(parts):
-        gate_up = dot(wg_ref[m], normed, TN)
+        gate_up = dot(w_gu(m), normed, TN)
         gate, up = gate_up[:units], gate_up[units:]
         phi, slope = gelu_parts(gate)
         act = gate * phi
         hidden = (act * up).astype(BF16)
-        total += dot(wd_ref[m], hidden, NN)
-        hidden_cot = dot(wd_ref[m], branch, TN)
-        gd_ref[m] = dot(branch, hidden, NT).astype(BF16)
+        total += dot(w_down(m), hidden, NN)
+        hidden_cot = dot(w_down(m), branch, TN)
+        g_ref[m, :, pair + width : pair + width + units] = dot(branch, hidden, NT).astype(BF16)
         cots = jnp.concatenate([hidden_cot * up * (phi + slope), hidden_cot * act], axis=0).astype(BF16)
-        gg_ref[m] = dot(normed, cots, NT).astype(BF16)
-        back += dot(wg_ref[m], cots, NN)
+        g_ref[m, :, :pair] = dot(normed, cots, NT).astype(BF16)
+        back += dot(w_gu(m), cots, NN)
     out_ref[...] = total.astype(BF16).T
-    gain_cot_ref[...] = jnp.sum(back * hat, axis=1, keepdims=True)
+    gain_cot = jnp.sum(back * hat, axis=1, keepdims=True).astype(BF16)
     d = back * gain
     middle_cot = branch.astype(F32) + inv_sigma * (
         d - jnp.mean(d, axis=0, keepdims=True) - hat * jnp.mean(d * hat, axis=0, keepdims=True)
@@ -250,68 +259,42 @@
     mcot_ref[...] = middle_cot
     attn_cot = middle_cot.astype(BF16)
     for m in range(parts):
+        g_ref[m, :, pair + width + units :] = gain_cot
         part = heads_ref[m * width : (m + 1) * width]
-        go_ref[m] = dot(attn_cot, part, NT).astype(BF16)
-        back_heads = dot(wo_ref[m], attn_cot, TN)
+        g_ref[m, :, pair : pair + width] = dot(attn_cot, part, NT).astype(BF16)
+        back_heads = dot(w_out(m), attn_cot, TN)
         for h in range(heads):
             head = m * heads + h
             rows = slice(h * HDIM, (h + 1) * HDIM)
-            inv = inv_ref[head]
-            cot = back_heads[rows] * inv
+            cot = back_heads[rows] * inv_ref[head]
             inner = jnp.sum(cot * part[rows].astype(F32), axis=0, keepdims=True)
             high = inner.astype(BF16).astype(F32)
             pad = jnp.zeros((AUG - HDIM - 2, own), F32)
             do_ref[head] = jnp.concatenate([cot, high, inner - high, pad], axis=0).astype(BF16)
 
 
-def mid(lengths, tokens, out_grad, gain, heads_out, inv, w_out, w_gu, w_down, own_axis="mp"):
+def mid(lengths, tokens, out_grad, heads_out, inv, w_rest, units, own_axis="mp"):
     features, own = heads_out.shape
     heads = inv.shape[0]
-    mine = lambda: (lax.axis_index(own_axis), 0)
-    args = (tokens, out_grad, gain, heads_out, inv, w_out, w_gu, w_down)
     tok = lax.dynamic_slice_in_dim(tokens, lax.axis_index(own_axis) * own, own, 0)
     cot = lax.dynamic_slice_in_dim(out_grad, lax.axis_index(own_axis) * own, own, 0)
     vm = pl.BlockSpec(memory_space=pltpu.VMEM)
-    units = w_down.shape[2]
     return pl.pallas_call(
-        functools.partial(mid_kernel, own_axis),
-        in_specs=[pl.BlockSpec(memory_space=pltpu.SMEM)] + [vm] * 8,
-        out_specs=[vm] * 7,
+        functools.partial(mid_kernel, own_axis, units),
+        in_specs=[pl.BlockSpec(memory_space=pltpu.SMEM)] + [vm] * 5,
+        out_specs=[vm] * 4,
         out_shape=[
             jax.ShapeDtypeStruct((own, features), BF16),
             jax.ShapeDtypeStruct((features, own), F32),
             jax.ShapeDtypeStruct((heads, AUG, own), BF16),
-            jax.ShapeDtypeStruct(w_out.shape, BF16),
-            jax.ShapeDtypeStruct(w_gu.shape, BF16),
-            jax.ShapeDtypeStruct(w_down.shape, BF16),
-            jax.ShapeDtypeStruct((features, 1), F32),
-        ],
-        scratch_shapes=[
-            pltpu.VMEM((8, 128), F32),
-            pltpu.VMEM((8, 128), F32),
+            jax.ShapeDtypeStruct(w_rest.shape, BF16),
         ],
         compiler_params=params(),
         name="mid",
-    )(lengths, tok, cot, gain, heads_out, inv, w_out, w_gu, w_down)
-
-
-def attend_back_kernel(q_ref, k_ref, v_ref, do_ref, p_ref, dq_ref, dk_ref, dv_ref, va_ref):
-    rows, own = k_ref.shape[1], q_ref.shape[1]
-
-    @pl.when(pl.program_id(0) == 0)
-    def _():
-        va_ref[HDIM:] = jnp.full((AUG - HDIM, rows), -1.0, BF16)
-
-    va_ref[:HDIM] = v_ref[...]
-    cot = dot(va_ref[...], do_ref[0], TN)
-    probs = p_ref[0]
-    score_cot = probs * cot.astype(BF16)
-    dv_ref[...] = dot(do_ref[0, :HDIM], probs, NT)
-    dk_ref[...] = dot(q_ref[...], score_cot, NT) * LN2
-    dq_ref[...] = dot(k_ref[...], score_cot, NN) * SCALE
-
-
-def last_kernel(own_axis, q_ref, k_ref, v_ref, do_ref, p_ref, cos_ref, sin_ref, n1_ref, w_ref, gq_ref, nc_ref, gc_ref, dq_ref, dk_ref, dv_ref, pc_ref, acc_ref, va_ref):
+    )(lengths, tok, cot, heads_out, inv, w_rest)
+
+
+def last_kernel(own_axis, q_ref, k_ref, v_ref, do_ref, p_ref, cos_ref, sin_ref, n1_ref, w_ref, gq_ref, nc_ref, gc_ref, dq_ref, pc_ref, acc_ref, va_ref):
     step, head = pl.program_id(0), pl.program_id(1)
     per = pl.num_programs(1)
     features, rows = n1_ref.shape
@@ -341,15 +324,15 @@
     def _():
         kv = dot(n1_ref[...], pc_ref[...], NT)
         q = dot(n1_ref[:, mine], dq_ref[...], NT)
-        gq_ref[0, :, :width] = q.astype(BF16)
-        gq_ref[0, :, width:] = kv.astype(BF16)
+        gq_ref[step, :, :width] = q.astype(BF16)
+        gq_ref[step, :, width : 3 * width] = kv.astype(BF16)
         gc_ref[...] += jnp.sum(q * w_ref[0, :, :width].astype(F32), axis=1, keepdims=True) + jnp.sum(
-            kv * w_ref[0, :, width:].astype(F32), axis=1, keepdims=True
+            kv * w_ref[0, :, width : 3 * width].astype(F32), axis=1, keepdims=True
         )
 
         def spread(i, carry):
             cols = pl.ds(pl.multiple_of(i * own, own), own)
-            acc_ref[:, cols] += dot(w_ref[0, :, width:], pc_ref[:, cols], NN)
+            acc_ref[:, cols] += dot(w_ref[0, :, width : 3 * width], pc_ref[:, cols], NN)
             return carry
 
         lax.fori_loop(0, rows // own, spread, 0)
@@ -357,7 +340,10 @@
 
     @pl.when((step == pl.num_programs(0) - 1) & (head == per - 1))
     def _():
-        nc_ref[...] = acc_ref[...].astype(BF16)
+        gain_cot = (gc_ref[...] / w_ref[0, :, 3 * width :].astype(F32)).astype(BF16)
+        for m in range(gq_ref.shape[0]):
+            nc_ref[m] = acc_ref[:, m * own : (m + 1) * own].astype(BF16)
+            gq_ref[m, :, 3 * width :] = gain_cot
 
 
 def last(q, k, v, do, p, cos, sin, n1, w_qkv, own_axis="mp"):
@@ -381,19 +367,16 @@
             pl.BlockSpec((1,) + w_qkv.shape[1:], lambda m, h: (m, 0, 0)),
         ],
         out_specs=[
-            pl.BlockSpec((1,) + w_qkv.shape[1:], lambda m, h: (m, 0, 0)),
-            whole(features, rows),
-            whole(features, 1),
+            whole(*w_qkv.shape),
+            whole(parts, features, own),
         ],
         out_shape=[
             jax.ShapeDtypeStruct(w_qkv.shape, BF16),
-            jax.ShapeDtypeStruct((features, rows), BF16),
-            jax.ShapeDtypeStruct((features, 1), F32),
+            jax.ShapeDtypeStruct((parts, features, own), BF16),
         ],
         scratch_shapes=[
+            pltpu.VMEM((features, 1), F32),
             pltpu.VMEM((width, own), BF16),
-            pltpu.VMEM((8, 128), F32),
-            pltpu.VMEM((8, 128), F32),
             pltpu.VMEM((2 * width, rows), BF16),
             pltpu.VMEM((features, rows), F32),
             pltpu.VMEM((AUG, rows), BF16),
@@ -403,72 +386,479 @@
     )(q, k, v, do, p, cos, sin, n1, w_qkv)
 
 
-def finish_kernel(tok_ref, gain_ref, nc_ref, mcot_ref, out_ref):
-    hat, inv_sigma = normalize(tok_ref[...].T.astype(F32))
-    d = nc_ref[...].astype(F32) * gain_ref[...]
-    made = mcot_ref[...] + inv_sigma * (
+def place():
+    dp, mp = lax.axis_index("dp"), lax.axis_index("mp")
+    return dp // 2, lax.rem(dp, 2), mp // 2, lax.rem(mp, 2)
+
+
+def device(z, x, y, c):
+    return (2 * z + x, 2 * y + c)
+
+
+def remote(src, dst, send, recv, target):
+    return pltpu.make_async_remote_copy(
+        src_ref=src, dst_ref=dst, send_sem=send, recv_sem=recv,
+        device_id=target, device_id_type=pl.DeviceIdType.MESH,
+    )
+
+
+def greet(targets):
+    barrier = pltpu.get_barrier_semaphore()
+    for target in targets:
+        pl.semaphore_signal(barrier, inc=1, device_id=target, device_id_type=pl.DeviceIdType.MESH)
+    pl.semaphore_wait(barrier, len(targets))
+
+
+def peers(nz):
+    z, x, y, c = place()
+    across = [device(z, 1 - x, y, c), device(z, x, 1 - y, c), device(z, x, y, 1 - c)]
+    return across + [device(lax.rem(z + d, nz), x, y, c) for d in range(1, nz)]
+
+
+class Gather:
+    def __init__(self, nz, src, full, send, recv, local):
+        self.nz, self.src, self.full, self.send, self.recv, self.local = nz, src, full, send, recv, local
+        self.depth = src.shape[0]
+        self.index = {}
+        for kind in ("Z", "X", "Y", "S", "YA", "XB", "SX", "SY", "SA", "SB"):
+            for d in range(1 if kind == "Z" else 0, nz):
+                self.index[kind, d] = len(self.index)
+
+    @staticmethod
+    def count(nz):
+        return nz - 1 + 9 * nz
+
+    def block(self, z, x, y, c, half=None):
+        first, size = (0, self.depth) if half is None else (half * self.depth // 2, self.depth // 2)
+        return self.full.at[2 * y + c, pl.ds(pl.multiple_of((2 * z + x) * self.depth + first, 16), size)]
+
+    def message(self, kind, d, sending):
+        z, x, y, c = place()
+        nz = self.nz
+        back = z if d == 0 else lax.rem(z - d + nz, nz)
+        ahead = lax.rem(z + d, nz)
+        sx, sy, sib = device(z, 1 - x, y, c), device(z, x, 1 - y, c), device(z, x, y, 1 - c)
+        sent, got, half, target = {
+            "Z": ((z, x, y, c), (back, x, y, c), None, device(ahead, x, y, c)),
+            "X": ((back, x, y, c), (back, 1 - x, y, c), None, sx),
+            "Y": ((back, x, y, c), (back, x, 1 - y, c), None, sy),
+            "S": ((back, x, y, c), (back, x, y, 1 - c), None, sib),
+            "YA": ((back, 1 - x, y, c), (back, 1 - x, 1 - y, c), 0, sy),
+            "XB": ((back, x, 1 - y, c), (back, 1 - x, 1 - y, c), 1, sx),
+            "SX": ((back, 1 - x, y, c), (back, 1 - x, y, 1 - c), None, sib),
+            "SY": ((back, x, 1 - y, c), (back, x, 1 - y, 1 - c), None, sib),
+            "SA": ((back, 1 - x, 1 - y, c), (back, 1 - x, 1 - y, 1 - c), 0, sib),
+            "SB": ((back, 1 - x, 1 - y, c), (back, 1 - x, 1 - y, 1 - c), 1, sib),
+        }[kind]
+        i = self.index[kind, d]
+        at = self.block(*(sent if sending else got), half)
+        own = sending and (kind == "Z" or (d == 0 and kind in ("X", "Y", "S")))
+        return remote(self.src if own else at, at, self.send.at[i], self.recv.at[i], target)
+
+    def start(self, kind, d):
+        self.message(kind, d, True).start()
+
+    def arrived(self, kind, d):
+        self.message(kind, d, False).wait_recv()
+
+    def own(self):
+        z, x, y, c = place()
+        return pltpu.make_async_copy(self.src, self.block(z, x, y, c), self.local)
+
+    def begin(self):
+        for d in range(1, self.nz):
+            self.start("Z", d)
+        for kind in ("X", "Y", "S"):
+            self.start(kind, 0)
+        self.own().start()
+
+    def along(self, d):
+        self.arrived("Z", d)
+        for kind in ("X", "Y", "S"):
+            self.start(kind, d)
+
+    def over(self, d):
+        self.arrived("X", d)
+        self.start("YA", d)
+        self.start("SX", d)
+        self.arrived("Y", d)
+        self.start("XB", d)
+        self.start("SY", d)
+
+    def corner(self, d):
+        self.arrived("YA", d)
+        self.start("SA", d)
+        self.arrived("XB", d)
+        self.start("SB", d)
+
+    def end(self):
+        self.own().wait()
+        for d in range(self.nz):
+            for kind in ("S", "SX", "SY", "SA", "SB"):
+                self.arrived(kind, d)
+        for kind, d in self.index:
+            self.message(kind, d, True).wait_send()
+
+    def order(self):
+        nz = self.nz
+        near = sorted(range(1, nz), key=lambda d: min(d, nz - d))
+        steps = [functools.partial(self.begin)]
+        for d in [0] + near:
+            if d:
+                steps.append(functools.partial(self.along, d))
+            steps.append(functools.partial(self.over, d))
+        for d in [0] + near:
+            steps.append(functools.partial(self.corner, d))
+        return steps + [self.end]
+
+
+def gather_kernel(nz, count, *refs):
+    srcs, fulls, sems = refs[:count], refs[count : 2 * count], refs[2 * count :]
+    greet(peers(nz))
+    gathers = [Gather(nz, srcs[i], fulls[i], *sems[3 * i : 3 * i + 3]) for i in range(count)]
+    for steps in zip(*[g.order() for g in gathers]):
+        for step in steps:
+            step()
+
+
+def gather_all(nz, n_mp, shards):
+    hbm = pl.BlockSpec(memory_space=pl.ANY)
+    n = Gather.count(nz)
+    dma = pltpu.SemaphoreType.DMA
+    return pl.pallas_call(
+        functools.partial(gather_kernel, nz, len(shards)),
+        in_specs=[hbm] * len(shards),
+        out_specs=[hbm] * len(shards),
+        out_shape=[jax.ShapeDtypeStruct((n_mp, 2 * nz * s.shape[0], s.shape[1]), BF16) for s in shards],
+        scratch_shapes=[dma((n,)), dma((n,)), dma] * len(shards),
+        compiler_params=pltpu.CompilerParams(collective_id=1, has_side_effects=True),
+        name="gather_all",
+    )(*shards)
+
+
+class Scatter:
+    def __init__(self, nz, part, out, core, side, line, last, send, recv):
+        self.nz, self.part, self.out, self.core, self.side, self.line, self.last = nz, part, out, core, side, line, last
+        self.send, self.recv = send, recv
+        self.depth = out.shape[0]
+
+    @staticmethod
+    def scratch(nz, depth, columns):
+        count = 2 * nz + nz + nz
+        return [
+            pltpu.VMEM((2, 2 * nz * depth, columns), BF16),
+            pltpu.VMEM((2, nz * depth, columns), BF16),
+            pltpu.VMEM((nz, 2, depth, columns), BF16),
+            pltpu.VMEM((depth, columns), BF16),
+            pltpu.SemaphoreType.DMA((count,)),
+            pltpu.SemaphoreType.DMA((count,)),
+        ]
+
+    def row(self, d):
+        z, _, _, _ = place()
+        return z if d == 0 else lax.rem(z + d, self.nz)
+
+    def rows(self, d, x):
+        return pl.ds(pl.multiple_of((2 * self.row(d) + x) * self.depth, 16), self.depth)
+
+    def both(self, d):
+        return pl.ds(pl.multiple_of(2 * self.row(d) * self.depth, 16), 2 * self.depth)
+
+    def lane(self, d):
+        return pl.ds(pl.multiple_of(self.row(d) * self.depth, 16), self.depth)
+
+    def message(self, kind, d, up=0):
+        z, x, y, c = place()
+        nz = self.nz
+        i = {"C": up * nz + d, "X": 2 * nz + d, "Z": 3 * nz + d, "Y": 3 * nz}[kind]
+        sems = self.send.at[i], self.recv.at[i]
+        if kind == "C":
+            both = self.both(d)
+            return remote(self.part.at[2 * up + 1 - c, both], self.core.at[up, both], *sems, device(z, x, y, 1 - c))
+        if kind == "X":
+            return remote(
+                self.core.at[:, self.rows(d, 1 - x)], self.side.at[:, self.lane(d)], *sems, device(z, 1 - x, y, c)
+            )
+        if kind == "Z":
+            return remote(self.side.at[:, self.lane(d)], self.line.at[d], *sems, device(self.row(d), x, y, c))
+        return remote(self.line.at[0, 1 - y], self.last, *sems, device(z, x, 1 - y, c))
+
+    def begin(self):
+        for d in [*range(1, self.nz), 0]:
+            for up in range(2):
+                self.message("C", d, up).start()
+
+    def chip(self, d):
+        _, x, _, c = place()
+        for up in range(2):
+            self.message("C", d, up).wait_recv()
+        for side in (1 - x, x):
+            rows = self.rows(d, side)
+            for up in range(2):
+                made = self.part[2 * up + c, rows].astype(F32) + self.core[up, rows].astype(F32)
+                self.core[up, rows] = made.astype(BF16)
+            if side is not x:
+                self.message("X", d).start()
+
+    def over(self, d):
+        _, x, _, _ = place()
+        self.message("X", d).wait_recv()
+        rows, lane = self.rows(d, x), self.lane(d)
+        for up in range(2):
+            made = self.core[up, rows].astype(F32) + self.side[up, lane].astype(F32)
+            self.side[up, lane] = made.astype(BF16)
+        if d:
+            self.message("Z", d).start()
+
+    def along(self):
+        _, _, y, _ = place()
+        for d in range(1, self.nz):
+            self.message("Z", d).wait_recv()
+        lane = self.lane(0)
+        for up in range(2):
+            made = self.side[up, lane].astype(F32)
+            for d in range(1, self.nz):
+                made += self.line[d, up].astype(F32)
+            self.line[0, up] = made.astype(BF16)
+        self.message("Y", 0).start()
+
+    def end(self):
+        _, _, y, _ = place()
+        self.message("Y", 0).wait_recv()
+        self.out[...] = self.line[0, y].astype(F32) + self.last[...].astype(F32)
+        for d in range(self.nz):
+            for up in range(2):
+                self.message("C", d, up).wait_send()
+            self.message("X", d).wait_send()
+            if d:
+                self.message("Z", d).wait_send()
+        self.message("Y", 0).wait_send()
+
+    def order(self):
+        far = [*range(1, self.nz), 0]
+        return (
+            [self.begin]
+            + [functools.partial(self.chip, d) for d in far]
+            + [functools.partial(self.over, d) for d in far]
+            + [self.along, self.end]
+        )
+
+
+class Share:
+    def __init__(self, src, full, send, recv, local, pieces=1):
+        self.src, self.full, self.send, self.recv, self.local, self.pieces = src, full, send, recv, local, pieces
+        self.size = src.shape[0] // pieces
+
+    @staticmethod
+    def sems(pieces):
+        dma = pltpu.SemaphoreType.DMA
+        return [dma((3 * pieces,)), dma((3 * pieces,)), dma((pieces,))]
+
+    def rows(self, y, c, i):
+        own = self.size * self.pieces
+        return pl.ds(pl.multiple_of((2 * y + c) * own + i * self.size, 16), self.size)
+
+    def message(self, kind, i):
+        z, x, y, c = place()
+        n = self.pieces
+        piece = self.src.at[pl.ds(i * self.size, self.size)]
+        if kind == "own":
+            return pltpu.make_async_copy(piece, self.full.at[self.rows(y, c, i)], self.local.at[i])
+        k = {"Y": 0, "C": 1, "F": 2}[kind] * n + i
+        sems = self.send.at[k], self.recv.at[k]
+        sib = device(z, x, y, 1 - c)
+        if kind == "Y":
+            return remote(piece, self.full.at[self.rows(y, c, i)], *sems, device(z, x, 1 - y, c))
+        if kind == "C":
+            return remote(piece, self.full.at[self.rows(y, c, i)], *sems, sib)
+        at = self.full.at[self.rows(1 - y, c, i)]
+        return remote(at, at, *sems, sib)
+
+    def begin(self, i):
+        for kind in ("Y", "C", "own"):
+            self.message(kind, i).start()
+
+    def on(self, i):
+        self.message("Y", i).wait_recv()
+        self.message("F", i).start()
+
+    def end(self):
+        for i in range(self.pieces):
+            self.message("own", i).wait()
+            self.message("C", i).wait_recv()
+            self.message("F", i).wait_recv()
+            for kind in ("Y", "C", "F"):
+                self.message(kind, i).wait_send()
+
+
+class Fold:
+    def __init__(self, part, near, far, send, recv, pieces):
+        self.part, self.near, self.far, self.send, self.recv, self.pieces = part, near, far, send, recv, pieces
+        self.size = part.shape[1] // pieces
+
+    @staticmethod
+    def scratch(features, own, pieces):
+        dma = pltpu.SemaphoreType.DMA
+        return [pltpu.VMEM((2, features, own), BF16), pltpu.VMEM((features, own), BF16), dma((3 * pieces,)), dma((3 * pieces,))]
+
+    def rows(self, i):
+        return pl.ds(i * self.size, self.size)
+
+    def message(self, kind, i):
+        z, x, y, c = place()
+        k = {"far": 0, "near": 1, "Y": 2}[kind] * self.pieces + i
+        sems = self.send.at[k], self.recv.at[k]
+        rows = self.rows(i)
+        if kind == "Y":
+            return remote(self.near.at[1 - y, rows], self.far.at[rows], *sems, device(z, x, 1 - y, c))
+        up = 1 - y if kind == "far" else y
+        return remote(self.part.at[2 * up + 1 - c, rows], self.near.at[up, rows], *sems, device(z, x, y, 1 - c))
+
+    def begin(self):
+        for kind in ("far", "near"):
+            for i in range(self.pieces):
+                self.message(kind, i).start()
+
+    def chip(self, i):
+        _, _, y, c = place()
+        self.message("far", i).wait_recv()
+        rows = self.rows(i)
+        made = self.part[2 * (1 - y) + c, rows].astype(F32) + self.near[1 - y, rows].astype(F32)
+        self.near[1 - y, rows] = made.astype(BF16)
+        self.message("Y", i).start()
+
+    def end(self):
+        _, _, y, c = place()
+        for i in range(self.pieces):
+            self.message("near", i).wait_recv()
+            self.message("Y", i).wait_recv()
+        made = self.part[2 * y + c].astype(F32) + self.near[y].astype(F32) + self.far[...].astype(F32)
+        for i in range(self.pieces):
+            for kind in ("far", "near", "Y"):
+                self.message(kind, i).wait_send()
+        return made
+
+
+def finish(tokens, gain, cot, middle_cot):
+    hat, inv_sigma = normalize(tokens.T.astype(F32))
+    d = cot * gain
+    made = middle_cot + inv_sigma * (
         d - jnp.mean(d, axis=0, keepdims=True) - hat * jnp.mean(d * hat, axis=0, keepdims=True)
     )
-    out_ref[...] = made.T.astype(BF16)
-
-
-def finish(tokens, gain, nc, middle_cot, own_axis="mp"):
+    return made.T.astype(BF16)
+
+
+FOLD_PIECES = 4
+
+
+def tail_kernel(nz, *refs):
+    tok_ref, gain_ref, nc_ref, mcot_ref, out_own, gq_ref, gr_ref = refs[:7]
+    out_full, in_full, dq_ref, dr_ref = refs[7:11]
+    in_own = refs[11]
+    a, b = Scatter(nz, gq_ref, dq_ref, *refs[12:18]), Scatter(nz, gr_ref, dr_ref, *refs[18:24])
+    fold = Fold(nc_ref, *refs[24:28], FOLD_PIECES)
+    out_share, in_share = Share(out_own, out_full, *refs[28:31]), Share(in_own, in_full, *refs[31:34])
+    greet(peers(nz))
+    fold.begin()
+    for i in range(FOLD_PIECES):
+        fold.chip(i)
+    a.begin()
+    b.begin()
+    a_steps, b_steps = a.order()[1:], b.order()[1:]
+    for i in range(nz):
+        a_steps[i]()
+        b_steps[i]()
+    in_own[...] = finish(tok_ref[...], gain_ref[...], fold.end(), mcot_ref[...])
+    in_share.begin(0)
+    out_share.begin(0)
+    for i in range(nz, len(a_steps)):
+        a_steps[i]()
+        b_steps[i]()
+    for share in (in_share, out_share):
+        share.on(0)
+    for share in (in_share, out_share):
+        share.end()
+
+
+def tail(nz, n_mp, tokens, gain, nc, middle_cot, out_own, g_qkv, g_rest):
     features, own = middle_cot.shape
-    tok = lax.dynamic_slice_in_dim(tokens, lax.axis_index(own_axis) * own, own, 0)
+    tok = lax.dynamic_slice_in_dim(tokens, lax.axis_index("mp") * own, own, 0)
     vm = pl.BlockSpec(memory_space=pltpu.VMEM)
+    hbm = pl.BlockSpec(memory_space=pl.ANY)
+    depth = features // (2 * nz)
     return pl.pallas_call(
-        finish_kernel,
-        in_specs=[vm] * 4,
-        out_specs=vm,
-        out_shape=jax.ShapeDtypeStruct((own, features), BF16),
-        compiler_params=params(),
-        name="finish",
-    )(tok, gain, nc, middle_cot)
+        functools.partial(tail_kernel, nz),
+        in_specs=[vm] * 7,
+        out_specs=[hbm, hbm, vm, vm],
+        out_shape=[
+            jax.ShapeDtypeStruct((n_mp * own, features), BF16),
+            jax.ShapeDtypeStruct((n_mp * own, features), BF16),
+            jax.ShapeDtypeStruct((depth, g_qkv.shape[2]), F32),
+            jax.ShapeDtypeStruct((depth, g_rest.shape[2]), F32),
+        ],
+        scratch_shapes=[pltpu.VMEM((own, features), BF16)]
+        + Scatter.scratch(nz, depth, g_qkv.shape[2])
+        + Scatter.scratch(nz, depth, g_rest.shape[2])
+        + Fold.scratch(features, own, FOLD_PIECES)
+        + Share.sems(1)
+        + Share.sems(1),
+        compiler_params=pltpu.CompilerParams(
+            collective_id=2, has_side_effects=True, vmem_limit_bytes=VMEM_BYTES
+        ),
+        name="tail",
+    )(tok, gain, nc, middle_cot, out_own, g_qkv, g_rest)
 
 
 def per_device(n_dp, n_mp, tokens, out_grad, w_qkv, w_out, w_gu, w_down, gain_attn, gain_mlp, lengths):
     rows, features = tokens.shape
     depth = w_qkv.shape[0]
+    units, width = w_down.shape[0], w_out.shape[0]
     everyone = ("mp", "dp")
-
-    def gather(shard):
-        full = lax.all_gather(shard, everyone, axis=0, tiled=True)
-        return full.reshape(n_mp, features, shard.shape[1])
-
-    full_qkv = gather(w_qkv.reshape(depth, -1))
-    full_out = gather(w_out.T)
-    full_gu = gather(w_gu.reshape(depth, -1))
-    full_down = gather(w_down.T)
-    gain_one = lax.all_gather(gain_attn, "dp", axis=0, tiled=True).astype(F32)[:, None]
-    gain_two = lax.all_gather(gain_mlp, "dp", axis=0, tiled=True).astype(F32)[:, None]
-    n1, q, k, v, cos, sin = prep(lengths, tokens, gain_one, full_qkv, n_mp)
+    linked = n_mp == 4 and n_dp % 2 == 0 and depth % 32 == 0
+    shards = [
+        jnp.concatenate([w_qkv.reshape(depth, -1), gain_attn[:, None]], axis=1),
+        jnp.concatenate([w_gu.reshape(depth, -1), w_out.T, w_down.T, gain_mlp[:, None]], axis=1),
+    ]
+    if linked:
+        full_qkv, full_rest = gather_all(n_dp // 2, n_mp, shards)
+    else:
+        full_qkv, full_rest = (
+            lax.all_gather(s, everyone, axis=0, tiled=True).reshape(n_mp, features, s.shape[1]) for s in shards
+        )
+    n1, q, k, v, cos, sin = prep(lengths, tokens, full_qkv, n_mp)
     heads_out, probs, inv = attend(lengths, q, k, v)
-    out_own, middle_cot, do, g_out, g_gu, g_down, gain_two_cot = mid(
-        lengths, tokens, out_grad, gain_two, heads_out, inv, full_out, full_gu, full_down
-    )
-    g_qkv, nc, gain_one_cot = last(q, k, v, do, probs, cos, sin, n1, full_qkv)
-    nc_own = lax.psum_scatter(nc, "mp", scatter_dimension=1, tiled=True)
-    in_own = finish(tokens, gain_one, nc_own, middle_cot)
-    layer_out = lax.all_gather(out_own, "mp", axis=0, tiled=True)
-    input_grad = lax.all_gather(in_own, "mp", axis=0, tiled=True).astype(F32)
-
-    def scatter(grad):
-        flat = grad.reshape(n_mp * features, grad.shape[2])
-        return lax.psum_scatter(flat, everyone, scatter_dimension=0, tiled=True).astype(F32)
-
-    def gain_grad(partial):
-        full = lax.psum(partial[:, 0], ("dp", "mp"))
-        return lax.dynamic_slice_in_dim(full, lax.axis_index("dp") * depth, depth, 0)
-
+    out_own, middle_cot, do, g_rest = mid(lengths, tokens, out_grad, heads_out, inv, full_rest, units)
+    g_qkv, nc = last(q, k, v, do, probs, cos, sin, n1, full_qkv)
+    gain_one = full_qkv[0, :, 3 * width :].astype(F32)
+    if linked:
+        layer_out, input_grad, d_qkv, d_rest = tail(
+            n_dp // 2, n_mp, tokens, gain_one, nc, middle_cot, out_own, g_qkv, g_rest
+        )
+    else:
+        own = middle_cot.shape[1]
+        tok = lax.dynamic_slice_in_dim(tokens, lax.axis_index("mp") * own, own, 0)
+        nc_own = lax.psum_scatter(nc, "mp", scatter_dimension=0, tiled=True)[0]
+        in_own = finish(tok, gain_one, nc_own.astype(F32), middle_cot)
+        layer_out, input_grad = (lax.all_gather(v, "mp", axis=0, tiled=True) for v in (out_own, in_own))
+        d_qkv, d_rest = (
+            lax.psum_scatter(
+                g.reshape(n_mp * features, -1), everyone, scatter_dimension=0, tiled=True
+            ).astype(F32)
+            for g in (g_qkv, g_rest)
+        )
+    pair = 2 * units
+    gains = [d_qkv[:, 3 * width], d_rest[:, pair + width + units]]
+    if not linked:
+        gains = [lax.all_gather(g, "mp")[0] for g in gains]
     return (
         layer_out,
-        input_grad,
-        scatter(g_qkv).reshape(w_qkv.shape),
-        scatter(g_out).T,
-        scatter(g_gu).reshape(w_gu.shape),
-        scatter(g_down).T,
-        gain_grad(gain_one_cot / gain_one),
-        gain_grad(gain_two_cot),
+        input_grad.astype(F32),
+        d_qkv[:, : 3 * width].reshape(w_qkv.shape),
+        d_rest[:, pair : pair + width].T,
+        d_rest[:, :pair].reshape(w_gu.shape),
+        d_rest[:, pair + width : pair + width + units].T,
+        gains[0],
+        gains[1],
     )
 
 

time: 873 us -> 342 us (0.39)
  the two profiles are of different devices: /device:TPU:0 before, /device:TPU:9 now
where the time goes in v2:
time: 342 us; the launch traced here: 341 us
  Pallas kernels  312 us (91%)
  local copies, waits for them, and re-layouts  21.3 us (6%)
  other arithmetic  7.61 us (2%)
    pallas_call x1, Pallas kernels, tail(): pl.pallas_call(functools.partial(tail_kernel, nz), in_specs=[vm] * 7, out...  109 us
    pallas_call x1, Pallas kernels, gather_all(): pl.pallas_call(functools.partial(gather_kernel, nz, len(shards)), in_spec...  61.3 us
    pallas_call x1, Pallas kernels, last(): pl.pallas_call(functools.partial(last_kernel, own_axis), grid=(parts, per...  60.1 us
    pallas_call x1, Pallas kernels, attend(): pl.pallas_call(functools.partial(attend_kernel, own_axis), grid=(heads,),...  35 us
    pallas_call x1, Pallas kernels, prep(): pl.pallas_call(functools.partial(prep_kernel, own_axis, own), grid=(n_mp,...  23.4 us
    pallas_call x1, Pallas kernels, mid(): pl.pallas_call(functools.partial(mid_kernel, own_axis, units), in_specs=[...  23.1 us
    unnamed x9, local copies, waits for them, and re-layouts  7.01 us

profile of v2, /device:TPU:9, one launch (start us, length us, event | category | flops | bytes accessed | tf_op | source)
XLA Modules:
  0.0 341.2 jit_solution(8106424579689136498)
XLA Ops:
  0.6 1.1 reshape.43
  1.7 1.0 copy.29
  2.7 0.9 copy.28
  3.6 0.8 copy.30
  4.4 0.8 concatenate.7.refs_1_
  5.2 1.1 copy.25
  6.2 0.2 copy.26
  6.4 0.8 copy.27
  7.2 0.7 pad_maximum_fusion.refs_0_
  7.9 61.3 %gather_all.1 = (bf16[4,768,577]{2,1,0:T(8,128)(2,1)}, bf16[4,768,1057]{2,1,0:T(8,128)(2,1)}) custom-call(bf16[96,577]{1,0:T(8,128)(2,1)} %pad_maximum_fusion.refs_0_, bf16[96,1057]{1,0:T(8,128)(2,1)} %concatenate.7.refs_1_), custom_call_target="tpu_custom_call" | custom-call | tf_op jit(solution)/shard_map/gather_all/pallas_call | solution.py:528
  69.2 23.4 %prep.1 = (bf16[768,2048]{1,0:T(8,128)(2,1)}, bf16[768,512]{1,0:T(8,128)(2,1)}, bf16[768,2048]{1,0:T(8,128)(2,1)}, bf16[768,2048]{1,0:T(8,128)(2,1)}, f32[32,2048]{1,0:T(8,128)}, /*index=5*/f32[32,2048]{1,0:T(8,128)}) custom-call(s32[1,8]{1,0:T(1,128)} %len_ref.5, bf16[2048,768]{1,0:T(8,128)(2,1)} %tok_ref.1, bf16[4,768,577]{2,1,0:T(8,128)(2,1)} %get-tuple-element.29.w_ref), custom_call_target="tpu_custom_call" | custom-call | tf_op jit(solution)/shard_map/prep/pallas_call | solution.py:115
  92.6 35.0 %attend.1 = (bf16[768,512]{1,0:T(8,128)(2,1)}, bf16[12,2048,512]{2,1,0:T(8,128)(2,1)}, f32[12,1,512]{2,1,0:T(1,128)}) custom-call(s32[1,8]{1,0:T(1,128)} %len_ref.5, bf16[768,512]{1,0:T(8,128)(2,1)} %get-tuple-element.30.q_ref, bf16[768,2048]{1,0:T(8,128)(2,1)} %get-tuple-element.31.k_ref, bf16[768,2048]{1,0:T(8,128)(2,1)} %get-tuple-element.32.v_ref), custom_call_target="tpu_custom_call" | custom-call | tf_op jit(solution)/shard_map/attend/pallas_call | solution.py:176
  127.6 2.6 constant_dynamic-slice_fusion
  130.3 23.1 %mid.1 = (bf16[512,768]{1,0:T(8,128)(2,1)}, f32[768,512]{1,0:T(8,128)}, bf16[12,80,512]{2,1,0:T(8,128)(2,1)}, bf16[4,768,1057]{2,1,0:T(8,128)(2,1)}) custom-call(s32[1,8]{1,0:T(1,128)} %len_ref.5, bf16[512,768]{1,0:T(8,128)(2,1)} %get-tuple-element.67.tok_ref.refs_0_, bf16[512,768]{1,0:T(8,128)(2,1)} %get-tuple-element.66.cot_ref, ...), custom_call_target="tpu_custom_call" | custom-call | tf_op jit(solution)/shard_map/mid/pallas_call | solution.py:282
  153.3 60.1 %last.1 = (bf16[4,768,577]{2,1,0:T(8,128)(2,1)}, bf16[4,768,512]{2,1,0:T(8,128)(2,1)}) custom-call(bf16[768,512]{1,0:T(8,128)(2,1)} %get-tuple-element.30.q_ref, bf16[768,2048]{1,0:T(8,128)(2,1)} %get-tuple-element.31.k_ref, bf16[768,2048]{1,0:T(8,128)(2,1)} %get-tuple-element.32.v_ref, bf16[12,80,512]{2,1,0:T(8,128)(2,1)} %get-tuple-element.36.do_ref, ...), custom_call_target="tpu_custom_call" | custom-call | tf_op jit(solution)/shard_map/last/pallas_call | solution.py:355
  213.4 1.8 bitcast_convert_fusion.refs_1_
  215.2 108.7 %tail.1 = (bf16[2048,768]{1,0:T(8,128)(2,1)}, bf16[2048,768]{1,0:T(8,128)(2,1)}, f32[96,577]{1,0:T(8,128)}, f32[96,1057]{1,0:T(8,128)}) custom-call(bf16[512,768]{1,0:T(8,128)(2,1)} %get-tuple-element.67.tok_ref.refs_0_, f32[768,1]{1,0:T(8,128)} %bitcast_convert_fusion.refs_1_, bf16[4,768,512]{2,1,0:T(8,128)(2,1)} %get-tuple-element.41.refs_2_, ...), custom_call_target="tpu_custom_call" | custom-call | tf_op jit(solution)/shard_map/tail/pallas_call | solution.py:789
  323.9 5.1 %convert_element_type.10 = f32[2048,768]{1,0:T(8,128)} convert(bf16[2048,768]{1,0:T(8,128)(2,1)} %get-tuple-element.47) | non-fusion elementwise | flops 1572864 | bytes 9437184 | tf_op jit(solution)/shard_map/convert_element_type | solution.py:855
  329.0 0.0 copy-start
  329.0 1.2 copy.31
  330.3 0.9 copy.32
  331.1 1.0 slice.24
  332.1 0.9 reshape.45
  333.1 0.9 slice_bitcast_fusion
  334.0 0.8 copy.34
  334.8 1.0 slice_bitcast_fusion.1
  335.7 0.7 copy.33
  336.5 1.5 slice_reduce_fusion
  338.0 1.5 slice_reduce_fusion.1
  339.5 0.0 copy-done
  339.5 1.7 copy.36
Async XLA Ops:
  329.0 10.5 %copy-start = (bf16[2048,768]{1,0:T(8,128)(2,1)S(1)}, bf16[2048,768]{1,0:T(8,128)(2,1)}, u32[]{:S(2)}) copy-start(bf16[2048,768]{1,0:T(8,128)(2,1)} %get-tuple-element.76) | copy-start | bytes 9437188

commit v3 on v2

v3 whole, which is shorter than its diff:
```python
import functools
import math

import jax
import jax.numpy as jnp
from jax import lax
from jax.experimental import pallas as pl
from jax.experimental.pallas import tpu as pltpu
from jax.sharding import PartitionSpec as P

HDIM = 64
HALF = HDIM // 2
AUG = HDIM + 16
EPS = 1e-05
ROPE_BASE = 160000.0
LOG2E = math.log2(math.e)
LN2 = math.log(2.0)
SCALE = HDIM ** (-0.5)
FAR = -1e30
BF16 = jnp.bfloat16
F32 = jnp.float32
VMEM_BYTES = 60 << 20
NN = (((1,), (0,)), ((), ()))
NT = (((1,), (1,)), ((), ()))
TN = (((0,), (0,)), ((), ()))


def dot(a, b, dims):
    return lax.dot_general(a, b, dims, preferred_element_type=F32)


def params(*semantics):
    return pltpu.CompilerParams(
        dimension_semantics=semantics or None, vmem_limit_bytes=VMEM_BYTES
    )


def whole(*shape):
    return pl.BlockSpec(shape, lambda *i: (0,) * len(shape))


def layout_rows(len_ref, docs, first, rows):
    index = first + lax.broadcasted_iota(jnp.int32, (1, rows), 1)
    segment = jnp.zeros((1, rows), jnp.int32)
    start = jnp.zeros((1, rows), jnp.int32)
    end = jnp.int32(0)
    for j in range(docs):
        end = end + len_ref[0, j]
        past = index >= end
        segment = segment + jnp.where(past, 1, 0)
        start = jnp.where(past, jnp.maximum(start, end), start)
    return segment, index - start, index < end


def normalize(columns):
    mean = jnp.mean(columns, axis=0, keepdims=True)
    centered = columns - mean
    var = jnp.mean(centered * centered, axis=0, keepdims=True)
    inv = lax.rsqrt(var + EPS)
    return centered * inv, inv


def turn(block, cos, sin, heads, back=False):
    out = []
    for h in range(heads):
        one = block[h * HDIM : h * HDIM + HALF]
        two = block[h * HDIM + HALF : (h + 1) * HDIM]
        if back:
            out += [one * cos + two * sin, two * cos - one * sin]
        else:
            out += [one * cos - two * sin, two * cos + one * sin]
    return jnp.concatenate(out, axis=0)


def gelu_parts(gate):
    phi = 0.5 * (1.0 + lax.erf(gate * math.sqrt(0.5)))
    density = jnp.exp2(gate * gate * (-0.5 * LOG2E)) * (1.0 / math.sqrt(2.0 * math.pi))
    return phi, gate * density


def last_kernel(own_axis, q_ref, k_ref, v_ref, do_ref, p_ref, cos_ref, sin_ref, n1_ref, w_ref, gq_ref, nc_ref, gc_ref, dq_ref, pc_ref, acc_ref, va_ref):
    step, head = pl.program_id(0), pl.program_id(1)
    per = pl.num_programs(1)
    features, rows = n1_ref.shape
    own = q_ref.shape[1]
    width = per * HDIM
    mine = pl.ds(pl.multiple_of(lax.axis_index(own_axis) * own, own), own)

    @pl.when((step == 0) & (head == 0))
    def _():
        va_ref[HDIM:] = jnp.full((AUG - HDIM, rows), -1.0, BF16)
        acc_ref[...] = jnp.zeros_like(acc_ref)
        gc_ref[...] = jnp.zeros_like(gc_ref)

    va_ref[:HDIM] = v_ref[...]
    cot = dot(va_ref[...], do_ref[0], TN)
    probs = p_ref[0]
    score_cot = probs * cot.astype(BF16)
    at = pl.ds(pl.multiple_of(head * HDIM, HDIM), HDIM)
    dv = dot(do_ref[0, :HDIM], probs, NT)
    dk = dot(q_ref[...], score_cot, NT) * LN2
    dq = dot(k_ref[...], score_cot, NN) * SCALE
    pc_ref[pl.ds(pl.multiple_of(width + head * HDIM, HDIM), HDIM)] = dv.astype(BF16)
    pc_ref[at] = turn(dk, cos_ref[...], sin_ref[...], 1, True).astype(BF16)
    dq_ref[at] = turn(dq, cos_ref[:, mine], sin_ref[:, mine], 1, True).astype(BF16)

    @pl.when(head == per - 1)
    def _():
        kv = dot(n1_ref[...], pc_ref[...], NT)
        q = dot(n1_ref[:, mine], dq_ref[...], NT)
        gq_ref[step, :, :width] = q.astype(BF16)
        gq_ref[step, :, width : 3 * width] = kv.astype(BF16)
        gc_ref[...] += jnp.sum(q * w_ref[0, :, :width].astype(F32), axis=1, keepdims=True) + jnp.sum(
            kv * w_ref[0, :, width : 3 * width].astype(F32), axis=1, keepdims=True
        )

        def spread(i, carry):
            cols = pl.ds(pl.multiple_of(i * own, own), own)
            acc_ref[:, cols] += dot(w_ref[0, :, width : 3 * width], pc_ref[:, cols], NN)
            return carry

        lax.fori_loop(0, rows // own, spread, 0)
        acc_ref[:, mine] += dot(w_ref[0, :, :width], dq_ref[...], NN)

    @pl.when((step == pl.num_programs(0) - 1) & (head == per - 1))
    def _():
        gain_cot = (gc_ref[...] / w_ref[0, :, 3 * width :].astype(F32)).astype(BF16)
        for m in range(gq_ref.shape[0]):
            nc_ref[m] = acc_ref[:, m * own : (m + 1) * own].astype(BF16)
            gq_ref[m, :, 3 * width :] = gain_cot


def last(q, k, v, do, p, cos, sin, n1, w_qkv, own_axis="mp"):
    (features, own), rows = q.shape, k.shape[1]
    parts = w_qkv.shape[0]
    per = features // parts // HDIM
    width = per * HDIM
    head = lambda m, h: (m * per + h, 0)
    return pl.pallas_call(
        functools.partial(last_kernel, own_axis),
        grid=(parts, per),
        in_specs=[
            pl.BlockSpec((HDIM, own), head),
            pl.BlockSpec((HDIM, rows), head),
            pl.BlockSpec((HDIM, rows), head),
            pl.BlockSpec((1, AUG, own), lambda m, h: (m * per + h, 0, 0)),
            pl.BlockSpec((1, rows, own), lambda m, h: (m * per + h, 0, 0)),
            whole(HALF, rows),
            whole(HALF, rows),
            whole(features, rows),
            pl.BlockSpec((1,) + w_qkv.shape[1:], lambda m, h: (m, 0, 0)),
        ],
        out_specs=[
            whole(*w_qkv.shape),
            whole(parts, features, own),
        ],
        out_shape=[
            jax.ShapeDtypeStruct(w_qkv.shape, BF16),
            jax.ShapeDtypeStruct((parts, features, own), BF16),
        ],
        scratch_shapes=[
            pltpu.VMEM((features, 1), F32),
            pltpu.VMEM((width, own), BF16),
            pltpu.VMEM((2 * width, rows), BF16),
            pltpu.VMEM((features, rows), F32),
            pltpu.VMEM((AUG, rows), BF16),
        ],
        compiler_params=params("arbitrary", "arbitrary"),
        name="last",
    )(q, k, v, do, p, cos, sin, n1, w_qkv)


def place():
    dp, mp = lax.axis_index("dp"), lax.axis_index("mp")
    return dp // 2, lax.rem(dp, 2), mp // 2, lax.rem(mp, 2)


def device(z, x, y, c):
    return (2 * z + x, 2 * y + c)


def remote(src, dst, send, recv, target):
    return pltpu.make_async_remote_copy(
        src_ref=src, dst_ref=dst, send_sem=send, recv_sem=recv,
        device_id=target, device_id_type=pl.DeviceIdType.MESH,
    )


def greet(targets):
    barrier = pltpu.get_barrier_semaphore()
    for target in targets:
        pl.semaphore_signal(barrier, inc=1, device_id=target, device_id_type=pl.DeviceIdType.MESH)
    pl.semaphore_wait(barrier, len(targets))


def peers(nz):
    z, x, y, c = place()
    across = [device(z, 1 - x, y, c), device(z, x, 1 - y, c), device(z, x, y, 1 - c)]
    return across + [device(lax.rem(z + d, nz), x, y, c) for d in range(1, nz)]


class Gather:
    def __init__(self, nz, src, full, send, recv, local):
        self.nz, self.src, self.full, self.send, self.recv, self.local = nz, src, full, send, recv, local
        self.depth = src.shape[0]
        self.index = {}
        for kind in ("Z", "X", "Y", "S", "YA", "XB", "SX", "SY", "SA", "SB"):
            for d in range(1 if kind == "Z" else 0, nz):
                self.index[kind, d] = len(self.index)

    @staticmethod
    def count(nz):
        return nz - 1 + 9 * nz

    def block(self, z, x, y, c, half=None):
        first, size = (0, self.depth) if half is None else (half * self.depth // 2, self.depth // 2)
        return self.full.at[2 * y + c, pl.ds(pl.multiple_of((2 * z + x) * self.depth + first, 16), size)]

    def message(self, kind, d, sending):
        z, x, y, c = place()
        nz = self.nz
        back = z if d == 0 else lax.rem(z - d + nz, nz)
        ahead = lax.rem(z + d, nz)
        sx, sy, sib = device(z, 1 - x, y, c), device(z, x, 1 - y, c), device(z, x, y, 1 - c)
        sent, got, half, target = {
            "Z": ((z, x, y, c), (back, x, y, c), None, device(ahead, x, y, c)),
            "X": ((back, x, y, c), (back, 1 - x, y, c), None, sx),
            "Y": ((back, x, y, c), (back, x, 1 - y, c), None, sy),
            "S": ((back, x, y, c), (back, x, y, 1 - c), None, sib),
            "YA": ((back, 1 - x, y, c), (back, 1 - x, 1 - y, c), 0, sy),
            "XB": ((back, x, 1 - y, c), (back, 1 - x, 1 - y, c), 1, sx),
            "SX": ((back, 1 - x, y, c), (back, 1 - x, y, 1 - c), None, sib),
            "SY": ((back, x, 1 - y, c), (back, x, 1 - y, 1 - c), None, sib),
            "SA": ((back, 1 - x, 1 - y, c), (back, 1 - x, 1 - y, 1 - c), 0, sib),
            "SB": ((back, 1 - x, 1 - y, c), (back, 1 - x, 1 - y, 1 - c), 1, sib),
        }[kind]
        i = self.index[kind, d]
        at = self.block(*(sent if sending else got), half)
        own = sending and (kind == "Z" or (d == 0 and kind in ("X", "Y", "S")))
        return remote(self.src if own else at, at, self.send.at[i], self.recv.at[i], target)

    def start(self, kind, d):
        self.message(kind, d, True).start()

    def arrived(self, kind, d):
        self.message(kind, d, False).wait_recv()

    def own(self):
        z, x, y, c = place()
        return pltpu.make_async_copy(self.src, self.block(z, x, y, c), self.local)

    def begin(self):
        for d in range(1, self.nz):
            self.start("Z", d)
        for kind in ("X", "Y", "S"):
            self.start(kind, 0)
        self.own().start()

    def along(self, d):
        self.arrived("Z", d)
        for kind in ("X", "Y", "S"):
            self.start(kind, d)

    def over(self, d):
        self.arrived("X", d)
        self.start("YA", d)
        self.start("SX", d)
        self.arrived("Y", d)
        self.start("XB", d)
        self.start("SY", d)

    def corner(self, d):
        self.arrived("YA", d)
        self.start("SA", d)
        self.arrived("XB", d)
        self.start("SB", d)

    def end(self):
        self.own().wait()
        for d in range(self.nz):
            for kind in ("S", "SX", "SY", "SA", "SB"):
                self.arrived(kind, d)
        for kind, d in self.index:
            self.message(kind, d, True).wait_send()

    def order(self):
        nz = self.nz
        near = sorted(range(1, nz), key=lambda d: min(d, nz - d))
        steps = [functools.partial(self.begin)]
        for d in [0] + near:
            if d:
                steps.append(functools.partial(self.along, d))
            steps.append(functools.partial(self.over, d))
        for d in [0] + near:
            steps.append(functools.partial(self.corner, d))
        return steps + [self.end]


class Share:
    def __init__(self, src, full, send, recv, local, pieces=1):
        self.src, self.full, self.send, self.recv, self.local, self.pieces = src, full, send, recv, local, pieces
        self.size = src.shape[0] // pieces

    @staticmethod
    def sems(pieces):
        dma = pltpu.SemaphoreType.DMA
        return [dma((3 * pieces,)), dma((3 * pieces,)), dma((pieces,))]

    def rows(self, y, c, i):
        own = self.size * self.pieces
        return pl.ds(pl.multiple_of((2 * y + c) * own + i * self.size, 16), self.size)

    def message(self, kind, i):
        z, x, y, c = place()
        n = self.pieces
        piece = self.src.at[pl.ds(i * self.size, self.size)]
        if kind == "own":
            return pltpu.make_async_copy(piece, self.full.at[self.rows(y, c, i)], self.local.at[i])
        k = {"Y": 0, "C": 1, "F": 2}[kind] * n + i
        sems = self.send.at[k], self.recv.at[k]
        sib = device(z, x, y, 1 - c)
        if kind == "Y":
            return remote(piece, self.full.at[self.rows(y, c, i)], *sems, device(z, x, 1 - y, c))
        if kind == "C":
            return remote(piece, self.full.at[self.rows(y, c, i)], *sems, sib)
        at = self.full.at[self.rows(1 - y, c, i)]
        return remote(at, at, *sems, sib)

    def begin(self, i):
        for kind in ("Y", "C", "own"):
            self.message(kind, i).start()

    def on(self, i):
        self.message("Y", i).wait_recv()
        self.message("F", i).start()

    def end(self):
        for i in range(self.pieces):
            self.message("own", i).wait()
            self.message("C", i).wait_recv()
            self.message("F", i).wait_recv()
            for kind in ("Y", "C", "F"):
                self.message(kind, i).wait_send()


def finish(tokens, gain, cot, middle_cot):
    hat, inv_sigma = normalize(tokens.T.astype(F32))
    d = cot * gain
    made = middle_cot + inv_sigma * (
        d - jnp.mean(d, axis=0, keepdims=True) - hat * jnp.mean(d * hat, axis=0, keepdims=True)
    )
    return made.T.astype(BF16)


class Scatter:
    def __init__(self, nz, ups, src, part, out, core, side, line, last, send, recv, shared=None):
        self.nz, self.ups, self.src, self.part, self.out, self.shared = nz, ups, src, part, out, shared
        self.core, self.side, self.line, self.last, self.send, self.recv = core, side, line, last, send, recv
        self.depth = out.shape[0]

    @staticmethod
    def scratch(nz, ups, depth, columns):
        count = len(ups) * nz + 2 * nz
        return [
            pltpu.VMEM((len(ups), 2 * nz * depth, columns), BF16),
            pltpu.VMEM((len(ups), nz * depth, columns), BF16),
            pltpu.VMEM((nz, len(ups), depth, columns), BF16),
            pltpu.VMEM((depth, columns), BF16),
            pltpu.SemaphoreType.DMA((count,)),
            pltpu.SemaphoreType.DMA((count,)),
        ]

    def row(self, d):
        z, _, _, _ = place()
        return z if d == 0 else lax.rem(z + d, self.nz)

    def rows(self, d, x):
        return pl.ds(pl.multiple_of((2 * self.row(d) + x) * self.depth, 16), self.depth)

    def both(self, d):
        return pl.ds(pl.multiple_of(2 * self.row(d) * self.depth, 16), 2 * self.depth)

    def lane(self, d):
        return pl.ds(pl.multiple_of(self.row(d) * self.depth, 16), self.depth)

    def message(self, kind, d, u=0):
        z, x, y, c = place()
        nz, n = self.nz, len(self.ups)
        i = {"C": u * nz + d, "X": n * nz + d, "Z": n * nz + nz + d, "Y": n * nz + nz}[kind]
        sems = self.send.at[i], self.recv.at[i]
        if kind == "C":
            both = self.both(d)
            return remote(self.src.at[2 * self.ups[u] + 1 - c, both], self.core.at[u, both], *sems, device(z, x, y, 1 - c))
        if kind == "X":
            return remote(
                self.core.at[:, self.rows(d, 1 - x)], self.side.at[:, self.lane(d)], *sems, device(z, 1 - x, y, c)
            )
        if kind == "Z":
            return remote(self.side.at[:, self.lane(d)], self.line.at[d], *sems, device(self.row(d), x, y, c))
        return remote(self.line.at[0, 1 - y if n == 2 else 0], self.last, *sems, device(z, x, 1 - y, c))

    def far(self):
        return [*range(1, self.nz), 0]

    def begin(self):
        for d in self.far():
            for u in range(len(self.ups)):
                self.message("C", d, u).start()

    def chip(self, d):
        _, x, _, c = place()
        for u in range(len(self.ups)):
            self.message("C", d, u).wait_recv()
        for near in (False, True):
            rows = self.rows(d, x if near else 1 - x)
            for u, up in enumerate(self.ups):
                made = self.part[2 * up + c, rows].astype(F32) + self.core[u, rows].astype(F32)
                self.core[u, rows] = made.astype(BF16)
            if not near:
                self.message("X", d).start()

    def over(self, d):
        _, x, _, _ = place()
        self.message("X", d).wait_recv()
        rows, lane = self.rows(d, x), self.lane(d)
        for u in range(len(self.ups)):
            made = self.core[u, rows].astype(F32) + self.side[u, lane].astype(F32)
            self.side[u, lane] = made.astype(BF16)
        if d:
            self.message("Z", d).start()

    def along(self):
        _, _, y, _ = place()
        for d in range(1, self.nz):
            self.message("Z", d).wait_recv()
        lane = self.lane(0)
        for u in range(len(self.ups)):
            made = self.side[u, lane].astype(F32)
            for d in range(1, self.nz):
                made += self.line[d, u].astype(F32)
            self.line[0, u] = made.astype(BF16)
        if len(self.ups) == 2 or self.shared:
            self.message("Y", 0).start()
        else:
            pl.when(y != self.ups[0])(lambda: self.message("Y", 0).start())

    def end(self):
        _, _, y, _ = place()

        def receive():
            self.message("Y", 0).wait_recv()
            mine = self.line[0, y if len(self.ups) == 2 else 0]
            self.out[...] = mine.astype(F32) + self.last[...].astype(F32)

        if len(self.ups) == 2:
            receive()
            self.message("Y", 0).wait_send()
        elif self.shared:
            pl.when(y == self.ups[0])(receive)

            @pl.when(y != self.ups[0])
            def _():
                self.message("Y", 0).wait_recv()
                self.out[:, self.shared :] = self.line[0, 0, :, self.shared :].astype(F32) + self.last[
                    :, self.shared :
                ].astype(F32)

            self.message("Y", 0).wait_send()
        else:
            pl.when(y == self.ups[0])(receive)
            pl.when(y != self.ups[0])(lambda: self.message("Y", 0).wait_send())
        for d in range(self.nz):
            for u in range(len(self.ups)):
                self.message("C", d, u).wait_send()
            self.message("X", d).wait_send()
            if d:
                self.message("Z", d).wait_send()

    def order(self):
        return (
            [self.begin]
            + [functools.partial(self.chip, d) for d in self.far()]
            + [functools.partial(self.over, d) for d in self.far()]
            + [self.along, self.end]
        )


class Fold:
    def __init__(self, part, near, far, send, recv):
        self.part, self.near, self.far, self.send, self.recv = part, near, far, send, recv
        self.slots = part.shape[0]

    @staticmethod
    def scratch(n_mp, own, slots):
        dma = pltpu.SemaphoreType.DMA
        return [
            pltpu.VMEM((slots, n_mp, 2 * HDIM, own), BF16),
            pltpu.VMEM((slots, 2, 2 * HDIM, own), BF16),
            pltpu.VMEM((slots, 2 * HDIM, own), BF16),
            dma((slots, 3)),
            dma((slots, 3)),
        ]

    def message(self, kind, head):
        z, x, y, c = place()
        slot = lax.rem(head, self.slots)
        k = {"far": 0, "near": 1, "Y": 2}[kind]
        sems = self.send.at[slot, k], self.recv.at[slot, k]
        if kind == "Y":
            return remote(self.near.at[slot, 1 - y], self.far.at[slot], *sems, device(z, x, 1 - y, c))
        up = 1 - y if kind == "far" else y
        return remote(self.part.at[slot, 2 * up + 1 - c], self.near.at[slot, up], *sems, device(z, x, y, 1 - c))

    def begin(self, head):
        self.message("far", head).start()
        self.message("near", head).start()

    def chip(self, head):
        _, _, y, c = place()
        slot = lax.rem(head, self.slots)
        self.message("far", head).wait_recv()
        made = self.part[slot, 2 * (1 - y) + c].astype(F32) + self.near[slot, 1 - y].astype(F32)
        self.near[slot, 1 - y] = made.astype(BF16)
        self.message("Y", head).start()

    def end(self, head):
        _, _, y, c = place()
        slot = lax.rem(head, self.slots)
        self.message("near", head).wait_recv()
        self.message("Y", head).wait_recv()
        made = self.part[slot, 2 * y + c].astype(F32) + self.near[slot, y].astype(F32) + self.far[slot].astype(F32)
        for kind in ("far", "near", "Y"):
            self.message(kind, head).wait_send()
        return made.astype(BF16)


def project(w_ref, part, n1_ref, cos_ref, sin_ref, mine, q_ref, k_ref, v_ref):
    width, own = q_ref.shape
    heads = width // HDIM

    def some(i, carry):
        at = pl.ds(pl.multiple_of(i * own, own), own)
        made = dot(w_ref[part, :, width : 3 * width], n1_ref[:, at], TN)
        k_ref[:, at] = turn(made[:width], cos_ref[:, at], sin_ref[:, at], heads).astype(BF16)
        v_ref[:, at] = made[width:].astype(BF16)
        return carry

    lax.fori_loop(0, n1_ref.shape[1] // own, some, 0)
    made = dot(w_ref[part, :, :width], n1_ref[:, mine], TN) * (SCALE * LOG2E)
    q_ref[...] = turn(made, cos_ref[:, mine], sin_ref[:, mine], heads).astype(BF16)


def forward_kernel(nz, len_ref, tok_ref, *refs):
    linked = nz > 0
    given, refs = refs[: 6 if linked else 1], refs[6 if linked else 1 :]
    mine_ref, q_ref, k_ref, v_ref, cos_ref, sin_ref, o_ref, p_ref, inv_ref = refs[:9]
    full_refs, refs = refs[9 : 11 if linked else 9], refs[11 if linked else 9 :]
    w_ref, n1_ref, ka_ref, qa_ref, va_ref, load = refs[:6]
    refs = refs[6:]
    rows, features = tok_ref.shape
    own = q_ref.shape[1]
    docs = len_ref.shape[1]
    width = q_ref.shape[0]
    per = width // HDIM
    step = pl.program_id(0)
    me = lax.axis_index("mp")
    mine = pl.ds(pl.multiple_of(me * own, own), own)

    if linked:
        src_a, src_b = refs[:2]
        one = Gather(nz, src_a, w_ref, *refs[2:5])
        two = Gather(nz, src_b, full_refs[1], *refs[5:8])
        keep = pltpu.make_async_copy(w_ref, full_refs[0], load)

    @pl.when(step == 0)
    def _():
        if linked:
            wq_ref, wg_ref, wo_ref, wd_ref, one_ref, two_ref = given
            for i in range(3):
                src_a[:, i * width : (i + 1) * width] = wq_ref[i]
            src_a[:, 3 * width :] = one_ref[...].astype(F32).T.astype(BF16)
            greet(peers(nz))
            first = one.order()
            first[0]()
            units = wd_ref.shape[0]
            pair = 2 * units
            for i in range(2):
                src_b[:, i * units : (i + 1) * units] = wg_ref[i]
            src_b[:, pair : pair + width] = wo_ref[...].T
            src_b[:, pair + width : pair + width + units] = wd_ref[...].T
            src_b[:, pair + width + units :] = two_ref[...].astype(F32).T.astype(BF16)
        else:
            fetch = pltpu.make_async_copy(given[0], w_ref, load)
            fetch.start()

        _, position, _ = layout_rows(len_ref, docs, 0, rows)
        power = lax.broadcasted_iota(jnp.int32, (HALF, 1), 0).astype(F32) * (-2.0 / HDIM * math.log2(ROPE_BASE))
        angle = position.astype(F32) * jnp.exp2(power)
        cos_ref[...] = jnp.cos(angle)
        sin_ref[...] = jnp.sin(angle)
        keys, _, _ = layout_rows(len_ref, docs, 0, rows)
        queries, _, _ = layout_rows(len_ref, docs, me * own, own)
        kind = lax.broadcasted_iota(jnp.int32, (AUG - HDIM, 1), 0)
        ka_ref[HDIM:] = jnp.where(kind == keys, 1.0, 0.0).astype(BF16)
        qa_ref[HDIM:] = jnp.where(kind == queries, 0.0, FAR).astype(BF16)
        va_ref[HDIM:] = jnp.ones((AUG - HDIM, rows), BF16)
        if linked:
            for act in first[1:]:
                act()
            keep.start()
            two.begin()
        else:
            fetch.wait()
        gain = w_ref[0, :, 3 * width :].astype(F32)

        def norm(i, carry):
            at = pl.ds(pl.multiple_of(i * own, own), own)
            hat, _ = normalize(tok_ref[at, :].T.astype(F32))
            n1_ref[:, at] = (hat * gain).astype(BF16)
            return carry

        lax.fori_loop(0, rows // own, norm, 0)
        mine_ref[...] = n1_ref[:, mine]

    if linked:
        acts = two.order()[1:]
        heads = pl.num_programs(0)
        for at, act in zip(spread(len(acts), 12), acts):
            pl.when(step == at)(act)

    @pl.when(lax.rem(step, per) == 0)
    def _():
        project(w_ref, step // per, n1_ref, cos_ref, sin_ref, mine, q_ref, k_ref, v_ref)

    head = pl.ds(pl.multiple_of(lax.rem(step, per) * HDIM, HDIM), HDIM)
    ka_ref[:HDIM] = k_ref[head]
    qa_ref[:HDIM] = q_ref[head]
    va_ref[:HDIM] = v_ref[head]
    wide = 256
    for i in range(own // wide):
        at = slice(i * wide, (i + 1) * wide)
        scores = dot(ka_ref[...], qa_ref[:, at], TN)
        top = jnp.max(scores, axis=0, keepdims=True)
        probs = jnp.exp2(scores - top).astype(BF16)
        p_ref[0, :, at] = probs
        out = dot(va_ref[...], probs, NN)
        inv = 1.0 / out[HDIM : HDIM + 1]
        o_ref[:, at] = (out[:HDIM] * inv).astype(BF16)
        inv_ref[0, :, at] = inv
    if linked:

        @pl.when(step == pl.num_programs(0) - 1)
        def _():
            keep.wait()


def spread(count, steps):
    return [min(steps - 1, 1 + i * (steps - 1) // count) for i in range(count)]


def forward(nz, n_mp, lengths, tokens, weights, columns):
    rows, features = tokens.shape
    own, width, heads = rows // n_mp, features // n_mp, features // HDIM
    per = width // HDIM
    linked = nz > 0
    hbm = pl.BlockSpec(memory_space=pl.ANY)
    part = lambda h: (h // per, 0)
    vm = pl.BlockSpec(memory_space=pltpu.VMEM)
    n = Gather.count(nz) if linked else 0
    dma = pltpu.SemaphoreType.DMA
    depth = features // (2 * nz) if linked else 0
    full_shapes = [jax.ShapeDtypeStruct((n_mp, features, c), BF16) for c in columns] if linked else []
    return pl.pallas_call(
        functools.partial(forward_kernel, nz),
        grid=(heads,),
        in_specs=[pl.BlockSpec(memory_space=pltpu.SMEM), vm] + ([vm] * 6 if linked else [hbm]),
        out_specs=[
            whole(features, own),
            pl.BlockSpec((width, own), part),
            pl.BlockSpec((width, rows), part),
            pl.BlockSpec((width, rows), part),
            whole(HALF, rows),
            whole(HALF, rows),
            pl.BlockSpec((HDIM, own), lambda h: (h, 0)),
            pl.BlockSpec((1, rows, own), lambda h: (h, 0, 0)),
            pl.BlockSpec((1, 1, own), lambda h: (h, 0, 0)),
        ]
        + [hbm] * len(full_shapes),
        out_shape=[
            jax.ShapeDtypeStruct((features, own), BF16),
            jax.ShapeDtypeStruct((features, own), BF16),
            jax.ShapeDtypeStruct((features, rows), BF16),
            jax.ShapeDtypeStruct((features, rows), BF16),
            jax.ShapeDtypeStruct((HALF, rows), F32),
            jax.ShapeDtypeStruct((HALF, rows), F32),
            jax.ShapeDtypeStruct((features, own), BF16),
            jax.ShapeDtypeStruct((heads, rows, own), BF16),
            jax.ShapeDtypeStruct((heads, 1, own), F32),
        ]
        + full_shapes,
        scratch_shapes=[
            pltpu.VMEM((n_mp, features, columns[0]), BF16),
            pltpu.VMEM((features, rows), BF16),
            pltpu.VMEM((AUG, rows), BF16),
            pltpu.VMEM((AUG, own), BF16),
            pltpu.VMEM((AUG, rows), BF16),
            dma,
        ]
        + (
            [pltpu.VMEM((depth, c), BF16) for c in columns] + [dma((n,)), dma((n,)), dma] * 2
            if linked
            else []
        ),
        compiler_params=pltpu.CompilerParams(
            dimension_semantics=("arbitrary",),
            vmem_limit_bytes=VMEM_BYTES,
            **({"collective_id": 1, "has_side_effects": True} if linked else {}),
        ),
        name="forward",
    )(lengths, tokens, *weights)


def mid_kernel(
    linked, units, len_ref, tok_hbm, cot_hbm, heads_ref, inv_ref, w_hbm,
    out_ref, mcot_ref, do_ref, g_ref, tok_ref, cot_ref, w_ref, load, *share,
):
    own, features = tok_ref.shape
    me = lax.axis_index("mp")
    mine = pl.ds(pl.multiple_of(me * own, own), own)
    loads = [
        pltpu.make_async_copy(tok_hbm.at[mine], tok_ref, load.at[0]),
        pltpu.make_async_copy(cot_hbm.at[mine], cot_ref, load.at[1]),
        pltpu.make_async_copy(w_hbm, w_ref, load.at[2]),
    ]
    for copy in loads:
        copy.start()
    if linked:
        out_own = share[0]
        share = Share(out_own, out_ref, *share[1:])
        greet(peers(1))
    else:
        out_own = out_ref
    parts = w_ref.shape[0]
    width = features // parts
    heads = width // HDIM
    pair = 2 * units
    _, _, live = layout_rows(len_ref, len_ref.shape[1], me * own, own)
    for copy in loads:
        copy.wait()

    def w_gu(m):
        return w_ref[m, :, :pair]

    def w_out(m):
        return w_ref[m, :, pair : pair + width]

    def w_down(m):
        return w_ref[m, :, pair + width : pair + width + units]

    total = dot(w_out(0), heads_ref[:width], NN)
    for m in range(1, parts):
        total += dot(w_out(m), heads_ref[m * width : (m + 1) * width], NN)
    middle = tok_ref[...].T.astype(F32) + total
    gain = w_ref[0, :, pair + width + units :].astype(F32)
    hat, inv_sigma = normalize(middle)
    normed = (hat * gain).astype(BF16)
    branch = jnp.where(live, cot_ref[...].T.astype(F32), 0.0).astype(BF16)
    total = middle
    back = jnp.zeros((features, own), F32)
    kept = []
    for m in range(parts):
        gate_up = dot(w_gu(m), normed, TN)
        gate, up = gate_up[:units], gate_up[units:]
        phi, slope = gelu_parts(gate)
        act = gate * phi
        hidden = (act * up).astype(BF16)
        total += dot(w_down(m), hidden, NN)
        kept.append((hidden, up * (phi + slope), act))
    out_own[...] = total.astype(BF16).T
    if linked:
        share.begin(0)
    for m in range(parts):
        hidden, one, two = kept[m]
        hidden_cot = dot(w_down(m), branch, TN)
        g_ref[m, :, pair + width : pair + width + units] = dot(branch, hidden, NT).astype(BF16)
        cots = jnp.concatenate([hidden_cot * one, hidden_cot * two], axis=0).astype(BF16)
        g_ref[m, :, :pair] = dot(normed, cots, NT).astype(BF16)
        back += dot(w_gu(m), cots, NN)
    gain_cot = jnp.sum(back * hat, axis=1, keepdims=True).astype(BF16)
    d = back * gain
    middle_cot = branch.astype(F32) + inv_sigma * (
        d - jnp.mean(d, axis=0, keepdims=True) - hat * jnp.mean(d * hat, axis=0, keepdims=True)
    )
    mcot_ref[...] = middle_cot
    attn_cot = middle_cot.astype(BF16)
    for m in range(parts):
        g_ref[m, :, pair + width + units :] = gain_cot
        part = heads_ref[m * width : (m + 1) * width]
        g_ref[m, :, pair : pair + width] = dot(attn_cot, part, NT).astype(BF16)
        back_heads = dot(w_out(m), attn_cot, TN)
        for h in range(heads):
            head = m * heads + h
            rows = slice(h * HDIM, (h + 1) * HDIM)
            cot = back_heads[rows] * inv_ref[head]
            inner = jnp.sum(cot * part[rows].astype(F32), axis=0, keepdims=True)
            high = inner.astype(BF16).astype(F32)
            pad = jnp.zeros((AUG - HDIM - 2, own), F32)
            do_ref[head] = jnp.concatenate([cot, high, inner - high, pad], axis=0).astype(BF16)
    if linked:
        share.on(0)
        share.end()


def mid(linked, n_mp, lengths, tokens, out_grad, heads_out, inv, w_rest, units):
    features, own = heads_out.shape
    heads = inv.shape[0]
    vm = pl.BlockSpec(memory_space=pltpu.VMEM)
    hbm = pl.BlockSpec(memory_space=pl.ANY)
    return pl.pallas_call(
        functools.partial(mid_kernel, linked, units),
        in_specs=[pl.BlockSpec(memory_space=pltpu.SMEM), hbm, hbm, vm, vm, hbm],
        out_specs=[hbm if linked else vm] + [vm] * 3,
        out_shape=[
            jax.ShapeDtypeStruct((own * n_mp if linked else own, features), BF16),
            jax.ShapeDtypeStruct((features, own), F32),
            jax.ShapeDtypeStruct((heads, AUG, own), BF16),
            jax.ShapeDtypeStruct(w_rest.shape, BF16),
        ],
        scratch_shapes=[
            pltpu.VMEM((own, features), BF16),
            pltpu.VMEM((own, features), BF16),
            pltpu.VMEM(w_rest.shape, BF16),
            pltpu.SemaphoreType.DMA((3,)),
        ]
        + ([pltpu.VMEM((own, features), BF16)] + Share.sems(1) if linked else []),
        compiler_params=pltpu.CompilerParams(
            vmem_limit_bytes=VMEM_BYTES, **({"collective_id": 2, "has_side_effects": True} if linked else {})
        ),
        name="mid",
    )(lengths, tokens, out_grad, heads_out, inv, w_rest)


SLOTS = 4


def backward_kernel(nz, *refs):
    q_ref, k_ref, v_ref, do_ref, p_ref, cos_ref, sin_ref, n1_ref, mcot_ref, tok_hbm, w_hbm, gr_hbm = refs[:12]
    dq_ref, dr_ref, in_full = refs[12:15]
    w_ref, gr_ref, gq_ref, pc_ref, acc_ref, gc_ref, va_ref, tok_ref, in_own, load = refs[15:25]
    refs = refs[25:]
    rest = Scatter(nz, (0, 1), gr_hbm, gr_ref, dr_ref, *refs[:6])
    low = Scatter(nz, (0,), gq_ref, gq_ref, dq_ref, *refs[6:12])
    high = Scatter(nz, (1,), gq_ref, gq_ref, dq_ref, *refs[12:18], shared=gq_ref.shape[2] - 1)
    fold = Fold(*refs[18:23])
    share = Share(in_own, in_full, *refs[23:26])
    step, heads = pl.program_id(0), pl.num_programs(0)
    parts = w_ref.shape[0]
    features, own = n1_ref.shape
    rows = k_ref.shape[1]
    width = features // parts
    per = width // HDIM
    me = lax.axis_index("mp")
    mine = pl.ds(pl.multiple_of(me * own, own), own)
    loads = [
        pltpu.make_async_copy(w_hbm, w_ref, load.at[0]),
        pltpu.make_async_copy(gr_hbm, gr_ref, load.at[1]),
        pltpu.make_async_copy(tok_hbm.at[mine], tok_ref, load.at[2]),
    ]

    @pl.when(step == 0)
    def _():
        for copy in loads:
            copy.start()
        greet(peers(nz))
        rest.begin()
        va_ref[HDIM:] = jnp.full((AUG - HDIM, rows), -1.0, BF16)
        acc_ref[...] = jnp.zeros_like(acc_ref)
        gc_ref[...] = jnp.zeros_like(gc_ref)
        for m in range(2):
            gq_ref[m, :, 3 * width :] = jnp.zeros((features, 1), BF16)

    @pl.when(step == 1)
    def _():
        for copy in loads:
            copy.wait()

    def collect(head):
        made = fold.end(head)
        at = lax.rem(head, per) * HDIM
        pc_ref[pl.ds(pl.multiple_of(width + at, HDIM), HDIM)] = made[:HDIM]
        pc_ref[pl.ds(pl.multiple_of(2 * width + at, HDIM), HDIM)] = made[HDIM:]

    def close(part):
        for i in range(per):
            pc_ref[i * HDIM : (i + 1) * HDIM] = qc_ref[lax.rem(part, 2), i * HDIM : (i + 1) * HDIM]
        made = dot(n1_ref[...], pc_ref[...], NT)
        gq_ref[part, :, : 3 * width] = made.astype(BF16)
        weights = w_ref[part, :, : 3 * width]
        gc_ref[...] += jnp.sum(made * weights.astype(F32), axis=1, keepdims=True)
        acc_ref[...] += dot(weights, pc_ref[...], NN)

    qc_ref = refs[26]
    acts = rest.order()[1:]
    for at, act in zip(REST_STEPS, acts):
        pl.when(step == at)(act)

    va_ref[:HDIM] = v_ref[...]
    cot = dot(va_ref[...], do_ref[0], TN)
    probs = p_ref[0]
    score_cot = probs * cot.astype(BF16)
    dv = dot(do_ref[0, :HDIM], probs, NT).astype(BF16)
    dk = turn(dot(q_ref[...], score_cot, NT) * LN2, cos_ref[...], sin_ref[...], 1, True).astype(BF16)
    dq = turn(dot(k_ref[...], score_cot, NN) * SCALE, cos_ref[:, mine], sin_ref[:, mine], 1, True)
    slot = lax.rem(step, SLOTS)
    for m in range(parts):
        fold.part[slot, m, :HDIM] = dk[:, m * own : (m + 1) * own]
        fold.part[slot, m, HDIM:] = dv[:, m * own : (m + 1) * own]
    at = pl.ds(pl.multiple_of(lax.rem(step, per) * HDIM, HDIM), HDIM)
    qc_ref[lax.rem(step // per, 2), at] = dq.astype(BF16)

    @pl.when(step >= 2)
    def _():
        collect(step - 2)

    @pl.when(step >= 1)
    def _():
        fold.chip(step - 1)

    fold.begin(step)

    @pl.when((step >= per + 1) & (lax.rem(step - 2, per) == per - 1))
    def _():
        close((step - 2) // per)

    @pl.when(step == LOW_STEP)
    def _():
        low.begin()

    for at, act in zip(LOW_STEPS, low.order()[1:]):
        pl.when(step == at)(act)

    @pl.when(step == heads - 1)
    def _():
        collect(step - 1)
        fold.chip(step)
        for act in acts[len(REST_STEPS) :]:
            act()
        collect(step)
        close(parts - 1)
        gain = w_ref[0, :, 3 * width :].astype(F32)
        gain_cot = (gc_ref[...] / gain).astype(BF16)
        for m in range(2, parts):
            gq_ref[m, :, 3 * width :] = gain_cot
        high.begin()
        in_own[...] = finish(tok_ref[...], gain, acc_ref[...], mcot_ref[...])
        share.begin(0)
        acts_high = high.order()[1:]
        for act in low.order()[1 + len(LOW_STEPS) :]:
            act()
        for act in acts_high:
            act()
        share.on(0)
        share.end()


REST_STEPS = (1, 1, 2, 2, 5, 7, 9)
LOW_STEP = 8
LOW_STEPS = (9, 9, 10, 10)


def backward(nz, q, k, v, do, p, cos, sin, n1, mcot, tokens, w_qkv, g_rest):
    (features, own), rows = q.shape, k.shape[1]
    n_mp = w_qkv.shape[0]
    heads = features // HDIM
    width = features // n_mp
    depth = features // (2 * nz)
    columns = w_qkv.shape[2], g_rest.shape[2]
    hbm = pl.BlockSpec(memory_space=pl.ANY)
    vm = pl.BlockSpec(memory_space=pltpu.VMEM)
    row = lambda h: (h, 0)
    cube = lambda h: (h, 0, 0)
    return pl.pallas_call(
        functools.partial(backward_kernel, nz),
        grid=(heads,),
        in_specs=[
            pl.BlockSpec((HDIM, own), row),
            pl.BlockSpec((HDIM, rows), row),
            pl.BlockSpec((HDIM, rows), row),
            pl.BlockSpec((1, AUG, own), cube),
            pl.BlockSpec((1, rows, own), cube),
            vm,
            vm,
            vm,
            vm,
            hbm,
            hbm,
            hbm,
        ],
        out_specs=[vm, vm, hbm],
        out_shape=[
            jax.ShapeDtypeStruct((depth, columns[0]), F32),
            jax.ShapeDtypeStruct((depth, columns[1]), F32),
            jax.ShapeDtypeStruct((rows, features), BF16),
        ],
        scratch_shapes=[
            pltpu.VMEM(w_qkv.shape, BF16),
            pltpu.VMEM(g_rest.shape, BF16),
            pltpu.VMEM(w_qkv.shape, BF16),
            pltpu.VMEM((3 * width, own), BF16),
            pltpu.VMEM((features, own), F32),
            pltpu.VMEM((features, 1), F32),
            pltpu.VMEM((AUG, rows), BF16),
            pltpu.VMEM((own, features), BF16),
            pltpu.VMEM((own, features), BF16),
            pltpu.SemaphoreType.DMA((3,)),
        ]
        + Scatter.scratch(nz, (0, 1), depth, columns[1])
        + Scatter.scratch(nz, (0,), depth, columns[0])
        + Scatter.scratch(nz, (1,), depth, columns[0])
        + Fold.scratch(n_mp, own, SLOTS)
        + Share.sems(1)
        + [pltpu.VMEM((2, width, own), BF16)],
        compiler_params=pltpu.CompilerParams(
            dimension_semantics=("arbitrary",), collective_id=3, has_side_effects=True, vmem_limit_bytes=VMEM_BYTES
        ),
        name="backward",
    )(q, k, v, do, p, cos, sin, n1, mcot, tokens, w_qkv, g_rest)


def deliver_kernel(units, in_ref, dq_ref, dr_ref, grad_ref, gq_ref, go_ref, gg_ref, gd_ref, one_ref, two_ref):
    grad_ref[...] = in_ref[...].astype(F32)

    @pl.when(pl.program_id(0) == 0)
    def _():
        width = go_ref.shape[0]
        pair = 2 * units
        for i in range(3):
            gq_ref[i] = dq_ref[:, i * width : (i + 1) * width]
        one_ref[...] = dq_ref[:, 3 * width :].T
        for i in range(2):
            gg_ref[i] = dr_ref[:, i * units : (i + 1) * units]
        go_ref[...] = dr_ref[:, pair : pair + width].T
        gd_ref[...] = dr_ref[:, pair + width : pair + width + units].T
        two_ref[...] = dr_ref[:, pair + width + units :].T


def deliver(input_grad, d_qkv, d_rest, width, units):
    rows, features = input_grad.shape
    depth = d_qkv.shape[0]
    shape = lambda *s: jax.ShapeDtypeStruct(s, F32)
    shapes = [(3, depth, width), (width, depth), (2, depth, units), (units, depth), (1, depth), (1, depth)]
    steps = 4
    return pl.pallas_call(
        functools.partial(deliver_kernel, units),
        grid=(steps,),
        in_specs=[pl.BlockSpec((rows // steps, features), lambda i: (i, 0)), whole(*d_qkv.shape), whole(*d_rest.shape)],
        out_specs=[pl.BlockSpec((rows // steps, features), lambda i: (i, 0))] + [whole(*s) for s in shapes],
        out_shape=[shape(rows, features)] + [shape(*s) for s in shapes],
        compiler_params=params("arbitrary"),
        name="deliver",
    )(input_grad, d_qkv, d_rest)


def per_device(n_dp, n_mp, tokens, out_grad, w_qkv, w_out, w_gu, w_down, gain_attn, gain_mlp, lengths):
    rows, features = tokens.shape
    depth = w_qkv.shape[0]
    units, width = w_down.shape[0], w_out.shape[0]
    everyone = ("mp", "dp")
    linked = n_mp == 4 and n_dp % 2 == 0 and depth % 32 == 0 and features // HDIM == 12
    nz = n_dp // 2 if linked else 0
    columns = 3 * width + 1, 3 * units + width + 1
    wq, wg = w_qkv.transpose(1, 0, 2), w_gu.transpose(1, 0, 2)
    if linked:
        weights = wq, wg, w_out, w_down, gain_attn[None], gain_mlp[None]
        n1, q, k, v, cos, sin, heads_out, probs, inv, full_qkv, full_rest = forward(
            nz, n_mp, lengths, tokens, weights, columns
        )
    else:
        shards = [
            jnp.concatenate([*wq, gain_attn[:, None]], axis=1),
            jnp.concatenate([*wg, w_out.T, w_down.T, gain_mlp[:, None]], axis=1),
        ]
        full_qkv, full_rest = (
            lax.all_gather(s, everyone, axis=0, tiled=True).reshape(n_mp, features, s.shape[1]) for s in shards
        )
        n1, q, k, v, cos, sin, heads_out, probs, inv = forward(nz, n_mp, lengths, tokens, [full_qkv], columns)
    layer_out, middle_cot, do, g_rest = mid(linked, n_mp, lengths, tokens, out_grad, heads_out, inv, full_rest, units)
    if linked:
        d_qkv, d_rest, in_full = backward(nz, q, k, v, do, probs, cos, sin, n1, middle_cot, tokens, full_qkv, g_rest)
    else:
        own = middle_cot.shape[1]
        g_qkv, nc = last(q, k, v, do, probs, cos, sin, lax.all_gather(n1, "mp", axis=1, tiled=True), full_qkv)
        gain_one = full_qkv[0, :, 3 * width :].astype(F32)
        tok = lax.dynamic_slice_in_dim(tokens, lax.axis_index("mp") * own, own, 0)
        nc_own = lax.psum_scatter(nc, "mp", scatter_dimension=0, tiled=True)[0]
        in_own = finish(tok, gain_one, nc_own.astype(F32), middle_cot)
        layer_out, in_full = (lax.all_gather(v, "mp", axis=0, tiled=True) for v in (layer_out, in_own))
        d_qkv, d_rest = (
            lax.psum_scatter(
                g.reshape(n_mp * features, -1), everyone, scatter_dimension=0, tiled=True
            ).astype(F32)
            for g in (g_qkv, g_rest)
        )
    input_grad, g_q, g_o, g_g, g_d, one, two = deliver(in_full, d_qkv, d_rest, width, units)
    if not linked:
        one, two = (lax.all_gather(g, "mp")[0] for g in (one, two))
    return layer_out, input_grad, g_q.transpose(1, 0, 2), g_o, g_g.transpose(1, 0, 2), g_d, one[0], two[0]


def solution(mesh):
    n_dp, n_mp = mesh.shape["dp"], mesh.shape["mp"]
    return jax.shard_map(
        functools.partial(per_device, n_dp, n_mp),
        mesh=mesh,
        in_specs=(
            P("dp", None),
            P("dp", None),
            P("dp", None, "mp"),
            P("mp", "dp"),
            P("dp", None, "mp"),
            P("mp", "dp"),
            P("dp"),
            P("dp"),
            P("dp", None),
        ),
        out_specs=(
            P("dp", None),
            P("dp", None),
            P("dp", None, "mp"),
            P("mp", "dp"),
            P("dp", None, "mp"),
            P("mp", "dp"),
            P("dp"),
            P("dp"),
        ),
        check_vma=False,
    )
```

time: 342 us -> 268 us (0.78)
  the two profiles are of different devices: /device:TPU:9 before, /device:TPU:0 now
where the time goes in v3:
time: 268 us
  Pallas kernels  262 us (98%)
  local copies, waits for them, and re-layouts  5.16 us (2%)
    pallas_call x1, Pallas kernels, backward(): pl.pallas_call(functools.partial(backward_kernel, nz), grid=(heads,), in_...  120 us
    pallas_call x1, Pallas kernels, forward(): pl.pallas_call(functools.partial(forward_kernel, nz), grid=(heads,), in_s...  101 us
    pallas_call x1, Pallas kernels, mid(): pl.pallas_call(functools.partial(mid_kernel, linked, units), in_specs=[pl...  35.5 us
    pallas_call x1, Pallas kernels, deliver(): pl.pallas_call(functools.partial(deliver_kernel, units), grid=(steps,), i...  5.98 us

profile of v3, /device:TPU:0, one launch (start us, length us, event | category | flops | bytes accessed | tf_op | source)
XLA Modules:
  0.0 268.2 jit_solution(16258610735460401345)
XLA Ops:
  0.6 1.6 copy.20
  2.2 100.9 %forward.1 = (bf16[768,512]{1,0:T(8,128)(2,1)}, bf16[768,512]{1,0:T(8,128)(2,1)}, bf16[768,2048]{1,0:T(8,128)(2,1)}, bf16[768,2048]{1,0:T(8,128)(2,1)}, f32[32,2...) custom-call(s32[1,8]{1,0:T(1,128)} %len_ref.3, ...), custom_call_target="tpu_custom_call" | custom-call | tf_op jit(solution)/shard_map/forward/pallas_call | solution.py:673
  103.2 35.5 %mid.1 = (bf16[2048,768]{1,0:T(8,128)(2,1)}, f32[768,512]{1,0:T(8,128)}, bf16[12,80,512]{2,1,0:T(8,128)(2,1)}, bf16[4,768,1057]{2,1,0:T(8,128)(2,1)}) custom-call(s32[1,8]{1,0:T(1,128)} %len_ref.3, bf16[2048,768]{1,0:T(8,128)(2,1)} %refs_9_.1, bf16[2048,768]{1,0:T(8,128)(2,1)} %cot_hbm.1, bf16[768,512]{1,0:T(8,128)(2,1)} %get-tuple-element.33.heads_ref, ...), custom_call_target="tpu_custom_call" | custom-call | tf_op jit(solution)/shard_map/mid/pallas_call | solution.py:819
  138.6 120.0 %backward.1 = (f32[96,577]{1,0:T(8,128)}, f32[96,1057]{1,0:T(8,128)}, bf16[2048,768]{1,0:T(8,128)(2,1)}) custom-call(bf16[768,512]{1,0:T(8,128)(2,1)} %get-tuple-element.37.refs_0_, bf16[768,2048]{1,0:T(8,128)(2,1)} %get-tuple-element.38.refs_1_, bf16[768,2048]{1,0:T(8,128)(2,1)} %get-tuple-element.39.refs_2_, ...), custom_call_target="tpu_custom_call" | custom-call | tf_op jit(solution)/shard_map/backward/pallas_call | solution.py:982
  258.6 0.0 copy-start
  258.6 6.0 %deliver.1 = (f32[2048,768]{1,0:T(8,128)}, f32[3,96,192]{2,1,0:T(8,128)}, f32[192,96]{1,0:T(8,128)}, f32[2,96,288]{2,1,0:T(8,128)}, f32[288,96]{1,0:T(8,128)}, /*index=5*/f32[1,96]{1,0:T(1,128)}, f32[1,96]{1,0:T(1,128)}) custom-call(bf16[2048,768]{1,0:T(8,128)(2,1)} %get-tuple-element.48.in_ref, f32[96,577]{1,0:T(8,128)} %get-tuple-element.49.dq_ref, ...), custom_call_target="tpu_custom_call" | custom-call | tf_op jit(solution)/shard_map/deliver/pallas_call | solution.py:1053
  264.6 1.9 copy.18
  266.5 0.0 copy-done
  266.5 1.7 copy.22
Async XLA Ops:
  258.6 7.9 %copy-start = (bf16[2048,768]{1,0:T(8,128)(2,1)S(1)}, bf16[2048,768]{1,0:T(8,128)(2,1)}, u32[]{:S(2)}) copy-start(bf16[2048,768]{1,0:T(8,128)(2,1)} %get-tuple-element.74) | copy-start | bytes 9437188

commit v4 on v3

--- a/solution.py
+++ b/solution.py
@@ -52,12 +52,15 @@
     return segment, index - start, index < end
 
 
-def normalize(columns):
+def moments(columns):
     mean = jnp.mean(columns, axis=0, keepdims=True)
     centered = columns - mean
-    var = jnp.mean(centered * centered, axis=0, keepdims=True)
-    inv = lax.rsqrt(var + EPS)
-    return centered * inv, inv
+    return mean, lax.rsqrt(jnp.mean(centered * centered, axis=0, keepdims=True) + EPS)
+
+
+def normalize(columns):
+    mean, inv = moments(columns)
+    return (columns - mean) * inv, inv
 
 
 def turn(block, cos, sin, heads, back=False):
@@ -196,7 +199,7 @@
 def peers(nz):
     z, x, y, c = place()
     across = [device(z, 1 - x, y, c), device(z, x, 1 - y, c), device(z, x, y, 1 - c)]
-    return across + [device(lax.rem(z + d, nz), x, y, c) for d in range(1, nz)]
+    return across + [device(lax.bitwise_xor(z, d), x, y, c) for d in range(1, nz)]
 
 
 class Gather:
@@ -218,12 +221,10 @@
 
     def message(self, kind, d, sending):
         z, x, y, c = place()
-        nz = self.nz
-        back = z if d == 0 else lax.rem(z - d + nz, nz)
-        ahead = lax.rem(z + d, nz)
+        back = lax.bitwise_xor(z, d)
         sx, sy, sib = device(z, 1 - x, y, c), device(z, x, 1 - y, c), device(z, x, y, 1 - c)
         sent, got, half, target = {
-            "Z": ((z, x, y, c), (back, x, y, c), None, device(ahead, x, y, c)),
+            "Z": ((z, x, y, c), (back, x, y, c), None, device(back, x, y, c)),
             "X": ((back, x, y, c), (back, 1 - x, y, c), None, sx),
             "Y": ((back, x, y, c), (back, x, 1 - y, c), None, sy),
             "S": ((back, x, y, c), (back, x, y, 1 - c), None, sib),
@@ -250,14 +251,15 @@
         return pltpu.make_async_copy(self.src, self.block(z, x, y, c), self.local)
 
     def begin(self):
-        for d in range(1, self.nz):
-            self.start("Z", d)
+        self.start("Z", 1)
         for kind in ("X", "Y", "S"):
             self.start(kind, 0)
         self.own().start()
 
     def along(self, d):
         self.arrived("Z", d)
+        if d + 1 < self.nz:
+            self.start("Z", d + 1)
         for kind in ("X", "Y", "S"):
             self.start(kind, d)
 
@@ -282,18 +284,6 @@
                 self.arrived(kind, d)
         for kind, d in self.index:
             self.message(kind, d, True).wait_send()
-
-    def order(self):
-        nz = self.nz
-        near = sorted(range(1, nz), key=lambda d: min(d, nz - d))
-        steps = [functools.partial(self.begin)]
-        for d in [0] + near:
-            if d:
-                steps.append(functools.partial(self.along, d))
-            steps.append(functools.partial(self.over, d))
-        for d in [0] + near:
-            steps.append(functools.partial(self.corner, d))
-        return steps + [self.end]
 
 
 class Share:
@@ -372,7 +362,7 @@
 
     def row(self, d):
         z, _, _, _ = place()
-        return z if d == 0 else lax.rem(z + d, self.nz)
+        return lax.bitwise_xor(z, d)
 
     def rows(self, d, x):
         return pl.ds(pl.multiple_of((2 * self.row(d) + x) * self.depth, 16), self.depth)
@@ -399,25 +389,23 @@
             return remote(self.side.at[:, self.lane(d)], self.line.at[d], *sems, device(self.row(d), x, y, c))
         return remote(self.line.at[0, 1 - y if n == 2 else 0], self.last, *sems, device(z, x, 1 - y, c))
 
-    def far(self):
-        return [*range(1, self.nz), 0]
-
-    def begin(self):
-        for d in self.far():
+    def begin(self, *rows):
+        for d in rows:
             for u in range(len(self.ups)):
                 self.message("C", d, u).start()
+
+    def cross(self, d):
+        self.message("X", d).start()
 
     def chip(self, d):
         _, x, _, c = place()
         for u in range(len(self.ups)):
             self.message("C", d, u).wait_recv()
-        for near in (False, True):
-            rows = self.rows(d, x if near else 1 - x)
+        for side in range(2):
+            rows = self.rows(d, side)
             for u, up in enumerate(self.ups):
                 made = self.part[2 * up + c, rows].astype(F32) + self.core[u, rows].astype(F32)
                 self.core[u, rows] = made.astype(BF16)
-            if not near:
-                self.message("X", d).start()
 
     def over(self, d):
         _, x, _, _ = place()
@@ -476,14 +464,6 @@
             if d:
                 self.message("Z", d).wait_send()
 
-    def order(self):
-        return (
-            [self.begin]
-            + [functools.partial(self.chip, d) for d in self.far()]
-            + [functools.partial(self.over, d) for d in self.far()]
-            + [self.along, self.end]
-        )
-
 
 class Fold:
     def __init__(self, part, near, far, send, recv):
@@ -538,14 +518,9 @@
     width, own = q_ref.shape
     heads = width // HDIM
 
-    def some(i, carry):
-        at = pl.ds(pl.multiple_of(i * own, own), own)
-        made = dot(w_ref[part, :, width : 3 * width], n1_ref[:, at], TN)
-        k_ref[:, at] = turn(made[:width], cos_ref[:, at], sin_ref[:, at], heads).astype(BF16)
-        v_ref[:, at] = made[width:].astype(BF16)
-        return carry
-
-    lax.fori_loop(0, n1_ref.shape[1] // own, some, 0)
+    made = dot(w_ref[part, :, width : 3 * width], n1_ref[...], TN)
+    k_ref[...] = turn(made[:width], cos_ref[...], sin_ref[...], heads).astype(BF16)
+    v_ref[...] = made[width:].astype(BF16)
     made = dot(w_ref[part, :, :width], n1_ref[:, mine], TN) * (SCALE * LOG2E)
     q_ref[...] = turn(made, cos_ref[:, mine], sin_ref[:, mine], heads).astype(BF16)
 
@@ -555,8 +530,8 @@
     given, refs = refs[: 6 if linked else 1], refs[6 if linked else 1 :]
     mine_ref, q_ref, k_ref, v_ref, cos_ref, sin_ref, o_ref, p_ref, inv_ref = refs[:9]
     full_refs, refs = refs[9 : 11 if linked else 9], refs[11 if linked else 9 :]
-    w_ref, n1_ref, ka_ref, qa_ref, va_ref, load = refs[:6]
-    refs = refs[6:]
+    w_ref, n1_ref, ka_ref, qa_ref, va_ref, stat_ref, load = refs[:7]
+    refs = refs[7:]
     rows, features = tok_ref.shape
     own = q_ref.shape[1]
     docs = len_ref.shape[1]
@@ -580,8 +555,7 @@
                 src_a[:, i * width : (i + 1) * width] = wq_ref[i]
             src_a[:, 3 * width :] = one_ref[...].astype(F32).T.astype(BF16)
             greet(peers(nz))
-            first = one.order()
-            first[0]()
+            one.begin()
             units = wd_ref.shape[0]
             pair = 2 * units
             for i in range(2):
@@ -604,29 +578,43 @@
         ka_ref[HDIM:] = jnp.where(kind == keys, 1.0, 0.0).astype(BF16)
         qa_ref[HDIM:] = jnp.where(kind == queries, 0.0, FAR).astype(BF16)
         va_ref[HDIM:] = jnp.ones((AUG - HDIM, rows), BF16)
+
+        def measure(i, carry):
+            at = pl.ds(pl.multiple_of(i * own, own), own)
+            turned = tok_ref[at, :].T
+            n1_ref[:, at] = turned
+            mean, inv = moments(turned.astype(F32))
+            stat_ref[0:1, at] = mean
+            stat_ref[1:2, at] = inv
+            return carry
+
+        lax.fori_loop(0, rows // own, measure, 0)
         if linked:
-            for act in first[1:]:
-                act()
+            for d in range(nz):
+                if d:
+                    one.along(d)
+                one.over(d)
+            two.begin()
+            for d in range(nz):
+                one.corner(d)
+            one.end()
             keep.start()
-            two.begin()
         else:
             fetch.wait()
         gain = w_ref[0, :, 3 * width :].astype(F32)
 
         def norm(i, carry):
             at = pl.ds(pl.multiple_of(i * own, own), own)
-            hat, _ = normalize(tok_ref[at, :].T.astype(F32))
-            n1_ref[:, at] = (hat * gain).astype(BF16)
+            made = (n1_ref[:, at].astype(F32) - stat_ref[0:1, at]) * stat_ref[1:2, at] * gain
+            n1_ref[:, at] = made.astype(BF16)
             return carry
 
         lax.fori_loop(0, rows // own, norm, 0)
         mine_ref[...] = n1_ref[:, mine]
 
     if linked:
-        acts = two.order()[1:]
-        heads = pl.num_programs(0)
-        for at, act in zip(spread(len(acts), 12), acts):
-            pl.when(step == at)(act)
+        for at, name, d in GATHER_STEPS:
+            pl.when(step == at)(functools.partial(getattr(two, name), d))
 
     @pl.when(lax.rem(step, per) == 0)
     def _():
@@ -636,7 +624,7 @@
     ka_ref[:HDIM] = k_ref[head]
     qa_ref[:HDIM] = q_ref[head]
     va_ref[:HDIM] = v_ref[head]
-    wide = 256
+    wide = own
     for i in range(own // wide):
         at = slice(i * wide, (i + 1) * wide)
         scores = dot(ka_ref[...], qa_ref[:, at], TN)
@@ -652,10 +640,22 @@
         @pl.when(step == pl.num_programs(0) - 1)
         def _():
             keep.wait()
-
-
-def spread(count, steps):
-    return [min(steps - 1, 1 + i * (steps - 1) // count) for i in range(count)]
+            two.corner(nz - 1)
+            two.end()
+
+
+GATHER_STEPS = (
+    (2, "along", 1),
+    (2, "over", 0),
+    (5, "over", 1),
+    (5, "along", 2),
+    (5, "corner", 0),
+    (7, "over", 2),
+    (8, "corner", 1),
+    (9, "along", 3),
+    (11, "over", 3),
+    (11, "corner", 2),
+)
 
 
 def forward(nz, n_mp, lengths, tokens, weights, columns):
@@ -704,6 +704,7 @@
             pltpu.VMEM((AUG, rows), BF16),
             pltpu.VMEM((AUG, own), BF16),
             pltpu.VMEM((AUG, rows), BF16),
+            pltpu.VMEM((8, rows), F32),
             dma,
         ]
         + (
@@ -840,7 +841,8 @@
     )(lengths, tokens, out_grad, heads_out, inv, w_rest)
 
 
-SLOTS = 4
+SLOTS = 7
+LAG = 4
 
 
 def backward_kernel(nz, *refs):
@@ -853,6 +855,7 @@
     high = Scatter(nz, (1,), gq_ref, gq_ref, dq_ref, *refs[12:18], shared=gq_ref.shape[2] - 1)
     fold = Fold(*refs[18:23])
     share = Share(in_own, in_full, *refs[23:26])
+    qc_ref = refs[26]
     step, heads = pl.program_id(0), pl.num_programs(0)
     parts = w_ref.shape[0]
     features, own = n1_ref.shape
@@ -872,7 +875,7 @@
         for copy in loads:
             copy.start()
         greet(peers(nz))
-        rest.begin()
+        rest.begin(2, 3)
         va_ref[HDIM:] = jnp.full((AUG - HDIM, rows), -1.0, BF16)
         acc_ref[...] = jnp.zeros_like(acc_ref)
         gc_ref[...] = jnp.zeros_like(gc_ref)
@@ -892,17 +895,12 @@
 
     def close(part):
         for i in range(per):
-            pc_ref[i * HDIM : (i + 1) * HDIM] = qc_ref[lax.rem(part, 2), i * HDIM : (i + 1) * HDIM]
+            pc_ref[i * HDIM : (i + 1) * HDIM] = qc_ref[lax.rem(part, 3), i * HDIM : (i + 1) * HDIM]
         made = dot(n1_ref[...], pc_ref[...], NT)
         gq_ref[part, :, : 3 * width] = made.astype(BF16)
         weights = w_ref[part, :, : 3 * width]
         gc_ref[...] += jnp.sum(made * weights.astype(F32), axis=1, keepdims=True)
         acc_ref[...] += dot(weights, pc_ref[...], NN)
-
-    qc_ref = refs[26]
-    acts = rest.order()[1:]
-    for at, act in zip(REST_STEPS, acts):
-        pl.when(step == at)(act)
 
     va_ref[:HDIM] = v_ref[...]
     cot = dot(va_ref[...], do_ref[0], TN)
@@ -916,11 +914,11 @@
         fold.part[slot, m, :HDIM] = dk[:, m * own : (m + 1) * own]
         fold.part[slot, m, HDIM:] = dv[:, m * own : (m + 1) * own]
     at = pl.ds(pl.multiple_of(lax.rem(step, per) * HDIM, HDIM), HDIM)
-    qc_ref[lax.rem(step // per, 2), at] = dq.astype(BF16)
-
-    @pl.when(step >= 2)
+    qc_ref[lax.rem(step // per, 3), at] = dq.astype(BF16)
+
+    @pl.when(step >= LAG)
     def _():
-        collect(step - 2)
+        collect(step - LAG)
 
     @pl.when(step >= 1)
     def _():
@@ -928,44 +926,80 @@
 
     fold.begin(step)
 
-    @pl.when((step >= per + 1) & (lax.rem(step - 2, per) == per - 1))
+    @pl.when((step >= LAG) & (lax.rem(step - LAG, per) == per - 1))
     def _():
-        close((step - 2) // per)
-
-    @pl.when(step == LOW_STEP)
-    def _():
-        low.begin()
-
-    for at, act in zip(LOW_STEPS, low.order()[1:]):
-        pl.when(step == at)(act)
+        close((step - LAG) // per)
+
+    sums = {"rest": rest, "low": low, "high": high}
+    for at, which, name, *d in SUM_STEPS:
+        pl.when(step == at)(functools.partial(getattr(sums[which], name), *d))
 
     @pl.when(step == heads - 1)
     def _():
-        collect(step - 1)
         fold.chip(step)
-        for act in acts[len(REST_STEPS) :]:
-            act()
-        collect(step)
-        close(parts - 1)
+        for back in range(LAG - 1, -1, -1):
+            collect(step - back)
+            if (heads - 1 - back) % per == per - 1:
+                close((step - back) // per)
         gain = w_ref[0, :, 3 * width :].astype(F32)
         gain_cot = (gc_ref[...] / gain).astype(BF16)
         for m in range(2, parts):
             gq_ref[m, :, 3 * width :] = gain_cot
-        high.begin()
+        high.begin(2, 3, 1, 0)
         in_own[...] = finish(tok_ref[...], gain, acc_ref[...], mcot_ref[...])
         share.begin(0)
-        acts_high = high.order()[1:]
-        for act in low.order()[1 + len(LOW_STEPS) :]:
-            act()
-        for act in acts_high:
-            act()
+        for which, name, *d in LAST_STEPS:
+            getattr(sums[which], name)(*d)
         share.on(0)
+        for which in sums.values():
+            which.along()
+        for which in sums.values():
+            which.end()
         share.end()
 
 
-REST_STEPS = (1, 1, 2, 2, 5, 7, 9)
-LOW_STEP = 8
-LOW_STEPS = (9, 9, 10, 10)
+SUM_STEPS = (
+    (1, "rest", "chip", 2),
+    (1, "rest", "cross", 2),
+    (1, "rest", "begin", 1, 0),
+    (1, "rest", "chip", 3),
+    (3, "rest", "chip", 1),
+    (3, "rest", "chip", 0),
+    (5, "rest", "over", 2),
+    (5, "rest", "cross", 3),
+    (9, "rest", "over", 3),
+    (9, "rest", "cross", 1),
+    (9, "low", "begin", 2, 3, 1, 0),
+    (11, "low", "chip", 2),
+    (11, "low", "chip", 3),
+    (11, "low", "chip", 1),
+    (11, "low", "chip", 0),
+)
+LAST_STEPS = (
+    ("rest", "over", 1),
+    ("rest", "cross", 0),
+    ("low", "cross", 2),
+    ("low", "cross", 3),
+    ("high", "chip", 2),
+    ("high", "chip", 3),
+    ("high", "chip", 1),
+    ("high", "chip", 0),
+    ("rest", "over", 0),
+    ("low", "cross", 1),
+    ("low", "cross", 0),
+    ("low", "over", 2),
+    ("low", "over", 3),
+    ("high", "cross", 2),
+    ("high", "cross", 3),
+    ("low", "over", 1),
+    ("low", "over", 0),
+    ("high", "cross", 1),
+    ("high", "cross", 0),
+    ("high", "over", 2),
+    ("high", "over", 3),
+    ("high", "over", 1),
+    ("high", "over", 0),
+)
 
 
 def backward(nz, q, k, v, do, p, cos, sin, n1, mcot, tokens, w_qkv, g_rest):
@@ -1019,7 +1053,7 @@
         + Scatter.scratch(nz, (1,), depth, columns[0])
         + Fold.scratch(n_mp, own, SLOTS)
         + Share.sems(1)
-        + [pltpu.VMEM((2, width, own), BF16)],
+        + [pltpu.VMEM((3, width, own), BF16)],
         compiler_params=pltpu.CompilerParams(
             dimension_semantics=("arbitrary",), collective_id=3, has_side_effects=True, vmem_limit_bytes=VMEM_BYTES
         ),
@@ -1066,7 +1100,7 @@
     depth = w_qkv.shape[0]
     units, width = w_down.shape[0], w_out.shape[0]
     everyone = ("mp", "dp")
-    linked = n_mp == 4 and n_dp % 2 == 0 and depth % 32 == 0 and features // HDIM == 12
+    linked = n_mp == 4 and n_dp == 8 and depth % 32 == 0 and features // HDIM == 12
     nz = n_dp // 2 if linked else 0
     columns = 3 * width + 1, 3 * units + width + 1
     wq, wg = w_qkv.transpose(1, 0, 2), w_gu.transpose(1, 0, 2)

time: 268 us -> 225 us (0.84)
  Pallas kernels: 262 us -> 219 us
    pallas_call x1, Pallas kernels: 120 us -> 97.8 us  [backward(): pl.pallas_call(functools.partial(backward_kernel, nz), grid=(heads,), in_...]
    pallas_call x1, Pallas kernels: 101 us -> 79.5 us  [forward(): pl.pallas_call(functools.partial(forward_kernel, nz), grid=(heads,), in_s...]
where the time goes in v4:
time: 225 us
  Pallas kernels  219 us (97%)
  local copies, waits for them, and re-layouts  5.16 us (2%)
    pallas_call x1, Pallas kernels, backward(): pl.pallas_call(functools.partial(backward_kernel, nz), grid=(heads,), in_...  97.8 us
    pallas_call x1, Pallas kernels, forward(): pl.pallas_call(functools.partial(forward_kernel, nz), grid=(heads,), in_s...  79.5 us
    pallas_call x1, Pallas kernels, mid(): pl.pallas_call(functools.partial(mid_kernel, linked, units), in_specs=[pl...  35.6 us
    pallas_call x1, Pallas kernels, deliver(): pl.pallas_call(functools.partial(deliver_kernel, units), grid=(steps,), i...  5.98 us
    unnamed x5, local copies, waits for them, and re-layouts  5.16 us

profile of v4, /device:TPU:0, one launch (start us, length us, event | category | flops | bytes accessed | tf_op | source)
XLA Modules:
  0.0 224.7 jit_solution(18298071026143852175)
XLA Ops:
  0.6 1.6 copy.20
  2.2 79.5 %forward.1 = (bf16[768,512]{1,0:T(8,128)(2,1)}, bf16[768,512]{1,0:T(8,128)(2,1)}, bf16[768,2048]{1,0:T(8,128)(2,1)}, bf16[768,2048]{1,0:T(8,128)(2,1)}, f32[32,2...) custom-call(s32[1,8]{1,0:T(1,128)} %len_ref.3, ...), custom_call_target="tpu_custom_call" | custom-call | tf_op jit(solution)/shard_map/forward/pallas_call | solution.py:673
  81.8 35.6 %mid.1 = (bf16[2048,768]{1,0:T(8,128)(2,1)}, f32[768,512]{1,0:T(8,128)}, bf16[12,80,512]{2,1,0:T(8,128)(2,1)}, bf16[4,768,1057]{2,1,0:T(8,128)(2,1)}) custom-call(s32[1,8]{1,0:T(1,128)} %len_ref.3, bf16[2048,768]{1,0:T(8,128)(2,1)} %refs_9_.1, bf16[2048,768]{1,0:T(8,128)(2,1)} %cot_hbm.1, bf16[768,512]{1,0:T(8,128)(2,1)} %get-tuple-element.33.heads_ref, ...), custom_call_target="tpu_custom_call" | custom-call | tf_op jit(solution)/shard_map/mid/pallas_call | solution.py:820
  117.4 97.8 %backward.1 = (f32[96,577]{1,0:T(8,128)}, f32[96,1057]{1,0:T(8,128)}, bf16[2048,768]{1,0:T(8,128)(2,1)}) custom-call(bf16[768,512]{1,0:T(8,128)(2,1)} %get-tuple-element.37.refs_0_, bf16[768,2048]{1,0:T(8,128)(2,1)} %get-tuple-element.38.refs_1_, bf16[768,2048]{1,0:T(8,128)(2,1)} %get-tuple-element.39.refs_2_, ...), custom_call_target="tpu_custom_call" | custom-call | tf_op jit(solution)/shard_map/backward/pallas_call | solution.py:1016
  215.1 0.0 copy-start
  215.1 6.0 %deliver.1 = (f32[2048,768]{1,0:T(8,128)}, f32[3,96,192]{2,1,0:T(8,128)}, f32[192,96]{1,0:T(8,128)}, f32[2,96,288]{2,1,0:T(8,128)}, f32[288,96]{1,0:T(8,128)}, /*index=5*/f32[1,96]{1,0:T(1,128)}, f32[1,96]{1,0:T(1,128)}) custom-call(bf16[2048,768]{1,0:T(8,128)(2,1)} %get-tuple-element.48.in_ref, f32[96,577]{1,0:T(8,128)} %get-tuple-element.49.dq_ref, ...), custom_call_target="tpu_custom_call" | custom-call | tf_op jit(solution)/shard_map/deliver/pallas_call | solution.py:1087
  221.1 1.9 copy.18
  223.0 0.0 copy-done
  223.0 1.7 copy.22
Async XLA Ops:
  215.1 7.9 %copy-start = (bf16[2048,768]{1,0:T(8,128)(2,1)S(1)}, bf16[2048,768]{1,0:T(8,128)(2,1)}, u32[]{:S(2)}) copy-start(bf16[2048,768]{1,0:T(8,128)(2,1)} %get-tuple-element.74) | copy-start | bytes 9437188

commit v5 on v4

--- a/solution.py
+++ b/solution.py
@@ -559,7 +559,7 @@
             units = wd_ref.shape[0]
             pair = 2 * units
             for i in range(2):
-                src_b[:, i * units : (i + 1) * units] = wg_ref[i]
+                src_b[:, i * units : (i + 1) * units] = wg_ref[:, i, :]
             src_b[:, pair : pair + width] = wo_ref[...].T
             src_b[:, pair + width : pair + width + units] = wd_ref[...].T
             src_b[:, pair + width + units :] = two_ref[...].astype(F32).T.astype(BF16)
@@ -721,11 +721,79 @@
     )(lengths, tokens, *weights)
 
 
+def middle(len_ref, me, tok_ref, cot_ref, heads_ref, inv_ref, w_ref, units, out_ref, mcot_ref, do_ref, keep, sent, done):
+    own, features = tok_ref.shape
+    parts = w_ref.shape[0]
+    width = features // parts
+    heads = width // HDIM
+    pair = 2 * units
+    _, _, live = layout_rows(len_ref, len_ref.shape[1], me * own, own)
+
+    def w_gu(m):
+        return w_ref[m, :, :pair]
+
+    def w_out(m):
+        return w_ref[m, :, pair : pair + width]
+
+    def w_down(m):
+        return w_ref[m, :, pair + width : pair + width + units]
+
+    total = dot(w_out(0), heads_ref[:width], NN)
+    for m in range(1, parts):
+        total += dot(w_out(m), heads_ref[m * width : (m + 1) * width], NN)
+    middle = tok_ref[...].T.astype(F32) + total
+    gain = w_ref[0, :, pair + width + units :].astype(F32)
+    hat, inv_sigma = normalize(middle)
+    normed = (hat * gain).astype(BF16)
+    total = middle
+    kept = []
+    for m in range(parts):
+        gate_up = dot(w_gu(m), normed, TN)
+        gate, up = gate_up[:units], gate_up[units:]
+        phi, slope = gelu_parts(gate)
+        act = gate * phi
+        hidden = (act * up).astype(BF16)
+        total += dot(w_down(m), hidden, NN)
+        kept.append((hidden, (up * (phi + slope)).astype(BF16), act.astype(BF16)))
+    out_ref[...] = total.astype(BF16).T
+    sent()
+    branch = jnp.where(live, cot_ref[...].T.astype(F32), 0.0).astype(BF16)
+    back = jnp.zeros((features, own), F32)
+    for m in range(parts):
+        hidden, one, two = kept[m]
+        hidden_cot = dot(w_down(m), branch, TN)
+        keep("down", m, dot(branch, hidden, NT).astype(BF16))
+        cots = jnp.concatenate([hidden_cot * one.astype(F32), hidden_cot * two.astype(F32)], axis=0).astype(BF16)
+        keep("gu", m, dot(normed, cots, NT).astype(BF16))
+        back += dot(w_gu(m), cots, NN)
+    done()
+    gain_cot = jnp.sum(back * hat, axis=1, keepdims=True).astype(BF16)
+    d = back * gain
+    middle_cot = branch.astype(F32) + inv_sigma * (
+        d - jnp.mean(d, axis=0, keepdims=True) - hat * jnp.mean(d * hat, axis=0, keepdims=True)
+    )
+    mcot_ref[...] = middle_cot
+    attn_cot = middle_cot.astype(BF16)
+    for m in range(parts):
+        back_heads = dot(w_out(m), attn_cot, TN)
+        for h in range(heads):
+            head = m * heads + h
+            rows = slice(h * HDIM, (h + 1) * HDIM)
+            cot = back_heads[rows] * inv_ref[head]
+            inner = jnp.sum(cot * heads_ref[head * HDIM : (head + 1) * HDIM].astype(F32), axis=0, keepdims=True)
+            high = inner.astype(BF16).astype(F32)
+            pad = jnp.zeros((AUG - HDIM - 2, own), F32)
+            do_ref[head] = jnp.concatenate([cot, high, inner - high, pad], axis=0).astype(BF16)
+    for m in range(parts):
+        keep("out", m, dot(attn_cot, heads_ref[m * width : (m + 1) * width], NT).astype(BF16))
+        keep("gain", m, gain_cot)
+
+
 def mid_kernel(
-    linked, units, len_ref, tok_hbm, cot_hbm, heads_ref, inv_ref, w_hbm,
-    out_ref, mcot_ref, do_ref, g_ref, tok_ref, cot_ref, w_ref, load, *share,
+    units, len_ref, tok_hbm, cot_hbm, heads_ref, inv_ref, w_hbm,
+    out_ref, mcot_ref, do_ref, g_ref, o_ref, tok_ref, cot_ref, w_ref, load,
 ):
-    own, features = tok_ref.shape
+    own = tok_ref.shape[0]
     me = lax.axis_index("mp")
     mine = pl.ds(pl.multiple_of(me * own, own), own)
     loads = [
@@ -735,108 +803,49 @@
     ]
     for copy in loads:
         copy.start()
-    if linked:
-        out_own = share[0]
-        share = Share(out_own, out_ref, *share[1:])
-        greet(peers(1))
-    else:
-        out_own = out_ref
-    parts = w_ref.shape[0]
-    width = features // parts
-    heads = width // HDIM
-    pair = 2 * units
-    _, _, live = layout_rows(len_ref, len_ref.shape[1], me * own, own)
     for copy in loads:
         copy.wait()
-
-    def w_gu(m):
-        return w_ref[m, :, :pair]
-
-    def w_out(m):
-        return w_ref[m, :, pair : pair + width]
-
-    def w_down(m):
-        return w_ref[m, :, pair + width : pair + width + units]
-
-    total = dot(w_out(0), heads_ref[:width], NN)
-    for m in range(1, parts):
-        total += dot(w_out(m), heads_ref[m * width : (m + 1) * width], NN)
-    middle = tok_ref[...].T.astype(F32) + total
-    gain = w_ref[0, :, pair + width + units :].astype(F32)
-    hat, inv_sigma = normalize(middle)
-    normed = (hat * gain).astype(BF16)
-    branch = jnp.where(live, cot_ref[...].T.astype(F32), 0.0).astype(BF16)
-    total = middle
-    back = jnp.zeros((features, own), F32)
-    kept = []
-    for m in range(parts):
-        gate_up = dot(w_gu(m), normed, TN)
-        gate, up = gate_up[:units], gate_up[units:]
-        phi, slope = gelu_parts(gate)
-        act = gate * phi
-        hidden = (act * up).astype(BF16)
-        total += dot(w_down(m), hidden, NN)
-        kept.append((hidden, up * (phi + slope), act))
-    out_own[...] = total.astype(BF16).T
-    if linked:
-        share.begin(0)
-    for m in range(parts):
-        hidden, one, two = kept[m]
-        hidden_cot = dot(w_down(m), branch, TN)
-        g_ref[m, :, pair + width : pair + width + units] = dot(branch, hidden, NT).astype(BF16)
-        cots = jnp.concatenate([hidden_cot * one, hidden_cot * two], axis=0).astype(BF16)
-        g_ref[m, :, :pair] = dot(normed, cots, NT).astype(BF16)
-        back += dot(w_gu(m), cots, NN)
-    gain_cot = jnp.sum(back * hat, axis=1, keepdims=True).astype(BF16)
-    d = back * gain
-    middle_cot = branch.astype(F32) + inv_sigma * (
-        d - jnp.mean(d, axis=0, keepdims=True) - hat * jnp.mean(d * hat, axis=0, keepdims=True)
+    pair, width = 2 * units, o_ref.shape[2] - 1
+
+    def keep(what, m, made):
+        if what == "gu":
+            g_ref[m, :, :pair] = made
+        elif what == "down":
+            g_ref[m, :, pair:] = made
+        elif what == "out":
+            o_ref[m, :, :width] = made
+        else:
+            o_ref[m, :, width:] = made
+
+    nothing = lambda: None
+    middle(
+        len_ref, me, tok_ref, cot_ref, heads_ref, inv_ref, w_ref, units, out_ref, mcot_ref, do_ref, keep, nothing, nothing
     )
-    mcot_ref[...] = middle_cot
-    attn_cot = middle_cot.astype(BF16)
-    for m in range(parts):
-        g_ref[m, :, pair + width + units :] = gain_cot
-        part = heads_ref[m * width : (m + 1) * width]
-        g_ref[m, :, pair : pair + width] = dot(attn_cot, part, NT).astype(BF16)
-        back_heads = dot(w_out(m), attn_cot, TN)
-        for h in range(heads):
-            head = m * heads + h
-            rows = slice(h * HDIM, (h + 1) * HDIM)
-            cot = back_heads[rows] * inv_ref[head]
-            inner = jnp.sum(cot * part[rows].astype(F32), axis=0, keepdims=True)
-            high = inner.astype(BF16).astype(F32)
-            pad = jnp.zeros((AUG - HDIM - 2, own), F32)
-            do_ref[head] = jnp.concatenate([cot, high, inner - high, pad], axis=0).astype(BF16)
-    if linked:
-        share.on(0)
-        share.end()
-
-
-def mid(linked, n_mp, lengths, tokens, out_grad, heads_out, inv, w_rest, units):
+
+
+def mid(n_mp, lengths, tokens, out_grad, heads_out, inv, w_rest, units):
     features, own = heads_out.shape
     heads = inv.shape[0]
     vm = pl.BlockSpec(memory_space=pltpu.VMEM)
     hbm = pl.BlockSpec(memory_space=pl.ANY)
     return pl.pallas_call(
-        functools.partial(mid_kernel, linked, units),
+        functools.partial(mid_kernel, units),
         in_specs=[pl.BlockSpec(memory_space=pltpu.SMEM), hbm, hbm, vm, vm, hbm],
-        out_specs=[hbm if linked else vm] + [vm] * 3,
+        out_specs=[vm] * 5,
         out_shape=[
-            jax.ShapeDtypeStruct((own * n_mp if linked else own, features), BF16),
+            jax.ShapeDtypeStruct((own, features), BF16),
             jax.ShapeDtypeStruct((features, own), F32),
             jax.ShapeDtypeStruct((heads, AUG, own), BF16),
-            jax.ShapeDtypeStruct(w_rest.shape, BF16),
+            jax.ShapeDtypeStruct((n_mp, features, 3 * units), BF16),
+            jax.ShapeDtypeStruct((n_mp, features, features // n_mp + 1), BF16),
         ],
         scratch_shapes=[
             pltpu.VMEM((own, features), BF16),
             pltpu.VMEM((own, features), BF16),
             pltpu.VMEM(w_rest.shape, BF16),
             pltpu.SemaphoreType.DMA((3,)),
-        ]
-        + ([pltpu.VMEM((own, features), BF16)] + Share.sems(1) if linked else []),
-        compiler_params=pltpu.CompilerParams(
-            vmem_limit_bytes=VMEM_BYTES, **({"collective_id": 2, "has_side_effects": True} if linked else {})
-        ),
+        ],
+        compiler_params=pltpu.CompilerParams(vmem_limit_bytes=VMEM_BYTES),
         name="mid",
     )(lengths, tokens, out_grad, heads_out, inv, w_rest)
 
@@ -845,18 +854,19 @@
 LAG = 4
 
 
-def backward_kernel(nz, *refs):
-    q_ref, k_ref, v_ref, do_ref, p_ref, cos_ref, sin_ref, n1_ref, mcot_ref, tok_hbm, w_hbm, gr_hbm = refs[:12]
-    dq_ref, dr_ref, in_full = refs[12:15]
-    w_ref, gr_ref, gq_ref, pc_ref, acc_ref, gc_ref, va_ref, tok_ref, in_own, load = refs[15:25]
-    refs = refs[25:]
-    rest = Scatter(nz, (0, 1), gr_hbm, gr_ref, dr_ref, *refs[:6])
+def backward_kernel(nz, units, *refs):
+    len_ref, q_ref, k_ref, v_ref, p_ref, cos_ref, sin_ref, n1_ref, heads_ref, inv_ref, tok_hbm, cot_hbm, w_hbm, wr_hbm = refs[:14]
+    dq_ref, dr_ref, in_full, out_full = refs[14:18]
+    w_ref, wr_ref, gr_ref, do_ref, mcot_ref, pc_ref, qc_ref, acc_ref, gc_ref, va_ref, tok_ref, cot_ref, own_ref, load = refs[18:32]
+    refs = refs[32:]
+    gq_ref = wr_ref.at[:, :, pl.ds(0, dq_ref.shape[1])]
+    rest = Scatter(nz, (0, 1), gr_ref, gr_ref, dr_ref, *refs[:6])
     low = Scatter(nz, (0,), gq_ref, gq_ref, dq_ref, *refs[6:12])
-    high = Scatter(nz, (1,), gq_ref, gq_ref, dq_ref, *refs[12:18], shared=gq_ref.shape[2] - 1)
+    high = Scatter(nz, (1,), gq_ref, gq_ref, dq_ref, *refs[12:18], shared=4 * (w_ref.shape[2] // 3))
     fold = Fold(*refs[18:23])
-    share = Share(in_own, in_full, *refs[23:26])
-    qc_ref = refs[26]
-    step, heads = pl.program_id(0), pl.num_programs(0)
+    in_share = Share(own_ref.at[0], in_full, *refs[23:26])
+    out_share = Share(own_ref.at[1], out_full, *refs[26:29])
+    step, heads = pl.program_id(0) - 1, pl.num_programs(0) - 1
     parts = w_ref.shape[0]
     features, own = n1_ref.shape
     rows = k_ref.shape[1]
@@ -864,28 +874,41 @@
     per = width // HDIM
     me = lax.axis_index("mp")
     mine = pl.ds(pl.multiple_of(me * own, own), own)
-    loads = [
-        pltpu.make_async_copy(w_hbm, w_ref, load.at[0]),
-        pltpu.make_async_copy(gr_hbm, gr_ref, load.at[1]),
-        pltpu.make_async_copy(tok_hbm.at[mine], tok_ref, load.at[2]),
-    ]
-
-    @pl.when(step == 0)
+    late = pltpu.make_async_copy(w_hbm, w_ref, load.at[3])
+
+    @pl.when(step < 0)
     def _():
+        loads = [
+            pltpu.make_async_copy(wr_hbm, wr_ref, load.at[0]),
+            pltpu.make_async_copy(tok_hbm.at[mine], tok_ref, load.at[1]),
+            pltpu.make_async_copy(cot_hbm.at[mine], cot_ref, load.at[2]),
+        ]
         for copy in loads:
             copy.start()
         greet(peers(nz))
-        rest.begin(2, 3)
+        for copy in loads:
+            copy.wait()
+        late.start()
+        pair = 2 * units
+
+        def keep(what, m, made):
+            if what == "gu":
+                gr_ref[m, :, :pair] = made
+            elif what == "down":
+                gr_ref[m, :, pair:] = made
+            elif what == "out":
+                wr_ref[m, :, 3 * width : 4 * width] = made
+            else:
+                wr_ref[m, :, 4 * width + 1 : 4 * width + 2] = made
+
+        middle(
+            len_ref, me, tok_ref, cot_ref, heads_ref, inv_ref, wr_ref, units, own_ref.at[1], mcot_ref, do_ref, keep,
+            lambda: out_share.begin(0), lambda: rest.begin(2, 3),
+        )
         va_ref[HDIM:] = jnp.full((AUG - HDIM, rows), -1.0, BF16)
         acc_ref[...] = jnp.zeros_like(acc_ref)
         gc_ref[...] = jnp.zeros_like(gc_ref)
-        for m in range(2):
-            gq_ref[m, :, 3 * width :] = jnp.zeros((features, 1), BF16)
-
-    @pl.when(step == 1)
-    def _():
-        for copy in loads:
-            copy.wait()
+        late.wait()
 
     def collect(head):
         made = fold.end(head)
@@ -897,40 +920,42 @@
         for i in range(per):
             pc_ref[i * HDIM : (i + 1) * HDIM] = qc_ref[lax.rem(part, 3), i * HDIM : (i + 1) * HDIM]
         made = dot(n1_ref[...], pc_ref[...], NT)
-        gq_ref[part, :, : 3 * width] = made.astype(BF16)
+        wr_ref[part, :, : 3 * width] = made.astype(BF16)
         weights = w_ref[part, :, : 3 * width]
         gc_ref[...] += jnp.sum(made * weights.astype(F32), axis=1, keepdims=True)
         acc_ref[...] += dot(weights, pc_ref[...], NN)
 
-    va_ref[:HDIM] = v_ref[...]
-    cot = dot(va_ref[...], do_ref[0], TN)
-    probs = p_ref[0]
-    score_cot = probs * cot.astype(BF16)
-    dv = dot(do_ref[0, :HDIM], probs, NT).astype(BF16)
-    dk = turn(dot(q_ref[...], score_cot, NT) * LN2, cos_ref[...], sin_ref[...], 1, True).astype(BF16)
-    dq = turn(dot(k_ref[...], score_cot, NN) * SCALE, cos_ref[:, mine], sin_ref[:, mine], 1, True)
-    slot = lax.rem(step, SLOTS)
-    for m in range(parts):
-        fold.part[slot, m, :HDIM] = dk[:, m * own : (m + 1) * own]
-        fold.part[slot, m, HDIM:] = dv[:, m * own : (m + 1) * own]
-    at = pl.ds(pl.multiple_of(lax.rem(step, per) * HDIM, HDIM), HDIM)
-    qc_ref[lax.rem(step // per, 3), at] = dq.astype(BF16)
-
-    @pl.when(step >= LAG)
+    @pl.when(step >= 0)
     def _():
-        collect(step - LAG)
-
-    @pl.when(step >= 1)
-    def _():
-        fold.chip(step - 1)
-
-    fold.begin(step)
-
-    @pl.when((step >= LAG) & (lax.rem(step - LAG, per) == per - 1))
-    def _():
-        close((step - LAG) // per)
-
-    sums = {"rest": rest, "low": low, "high": high}
+        va_ref[:HDIM] = v_ref[...]
+        cot = dot(va_ref[...], do_ref[step], TN)
+        probs = p_ref[0]
+        score_cot = probs * cot.astype(BF16)
+        dv = dot(do_ref[step, :HDIM], probs, NT).astype(BF16)
+        dk = turn(dot(q_ref[...], score_cot, NT) * LN2, cos_ref[...], sin_ref[...], 1, True).astype(BF16)
+        dq = turn(dot(k_ref[...], score_cot, NN) * SCALE, cos_ref[:, mine], sin_ref[:, mine], 1, True)
+        slot = lax.rem(step, SLOTS)
+        for m in range(parts):
+            fold.part[slot, m, :HDIM] = dk[:, m * own : (m + 1) * own]
+            fold.part[slot, m, HDIM:] = dv[:, m * own : (m + 1) * own]
+        at = pl.ds(pl.multiple_of(lax.rem(step, per) * HDIM, HDIM), HDIM)
+        qc_ref[lax.rem(step // per, 3), at] = dq.astype(BF16)
+
+        @pl.when(step >= LAG)
+        def _():
+            collect(step - LAG)
+
+        @pl.when(step >= 1)
+        def _():
+            fold.chip(step - 1)
+
+        fold.begin(step)
+
+        @pl.when((step >= LAG) & (lax.rem(step - LAG, per) == per - 1))
+        def _():
+            close((step - LAG) // per)
+
+    sums = {"rest": rest, "low": low, "high": high, "out": out_share}
     for at, which, name, *d in SUM_STEPS:
         pl.when(step == at)(functools.partial(getattr(sums[which], name), *d))
 
@@ -944,155 +969,164 @@
         gain = w_ref[0, :, 3 * width :].astype(F32)
         gain_cot = (gc_ref[...] / gain).astype(BF16)
         for m in range(2, parts):
-            gq_ref[m, :, 3 * width :] = gain_cot
+            wr_ref[m, :, 4 * width : 4 * width + 1] = gain_cot
         high.begin(2, 3, 1, 0)
-        in_own[...] = finish(tok_ref[...], gain, acc_ref[...], mcot_ref[...])
-        share.begin(0)
+        own_ref[0] = finish(tok_ref[...], gain, acc_ref[...], mcot_ref[...])
+        in_share.begin(0)
         for which, name, *d in LAST_STEPS:
             getattr(sums[which], name)(*d)
-        share.on(0)
-        for which in sums.values():
+        in_share.on(0)
+        for which in (rest, low, high):
             which.along()
-        for which in sums.values():
+        for which in (rest, low, high):
             which.end()
-        share.end()
+        out_share.end()
+        in_share.end()
 
 
 SUM_STEPS = (
-    (1, "rest", "chip", 2),
-    (1, "rest", "cross", 2),
-    (1, "rest", "begin", 1, 0),
-    (1, "rest", "chip", 3),
-    (3, "rest", "chip", 1),
-    (3, "rest", "chip", 0),
-    (5, "rest", "over", 2),
-    (5, "rest", "cross", 3),
-    (9, "rest", "over", 3),
-    (9, "rest", "cross", 1),
+    (-1, "rest", "chip", 2),
+    (-1, "rest", "cross", 2),
+    (-1, "rest", "begin", 1, 0),
+    (-1, "rest", "chip", 3),
+    (1, "rest", "chip", 1),
+    (1, "rest", "chip", 0),
+    (1, "out", "on", 0),
+    (2, "rest", "over", 2),
+    (2, "rest", "cross", 3),
+    (5, "rest", "over", 3),
+    (5, "rest", "cross", 1),
+    (8, "rest", "over", 1),
+    (8, "rest", "cross", 0),
     (9, "low", "begin", 2, 3, 1, 0),
-    (11, "low", "chip", 2),
-    (11, "low", "chip", 3),
-    (11, "low", "chip", 1),
-    (11, "low", "chip", 0),
+    (10, "low", "chip", 2),
+    (10, "low", "chip", 3),
+    (10, "low", "chip", 1),
+    (10, "low", "chip", 0),
+    (11, "rest", "over", 0),
+    (11, "low", "cross", 2),
+    (11, "low", "cross", 3),
 )
 LAST_STEPS = (
-    ("rest", "over", 1),
-    ("rest", "cross", 0),
-    ("low", "cross", 2),
-    ("low", "cross", 3),
     ("high", "chip", 2),
     ("high", "chip", 3),
     ("high", "chip", 1),
     ("high", "chip", 0),
-    ("rest", "over", 0),
+    ("low", "over", 2),
     ("low", "cross", 1),
+    ("low", "over", 3),
     ("low", "cross", 0),
-    ("low", "over", 2),
-    ("low", "over", 3),
+    ("low", "over", 1),
     ("high", "cross", 2),
     ("high", "cross", 3),
-    ("low", "over", 1),
     ("low", "over", 0),
+    ("high", "over", 2),
     ("high", "cross", 1),
     ("high", "cross", 0),
-    ("high", "over", 2),
     ("high", "over", 3),
     ("high", "over", 1),
     ("high", "over", 0),
 )
 
 
-def backward(nz, q, k, v, do, p, cos, sin, n1, mcot, tokens, w_qkv, g_rest):
+def backward(nz, lengths, q, k, v, p, cos, sin, n1, heads_out, inv, tokens, out_grad, w_qkv, w_rest, units):
     (features, own), rows = q.shape, k.shape[1]
     n_mp = w_qkv.shape[0]
     heads = features // HDIM
     width = features // n_mp
     depth = features // (2 * nz)
-    columns = w_qkv.shape[2], g_rest.shape[2]
+    columns = lanes(4 * width + 2), 3 * units
     hbm = pl.BlockSpec(memory_space=pl.ANY)
     vm = pl.BlockSpec(memory_space=pltpu.VMEM)
-    row = lambda h: (h, 0)
-    cube = lambda h: (h, 0, 0)
+    row = lambda h: (jnp.maximum(h - 1, 0), 0)
+    cube = lambda h: (jnp.maximum(h - 1, 0), 0, 0)
+    dma = pltpu.SemaphoreType.DMA
     return pl.pallas_call(
-        functools.partial(backward_kernel, nz),
-        grid=(heads,),
+        functools.partial(backward_kernel, nz, units),
+        grid=(heads + 1,),
         in_specs=[
+            pl.BlockSpec(memory_space=pltpu.SMEM),
             pl.BlockSpec((HDIM, own), row),
             pl.BlockSpec((HDIM, rows), row),
             pl.BlockSpec((HDIM, rows), row),
-            pl.BlockSpec((1, AUG, own), cube),
             pl.BlockSpec((1, rows, own), cube),
-            vm,
-            vm,
-            vm,
-            vm,
-            hbm,
-            hbm,
-            hbm,
-        ],
-        out_specs=[vm, vm, hbm],
+        ]
+        + [vm] * 5
+        + [hbm] * 4,
+        out_specs=[vm, vm, hbm, hbm],
         out_shape=[
             jax.ShapeDtypeStruct((depth, columns[0]), F32),
             jax.ShapeDtypeStruct((depth, columns[1]), F32),
             jax.ShapeDtypeStruct((rows, features), BF16),
+            jax.ShapeDtypeStruct((rows, features), BF16),
         ],
         scratch_shapes=[
             pltpu.VMEM(w_qkv.shape, BF16),
-            pltpu.VMEM(g_rest.shape, BF16),
-            pltpu.VMEM(w_qkv.shape, BF16),
+            pltpu.VMEM(w_rest.shape, BF16),
+            pltpu.VMEM((n_mp, features, 3 * units), BF16),
+            pltpu.VMEM((heads, AUG, own), BF16),
+            pltpu.VMEM((features, own), F32),
             pltpu.VMEM((3 * width, own), BF16),
+            pltpu.VMEM((3, width, own), BF16),
             pltpu.VMEM((features, own), F32),
             pltpu.VMEM((features, 1), F32),
             pltpu.VMEM((AUG, rows), BF16),
             pltpu.VMEM((own, features), BF16),
             pltpu.VMEM((own, features), BF16),
-            pltpu.SemaphoreType.DMA((3,)),
+            pltpu.VMEM((2, own, features), BF16),
+            dma((4,)),
         ]
         + Scatter.scratch(nz, (0, 1), depth, columns[1])
         + Scatter.scratch(nz, (0,), depth, columns[0])
         + Scatter.scratch(nz, (1,), depth, columns[0])
         + Fold.scratch(n_mp, own, SLOTS)
         + Share.sems(1)
-        + [pltpu.VMEM((3, width, own), BF16)],
+        + Share.sems(1),
         compiler_params=pltpu.CompilerParams(
             dimension_semantics=("arbitrary",), collective_id=3, has_side_effects=True, vmem_limit_bytes=VMEM_BYTES
         ),
         name="backward",
-    )(q, k, v, do, p, cos, sin, n1, mcot, tokens, w_qkv, g_rest)
-
-
-def deliver_kernel(units, in_ref, dq_ref, dr_ref, grad_ref, gq_ref, go_ref, gg_ref, gd_ref, one_ref, two_ref):
-    grad_ref[...] = in_ref[...].astype(F32)
-
+    )(lengths, q, k, v, p, cos, sin, n1, heads_out, inv, tokens, out_grad, w_qkv, w_rest)
+
+
+def lanes(columns):
+    return (columns + 127) // 128 * 128
+
+
+def deliver_kernel(units, in_ref, out_ref, dq_ref, dr_ref, grad_ref, to_ref, gq_ref, go_ref, gg_ref, gd_ref, one_ref, two_ref):
     @pl.when(pl.program_id(0) == 0)
     def _():
         width = go_ref.shape[0]
         pair = 2 * units
         for i in range(3):
             gq_ref[i] = dq_ref[:, i * width : (i + 1) * width]
-        one_ref[...] = dq_ref[:, 3 * width :].T
+        go_ref[...] = dq_ref[:, 3 * width : 4 * width].T
+        one_ref[...] = dq_ref[:, 4 * width : 4 * width + 1].T
+        two_ref[...] = dq_ref[:, 4 * width + 1 : 4 * width + 2].T
         for i in range(2):
-            gg_ref[i] = dr_ref[:, i * units : (i + 1) * units]
-        go_ref[...] = dr_ref[:, pair : pair + width].T
-        gd_ref[...] = dr_ref[:, pair + width : pair + width + units].T
-        two_ref[...] = dr_ref[:, pair + width + units :].T
-
-
-def deliver(input_grad, d_qkv, d_rest, width, units):
+            gg_ref[:, i, :] = dr_ref[:, i * units : (i + 1) * units]
+        gd_ref[...] = dr_ref[:, pair : pair + units].T
+
+    grad_ref[...] = in_ref[...].astype(F32)
+    to_ref[...] = out_ref[...]
+
+
+def deliver(layer_out, input_grad, d_qkv, d_rest, width, units):
     rows, features = input_grad.shape
     depth = d_qkv.shape[0]
     shape = lambda *s: jax.ShapeDtypeStruct(s, F32)
-    shapes = [(3, depth, width), (width, depth), (2, depth, units), (units, depth), (1, depth), (1, depth)]
+    shapes = [(3, depth, width), (width, depth), (depth, 2, units), (units, depth), (1, depth), (1, depth)]
     steps = 4
+    slab = pl.BlockSpec((rows // steps, features), lambda i: (i, 0))
     return pl.pallas_call(
         functools.partial(deliver_kernel, units),
         grid=(steps,),
-        in_specs=[pl.BlockSpec((rows // steps, features), lambda i: (i, 0)), whole(*d_qkv.shape), whole(*d_rest.shape)],
-        out_specs=[pl.BlockSpec((rows // steps, features), lambda i: (i, 0))] + [whole(*s) for s in shapes],
-        out_shape=[shape(rows, features)] + [shape(*s) for s in shapes],
+        in_specs=[slab, slab, whole(*d_qkv.shape), whole(*d_rest.shape)],
+        out_specs=[slab, slab] + [whole(*s) for s in shapes],
+        out_shape=[shape(rows, features), jax.ShapeDtypeStruct((rows, features), BF16)] + [shape(*s) for s in shapes],
         compiler_params=params("arbitrary"),
         name="deliver",
-    )(input_grad, d_qkv, d_rest)
+    )(input_grad, layer_out, d_qkv, d_rest)
 
 
 def per_device(n_dp, n_mp, tokens, out_grad, w_qkv, w_out, w_gu, w_down, gain_attn, gain_mlp, lengths):
@@ -1103,25 +1137,27 @@
     linked = n_mp == 4 and n_dp == 8 and depth % 32 == 0 and features // HDIM == 12
     nz = n_dp // 2 if linked else 0
     columns = 3 * width + 1, 3 * units + width + 1
-    wq, wg = w_qkv.transpose(1, 0, 2), w_gu.transpose(1, 0, 2)
+    wq = w_qkv.transpose(1, 0, 2)
     if linked:
-        weights = wq, wg, w_out, w_down, gain_attn[None], gain_mlp[None]
+        weights = wq, w_gu, w_out, w_down, gain_attn[None], gain_mlp[None]
         n1, q, k, v, cos, sin, heads_out, probs, inv, full_qkv, full_rest = forward(
             nz, n_mp, lengths, tokens, weights, columns
+        )
+        d_qkv, d_rest, in_full, layer_out = backward(
+            nz, lengths, q, k, v, probs, cos, sin, n1, heads_out, inv, tokens, out_grad, full_qkv, full_rest, units
         )
     else:
         shards = [
             jnp.concatenate([*wq, gain_attn[:, None]], axis=1),
-            jnp.concatenate([*wg, w_out.T, w_down.T, gain_mlp[:, None]], axis=1),
+            jnp.concatenate([w_gu.reshape(depth, -1), w_out.T, w_down.T, gain_mlp[:, None]], axis=1),
         ]
         full_qkv, full_rest = (
             lax.all_gather(s, everyone, axis=0, tiled=True).reshape(n_mp, features, s.shape[1]) for s in shards
         )
         n1, q, k, v, cos, sin, heads_out, probs, inv = forward(nz, n_mp, lengths, tokens, [full_qkv], columns)
-    layer_out, middle_cot, do, g_rest = mid(linked, n_mp, lengths, tokens, out_grad, heads_out, inv, full_rest, units)
-    if linked:
-        d_qkv, d_rest, in_full = backward(nz, q, k, v, do, probs, cos, sin, n1, middle_cot, tokens, full_qkv, g_rest)
-    else:
+        layer_out, middle_cot, do, g_rest, g_out = mid(
+            n_mp, lengths, tokens, out_grad, heads_out, inv, full_rest, units
+        )
         own = middle_cot.shape[1]
         g_qkv, nc = last(q, k, v, do, probs, cos, sin, lax.all_gather(n1, "mp", axis=1, tiled=True), full_qkv)
         gain_one = full_qkv[0, :, 3 * width :].astype(F32)
@@ -1129,16 +1165,19 @@
         nc_own = lax.psum_scatter(nc, "mp", scatter_dimension=0, tiled=True)[0]
         in_own = finish(tok, gain_one, nc_own.astype(F32), middle_cot)
         layer_out, in_full = (lax.all_gather(v, "mp", axis=0, tiled=True) for v in (layer_out, in_own))
+        g_qkv = jnp.concatenate(
+            [g_qkv[..., : 3 * width], g_out[..., :width], g_qkv[..., 3 * width :], g_out[..., width:]], axis=2
+        )
         d_qkv, d_rest = (
             lax.psum_scatter(
                 g.reshape(n_mp * features, -1), everyone, scatter_dimension=0, tiled=True
             ).astype(F32)
             for g in (g_qkv, g_rest)
         )
-    input_grad, g_q, g_o, g_g, g_d, one, two = deliver(in_full, d_qkv, d_rest, width, units)
+    input_grad, layer_out, g_q, g_o, g_g, g_d, one, two = deliver(layer_out, in_full, d_qkv, d_rest, width, units)
     if not linked:
         one, two = (lax.all_gather(g, "mp")[0] for g in (one, two))
-    return layer_out, input_grad, g_q.transpose(1, 0, 2), g_o, g_g.transpose(1, 0, 2), g_d, one[0], two[0]
+    return layer_out, input_grad, g_q.transpose(1, 0, 2), g_o, g_g, g_d, one[0], two[0]
 
 
 def solution(mesh):

time: 225 us -> 202 us (0.90)
  Pallas kernels: 219 us -> 201 us
  local copies, waits for them, and re-layouts: 5.16 us -> 0 us
    pallas_call x2 -> x1, Pallas kernels: 133 us -> 114 us  [backward(): pl.pallas_call(functools.partial(backward_kernel, nz, units), grid=(heads...]
    unnamed x5 -> x0, local copies, waits for them, and re-layouts: 5.16 us -> none
where the time goes in v5:
time: 202 us
  Pallas kernels  201 us (100%)
    pallas_call x1, Pallas kernels, backward(): pl.pallas_call(functools.partial(backward_kernel, nz, units), grid=(heads...  114 us
    pallas_call x1, Pallas kernels, forward(): pl.pallas_call(functools.partial(forward_kernel, nz), grid=(heads,), in_s...  79.6 us
    pallas_call x1, Pallas kernels, deliver(): pl.pallas_call(functools.partial(deliver_kernel, units), grid=(steps,), i...  7.59 us

profile of v5, /device:TPU:0, one launch (start us, length us, event | category | flops | bytes accessed | tf_op | source)
XLA Modules:
  0.0 201.7 jit_solution(1138653231683106001)
XLA Ops:
  0.6 79.6 %forward.1 = (bf16[768,512]{1,0:T(8,128)(2,1)}, bf16[768,512]{1,0:T(8,128)(2,1)}, bf16[768,2048]{1,0:T(8,128)(2,1)}, bf16[768,2048]{1,0:T(8,128)(2,1)}, f32[32,2...) custom-call(s32[1,8]{1,0:T(1,128)} %refs_0_.1, ...), custom_call_target="tpu_custom_call" | custom-call | tf_op jit(solution)/shard_map/forward/pallas_call | solution.py:673
  80.2 113.7 %backward.1 = (f32[96,896]{1,0:T(8,128)}, f32[96,864]{1,0:T(8,128)}, bf16[2048,768]{1,0:T(8,128)(2,1)}, bf16[2048,768]{1,0:T(8,128)(2,1)}) custom-call(s32[1,8]{1,0:T(1,128)} %refs_0_.1, bf16[768,512]{1,0:T(8,128)(2,1)} %get-tuple-element.31.refs_1_, bf16[768,2048]{1,0:T(8,128)(2,1)} %get-tuple-element.32.refs_2_, ...), custom_call_target="tpu_custom_call" | custom-call | tf_op jit(solution)/shard_map/backward/pallas_call | solution.py:1044
  194.0 7.6 %deliver.1 = (f32[2048,768]{1,0:T(8,128)}, bf16[2048,768]{1,0:T(8,128)(2,1)}, f32[3,96,192]{2,1,0:T(8,128)}, f32[192,96]{1,0:T(8,128)}, f32[96,2,288]{2,1,0:T(2,...) custom-call(bf16[2048,768]{1,0:T(8,128)(2,1)} %get-tuple-element.42.in_ref, ...), custom_call_target="tpu_custom_call" | custom-call | tf_op jit(solution)/shard_map/deliver/pallas_call | solution.py:1121

commit v6 on v5

--- a/solution.py
+++ b/solution.py
@@ -203,8 +203,9 @@
 
 
 class Gather:
-    def __init__(self, nz, src, full, send, recv, local):
+    def __init__(self, nz, src, full, send, recv, local, eager=False):
         self.nz, self.src, self.full, self.send, self.recv, self.local = nz, src, full, send, recv, local
+        self.eager = eager
         self.depth = src.shape[0]
         self.index = {}
         for kind in ("Z", "X", "Y", "S", "YA", "XB", "SX", "SY", "SA", "SB"):
@@ -251,14 +252,28 @@
         return pltpu.make_async_copy(self.src, self.block(z, x, y, c), self.local)
 
     def begin(self):
-        self.start("Z", 1)
+        for d in range(1, self.nz if self.eager else 2):
+            self.start("Z", d)
         for kind in ("X", "Y", "S"):
             self.start(kind, 0)
         self.own().start()
 
+    def all_along(self):
+        for d in range(1, self.nz):
+            self.along(d)
+
+    def all_over(self):
+        for d in range(self.nz):
+            self.over(d)
+
+    def rest(self):
+        for d in range(self.nz):
+            self.corner(d)
+        self.end()
+
     def along(self, d):
         self.arrived("Z", d)
-        if d + 1 < self.nz:
+        if d + 1 < self.nz and not self.eager:
             self.start("Z", d + 1)
         for kind in ("X", "Y", "S"):
             self.start(kind, d)
@@ -343,8 +358,8 @@
 
 
 class Scatter:
-    def __init__(self, nz, ups, src, part, out, core, side, line, last, send, recv, shared=None):
-        self.nz, self.ups, self.src, self.part, self.out, self.shared = nz, ups, src, part, out, shared
+    def __init__(self, nz, ups, src, part, out, core, side, line, last, send, recv):
+        self.nz, self.ups, self.src, self.part, self.out = nz, ups, src, part, out
         self.core, self.side, self.line, self.last, self.send, self.recv = core, side, line, last, send, recv
         self.depth = out.shape[0]
 
@@ -427,7 +442,7 @@
             for d in range(1, self.nz):
                 made += self.line[d, u].astype(F32)
             self.line[0, u] = made.astype(BF16)
-        if len(self.ups) == 2 or self.shared:
+        if len(self.ups) == 2:
             self.message("Y", 0).start()
         else:
             pl.when(y != self.ups[0])(lambda: self.message("Y", 0).start())
@@ -442,17 +457,6 @@
 
         if len(self.ups) == 2:
             receive()
-            self.message("Y", 0).wait_send()
-        elif self.shared:
-            pl.when(y == self.ups[0])(receive)
-
-            @pl.when(y != self.ups[0])
-            def _():
-                self.message("Y", 0).wait_recv()
-                self.out[:, self.shared :] = self.line[0, 0, :, self.shared :].astype(F32) + self.last[
-                    :, self.shared :
-                ].astype(F32)
-
             self.message("Y", 0).wait_send()
         else:
             pl.when(y == self.ups[0])(receive)
@@ -465,6 +469,42 @@
                 self.message("Z", d).wait_send()
 
 
+class Everyone:
+    def __init__(self, held, got, send, recv):
+        self.held, self.got, self.send, self.recv = held, got, send, recv
+        self.hops = got.shape[0]
+
+    @staticmethod
+    def scratch(nz, rows):
+        hops = 3 + nz.bit_length() - 1
+        dma = pltpu.SemaphoreType.DMA
+        return [pltpu.VMEM((hops + 1, rows, 128), F32), pltpu.VMEM((hops, rows, 128), F32), dma((hops,)), dma((hops,))]
+
+    def message(self, i):
+        z, x, y, c = place()
+        target = (
+            device(z, x, y, 1 - c) if i == 0
+            else device(z, x, 1 - y, c) if i == 1
+            else device(z, 1 - x, y, c) if i == 2
+            else device(lax.bitwise_xor(z, 1 << (i - 3)), x, y, c)
+        )
+        return remote(self.held.at[i], self.got.at[i], self.send.at[i], self.recv.at[i], target)
+
+    def begin(self):
+        self.message(0).start()
+
+    def hop(self, i):
+        self.message(i).wait_recv()
+        self.held[i + 1] = self.held[i] + self.got[i]
+        if i + 1 < self.hops:
+            self.message(i + 1).start()
+
+    def end(self):
+        for i in range(self.hops):
+            self.message(i).wait_send()
+        return self.held[self.hops]
+
+
 class Fold:
     def __init__(self, part, near, far, send, recv):
         self.part, self.near, self.far, self.send, self.recv = part, near, far, send, recv
@@ -514,59 +554,59 @@
         return made.astype(BF16)
 
 
-def project(w_ref, part, n1_ref, cos_ref, sin_ref, mine, q_ref, k_ref, v_ref):
-    width, own = q_ref.shape
-    heads = width // HDIM
-
-    made = dot(w_ref[part, :, width : 3 * width], n1_ref[...], TN)
-    k_ref[...] = turn(made[:width], cos_ref[...], sin_ref[...], heads).astype(BF16)
-    v_ref[...] = made[width:].astype(BF16)
-    made = dot(w_ref[part, :, :width], n1_ref[:, mine], TN) * (SCALE * LOG2E)
-    q_ref[...] = turn(made, cos_ref[:, mine], sin_ref[:, mine], heads).astype(BF16)
-
-
-def forward_kernel(nz, len_ref, tok_ref, *refs):
+def forward_kernel(nz, units, len_ref, tok_ref, *refs):
     linked = nz > 0
-    given, refs = refs[: 6 if linked else 1], refs[6 if linked else 1 :]
+    given, refs = refs[: 6 if linked else 2], refs[6 if linked else 2 :]
     mine_ref, q_ref, k_ref, v_ref, cos_ref, sin_ref, o_ref, p_ref, inv_ref = refs[:9]
-    full_refs, refs = refs[9 : 11 if linked else 9], refs[11 if linked else 9 :]
-    w_ref, n1_ref, ka_ref, qa_ref, va_ref, stat_ref, load = refs[:7]
-    refs = refs[7:]
+    full_refs, refs = refs[9 : 12 if linked else 9], refs[12 if linked else 9 :]
+    wa_ref, wb_ref, w_ref, n1_ref, ka_ref, qa_ref, va_ref, stat_ref, load = refs[:9]
+    refs = refs[9:]
     rows, features = tok_ref.shape
     own = q_ref.shape[1]
     docs = len_ref.shape[1]
-    width = q_ref.shape[0]
-    per = width // HDIM
     step = pl.program_id(0)
+    parts = wa_ref.shape[0]
+    part, turn_at = lax.rem(step, parts), step // parts
     me = lax.axis_index("mp")
     mine = pl.ds(pl.multiple_of(me * own, own), own)
+    three = 3 * HDIM
 
     if linked:
-        src_a, src_b = refs[:2]
-        one = Gather(nz, src_a, w_ref, *refs[2:5])
-        two = Gather(nz, src_b, full_refs[1], *refs[5:8])
-        keep = pltpu.make_async_copy(w_ref, full_refs[0], load)
+        srcs = refs[:3]
+        one = Gather(nz, srcs[0], wa_ref, *refs[3:6], eager=True)
+        two = Gather(nz, srcs[1], wb_ref, *refs[6:9], eager=True)
+        last = Gather(nz, srcs[2], full_refs[2], *refs[9:12])
+        keeps = [
+            pltpu.make_async_copy(wa_ref, full_refs[0], load.at[0]),
+            pltpu.make_async_copy(wb_ref, full_refs[1], load.at[1]),
+        ]
 
     @pl.when(step == 0)
     def _():
         if linked:
             wq_ref, wg_ref, wo_ref, wd_ref, one_ref, two_ref = given
             for i in range(3):
-                src_a[:, i * width : (i + 1) * width] = wq_ref[i]
-            src_a[:, 3 * width :] = one_ref[...].astype(F32).T.astype(BF16)
+                srcs[0][:, i * HDIM : (i + 1) * HDIM] = wq_ref[i, :, :HDIM]
+            srcs[0][:, three : three + 1] = one_ref[...].astype(F32).T.astype(BF16)
+            srcs[0][:, three + 1 : three + 2] = two_ref[...].astype(F32).T.astype(BF16)
+            down = wd_ref[...].T
+            srcs[0][:, 256 - units % 128 :] = down[:, units - units % 128 :]
             greet(peers(nz))
             one.begin()
-            units = wd_ref.shape[0]
-            pair = 2 * units
+            for r in range(1, wq_ref.shape[2] // HDIM):
+                for i in range(3):
+                    at = (r - 1) * three + i * HDIM
+                    srcs[1][:, at : at + HDIM] = wq_ref[i, :, r * HDIM : (r + 1) * HDIM]
+            two.begin()
+            pair, width = 2 * units, wo_ref.shape[0]
             for i in range(2):
-                src_b[:, i * units : (i + 1) * units] = wg_ref[:, i, :]
-            src_b[:, pair : pair + width] = wo_ref[...].T
-            src_b[:, pair + width : pair + width + units] = wd_ref[...].T
-            src_b[:, pair + width + units :] = two_ref[...].astype(F32).T.astype(BF16)
+                srcs[2][:, i * units : (i + 1) * units] = wg_ref[:, i, :]
+            srcs[2][:, pair : pair + width] = wo_ref[...].T
+            srcs[2][:, pair + width :] = down[:, : units - units % 128]
         else:
-            fetch = pltpu.make_async_copy(given[0], w_ref, load)
-            fetch.start()
-
+            fetches = [pltpu.make_async_copy(g, w, load.at[i]) for i, (g, w) in enumerate(zip(given, (wa_ref, wb_ref)))]
+            for fetch in fetches:
+                fetch.start()
         _, position, _ = layout_rows(len_ref, docs, 0, rows)
         power = lax.broadcasted_iota(jnp.int32, (HALF, 1), 0).astype(F32) * (-2.0 / HDIM * math.log2(ROPE_BASE))
         angle = position.astype(F32) * jnp.exp2(power)
@@ -588,20 +628,18 @@
             stat_ref[1:2, at] = inv
             return carry
 
+        if linked:
+            one.all_along()
         lax.fori_loop(0, rows // own, measure, 0)
         if linked:
-            for d in range(nz):
-                if d:
-                    one.along(d)
-                one.over(d)
-            two.begin()
-            for d in range(nz):
-                one.corner(d)
-            one.end()
-            keep.start()
+            one.all_over()
+            last.begin()
+            one.rest()
+            keeps[0].start()
         else:
-            fetch.wait()
-        gain = w_ref[0, :, 3 * width :].astype(F32)
+            for fetch in fetches:
+                fetch.wait()
+        gain = wa_ref[0, :, three : three + 1].astype(F32)
 
         def norm(i, carry):
             at = pl.ds(pl.multiple_of(i * own, own), own)
@@ -613,77 +651,103 @@
         mine_ref[...] = n1_ref[:, mine]
 
     if linked:
-        for at, name, d in GATHER_STEPS:
-            pl.when(step == at)(functools.partial(getattr(two, name), d))
-
-    @pl.when(lax.rem(step, per) == 0)
+        gathers = {"two": two, "last": last}
+        for at, which, name, *d in GATHER_STEPS:
+            pl.when(step == at)(functools.partial(getattr(gathers[which], name), *d))
+
+        @pl.when(step == parts)
+        def _():
+            two.rest()
+            keeps[1].start()
+
+    @pl.when(turn_at == 0)
     def _():
-        project(w_ref, step // per, n1_ref, cos_ref, sin_ref, mine, q_ref, k_ref, v_ref)
-
-    head = pl.ds(pl.multiple_of(lax.rem(step, per) * HDIM, HDIM), HDIM)
-    ka_ref[:HDIM] = k_ref[head]
-    qa_ref[:HDIM] = q_ref[head]
-    va_ref[:HDIM] = v_ref[head]
-    wide = own
-    for i in range(own // wide):
-        at = slice(i * wide, (i + 1) * wide)
-        scores = dot(ka_ref[...], qa_ref[:, at], TN)
-        top = jnp.max(scores, axis=0, keepdims=True)
-        probs = jnp.exp2(scores - top).astype(BF16)
-        p_ref[0, :, at] = probs
-        out = dot(va_ref[...], probs, NN)
-        inv = 1.0 / out[HDIM : HDIM + 1]
-        o_ref[:, at] = (out[:HDIM] * inv).astype(BF16)
-        inv_ref[0, :, at] = inv
+        w_ref[...] = wa_ref[part, :, :three]
+
+    for r in range(1, 1 + wb_ref.shape[2] // three):
+
+        @pl.when(turn_at == r)
+        def _():
+            w_ref[...] = wb_ref[part, :, (r - 1) * three : r * three]
+
+    made = dot(w_ref[:, HDIM:], n1_ref[...], TN)
+    keys = turn(made[:HDIM], cos_ref[...], sin_ref[...], 1).astype(BF16)
+    k_ref[...] = keys
+    ka_ref[:HDIM] = keys
+    values = made[HDIM:].astype(BF16)
+    v_ref[...] = values
+    va_ref[:HDIM] = values
+    made = dot(w_ref[:, :HDIM], n1_ref[:, mine], TN) * (SCALE * LOG2E)
+    queries = turn(made, cos_ref[:, mine], sin_ref[:, mine], 1).astype(BF16)
+    q_ref[...] = queries
+    qa_ref[:HDIM] = queries
+    scores = dot(ka_ref[...], qa_ref[...], TN)
+    top = jnp.max(scores, axis=0, keepdims=True)
+    probs = jnp.exp2(scores - top).astype(BF16)
+    p_ref[0] = probs
+    out = dot(va_ref[...], probs, NN)
+    inv = 1.0 / out[HDIM : HDIM + 1]
+    o_ref[...] = (out[:HDIM] * inv).astype(BF16)
+    inv_ref[0] = inv
     if linked:
 
         @pl.when(step == pl.num_programs(0) - 1)
         def _():
-            keep.wait()
-            two.corner(nz - 1)
-            two.end()
+            for keep in keeps:
+                keep.wait()
+            last.corner(3)
+            last.end()
 
 
 GATHER_STEPS = (
-    (2, "along", 1),
-    (2, "over", 0),
-    (5, "over", 1),
-    (5, "along", 2),
-    (5, "corner", 0),
-    (7, "over", 2),
-    (8, "corner", 1),
-    (9, "along", 3),
-    (11, "over", 3),
-    (11, "corner", 2),
+    (0, "two", "along", 1),
+    (0, "two", "along", 2),
+    (0, "two", "along", 3),
+    (1, "two", "over", 0),
+    (1, "two", "over", 1),
+    (2, "two", "over", 2),
+    (2, "two", "over", 3),
+    (3, "last", "along", 1),
+    (3, "last", "over", 0),
+    (5, "last", "over", 1),
+    (5, "last", "along", 2),
+    (6, "last", "corner", 0),
+    (7, "last", "over", 2),
+    (8, "last", "corner", 1),
+    (8, "last", "along", 3),
+    (10, "last", "corner", 2),
+    (10, "last", "over", 3),
 )
 
 
-def forward(nz, n_mp, lengths, tokens, weights, columns):
+def forward(nz, n_mp, units, lengths, tokens, weights, columns):
     rows, features = tokens.shape
     own, width, heads = rows // n_mp, features // n_mp, features // HDIM
     per = width // HDIM
     linked = nz > 0
     hbm = pl.BlockSpec(memory_space=pl.ANY)
-    part = lambda h: (h // per, 0)
+    head = lambda h: lax.rem(h, n_mp) * per + h // n_mp
+    row = lambda h: (head(h), 0)
+    cube = lambda h: (head(h), 0, 0)
     vm = pl.BlockSpec(memory_space=pltpu.VMEM)
     n = Gather.count(nz) if linked else 0
     dma = pltpu.SemaphoreType.DMA
     depth = features // (2 * nz) if linked else 0
     full_shapes = [jax.ShapeDtypeStruct((n_mp, features, c), BF16) for c in columns] if linked else []
     return pl.pallas_call(
-        functools.partial(forward_kernel, nz),
+        functools.partial(forward_kernel, nz, units),
         grid=(heads,),
-        in_specs=[pl.BlockSpec(memory_space=pltpu.SMEM), vm] + ([vm] * 6 if linked else [hbm]),
+        in_specs=[pl.BlockSpec(memory_space=pltpu.SMEM), vm] + ([vm] * 6 if linked else [hbm] * 2),
         out_specs=[
             whole(features, own),
-            pl.BlockSpec((width, own), part),
-            pl.BlockSpec((width, rows), part),
-            pl.BlockSpec((width, rows), part),
+            pl.BlockSpec((HDIM, own), row),
+            pl.BlockSpec((HDIM, rows), row),
+            pl.BlockSpec((HDIM, rows), row),
             whole(HALF, rows),
             whole(HALF, rows),
-            pl.BlockSpec((HDIM, own), lambda h: (h, 0)),
-            pl.BlockSpec((1, rows, own), lambda h: (h, 0, 0)),
-            pl.BlockSpec((1, 1, own), lambda h: (h, 0, 0)),
+            pl.BlockSpec((HDIM, own), row),
+            pl.BlockSpec((1, rows, own), cube),
+            pl.BlockSpec((1, 1, own), cube),
         ]
         + [hbm] * len(full_shapes),
         out_shape=[
@@ -700,15 +764,17 @@
         + full_shapes,
         scratch_shapes=[
             pltpu.VMEM((n_mp, features, columns[0]), BF16),
+            pltpu.VMEM((n_mp, features, columns[1]), BF16),
+            pltpu.VMEM((features, 3 * HDIM), BF16),
             pltpu.VMEM((features, rows), BF16),
             pltpu.VMEM((AUG, rows), BF16),
             pltpu.VMEM((AUG, own), BF16),
             pltpu.VMEM((AUG, rows), BF16),
             pltpu.VMEM((8, rows), F32),
-            dma,
+            dma((2,)),
         ]
         + (
-            [pltpu.VMEM((depth, c), BF16) for c in columns] + [dma((n,)), dma((n,)), dma] * 2
+            [pltpu.VMEM((depth, c), BF16) for c in columns] + [dma((n,)), dma((n,)), dma] * 3
             if linked
             else []
         ),
@@ -721,7 +787,7 @@
     )(lengths, tokens, *weights)
 
 
-def middle(len_ref, me, tok_ref, cot_ref, heads_ref, inv_ref, w_ref, units, out_ref, mcot_ref, do_ref, keep, sent, done):
+def middle(len_ref, me, tok_ref, cot_ref, heads_ref, inv_ref, w_ref, gain, units, out_ref, mcot_ref, do_ref, keep, sent, done):
     own, features = tok_ref.shape
     parts = w_ref.shape[0]
     width = features // parts
@@ -742,7 +808,6 @@
     for m in range(1, parts):
         total += dot(w_out(m), heads_ref[m * width : (m + 1) * width], NN)
     middle = tok_ref[...].T.astype(F32) + total
-    gain = w_ref[0, :, pair + width + units :].astype(F32)
     hat, inv_sigma = normalize(middle)
     normed = (hat * gain).astype(BF16)
     total = middle
@@ -767,7 +832,7 @@
         keep("gu", m, dot(normed, cots, NT).astype(BF16))
         back += dot(w_gu(m), cots, NN)
     done()
-    gain_cot = jnp.sum(back * hat, axis=1, keepdims=True).astype(BF16)
+    keep("gain", 0, jnp.sum(back * hat, axis=1, keepdims=True))
     d = back * gain
     middle_cot = branch.astype(F32) + inv_sigma * (
         d - jnp.mean(d, axis=0, keepdims=True) - hat * jnp.mean(d * hat, axis=0, keepdims=True)
@@ -786,12 +851,11 @@
             do_ref[head] = jnp.concatenate([cot, high, inner - high, pad], axis=0).astype(BF16)
     for m in range(parts):
         keep("out", m, dot(attn_cot, heads_ref[m * width : (m + 1) * width], NT).astype(BF16))
-        keep("gain", m, gain_cot)
 
 
 def mid_kernel(
-    units, len_ref, tok_hbm, cot_hbm, heads_ref, inv_ref, w_hbm,
-    out_ref, mcot_ref, do_ref, g_ref, o_ref, tok_ref, cot_ref, w_ref, load,
+    units, len_ref, tok_hbm, cot_hbm, heads_ref, inv_ref, two_ref, w_hbm,
+    out_ref, mcot_ref, do_ref, g_ref, o_ref, gain_ref, tok_ref, cot_ref, w_ref, load,
 ):
     own = tok_ref.shape[0]
     me = lax.axis_index("mp")
@@ -805,7 +869,7 @@
         copy.start()
     for copy in loads:
         copy.wait()
-    pair, width = 2 * units, o_ref.shape[2] - 1
+    pair = 2 * units
 
     def keep(what, m, made):
         if what == "gu":
@@ -813,31 +877,33 @@
         elif what == "down":
             g_ref[m, :, pair:] = made
         elif what == "out":
-            o_ref[m, :, :width] = made
+            o_ref[m] = made
         else:
-            o_ref[m, :, width:] = made
+            gain_ref[...] = made
 
     nothing = lambda: None
     middle(
-        len_ref, me, tok_ref, cot_ref, heads_ref, inv_ref, w_ref, units, out_ref, mcot_ref, do_ref, keep, nothing, nothing
+        len_ref, me, tok_ref, cot_ref, heads_ref, inv_ref, w_ref, two_ref[...].astype(F32), units, out_ref, mcot_ref, do_ref,
+        keep, nothing, nothing,
     )
 
 
-def mid(n_mp, lengths, tokens, out_grad, heads_out, inv, w_rest, units):
+def mid(n_mp, lengths, tokens, out_grad, heads_out, inv, gain, w_rest, units):
     features, own = heads_out.shape
     heads = inv.shape[0]
     vm = pl.BlockSpec(memory_space=pltpu.VMEM)
     hbm = pl.BlockSpec(memory_space=pl.ANY)
     return pl.pallas_call(
         functools.partial(mid_kernel, units),
-        in_specs=[pl.BlockSpec(memory_space=pltpu.SMEM), hbm, hbm, vm, vm, hbm],
-        out_specs=[vm] * 5,
+        in_specs=[pl.BlockSpec(memory_space=pltpu.SMEM), hbm, hbm, vm, vm, vm, hbm],
+        out_specs=[vm] * 6,
         out_shape=[
             jax.ShapeDtypeStruct((own, features), BF16),
             jax.ShapeDtypeStruct((features, own), F32),
             jax.ShapeDtypeStruct((heads, AUG, own), BF16),
             jax.ShapeDtypeStruct((n_mp, features, 3 * units), BF16),
-            jax.ShapeDtypeStruct((n_mp, features, features // n_mp + 1), BF16),
+            jax.ShapeDtypeStruct((n_mp, features, features // n_mp), BF16),
+            jax.ShapeDtypeStruct((features, 1), F32),
         ],
         scratch_shapes=[
             pltpu.VMEM((own, features), BF16),
@@ -847,7 +913,7 @@
         ],
         compiler_params=pltpu.CompilerParams(vmem_limit_bytes=VMEM_BYTES),
         name="mid",
-    )(lengths, tokens, out_grad, heads_out, inv, w_rest)
+    )(lengths, tokens, out_grad, heads_out, inv, gain, w_rest)
 
 
 SLOTS = 7
@@ -855,31 +921,40 @@
 
 
 def backward_kernel(nz, units, *refs):
-    len_ref, q_ref, k_ref, v_ref, p_ref, cos_ref, sin_ref, n1_ref, heads_ref, inv_ref, tok_hbm, cot_hbm, w_hbm, wr_hbm = refs[:14]
-    dq_ref, dr_ref, in_full, out_full = refs[14:18]
-    w_ref, wr_ref, gr_ref, do_ref, mcot_ref, pc_ref, qc_ref, acc_ref, gc_ref, va_ref, tok_ref, cot_ref, own_ref, load = refs[18:32]
-    refs = refs[32:]
+    len_ref, q_ref, k_ref, v_ref, p_ref, cos_ref, sin_ref, n1_ref, heads_ref, inv_ref, wa_ref, tok_hbm, cot_hbm, wb_hbm, wr_hbm = refs[:15]
+    dq_ref, dr_ref, gains_ref, in_full, out_full = refs[15:20]
+    wb_ref, wr_ref, gr_ref, do_ref, mcot_ref, pc_ref, qc_ref, acc_ref, gc_ref, va_ref, tok_ref, cot_ref, own_ref, load = refs[20:34]
+    refs = refs[34:]
     gq_ref = wr_ref.at[:, :, pl.ds(0, dq_ref.shape[1])]
     rest = Scatter(nz, (0, 1), gr_ref, gr_ref, dr_ref, *refs[:6])
     low = Scatter(nz, (0,), gq_ref, gq_ref, dq_ref, *refs[6:12])
-    high = Scatter(nz, (1,), gq_ref, gq_ref, dq_ref, *refs[12:18], shared=4 * (w_ref.shape[2] // 3))
+    high = Scatter(nz, (1,), gq_ref, gq_ref, dq_ref, *refs[12:18])
     fold = Fold(*refs[18:23])
     in_share = Share(own_ref.at[0], in_full, *refs[23:26])
     out_share = Share(own_ref.at[1], out_full, *refs[26:29])
+    gains = Everyone(*refs[29:33])
     step, heads = pl.program_id(0) - 1, pl.num_programs(0) - 1
-    parts = w_ref.shape[0]
+    parts = wa_ref.shape[0]
     features, own = n1_ref.shape
     rows = k_ref.shape[1]
     width = features // parts
     per = width // HDIM
     me = lax.axis_index("mp")
     mine = pl.ds(pl.multiple_of(me * own, own), own)
-    late = pltpu.make_async_copy(w_hbm, w_ref, load.at[3])
+    late = pltpu.make_async_copy(wb_hbm, wb_ref, load.at[3])
+    three = 3 * HDIM
+    shards = features // gains_ref.shape[1]
+
+    def put(row, column):
+        for i in range(shards):
+            at = row * shards + i
+            gains.held[0, at : at + 1, : features // shards] = column[i * (features // shards) : (i + 1) * (features // shards)].T
 
     @pl.when(step < 0)
     def _():
+        gains.held[0] = jnp.zeros(gains.held.shape[1:], F32)
         loads = [
-            pltpu.make_async_copy(wr_hbm, wr_ref, load.at[0]),
+            pltpu.make_async_copy(wr_hbm, wr_ref.at[:, :, pl.ds(0, wr_hbm.shape[2])], load.at[0]),
             pltpu.make_async_copy(tok_hbm.at[mine], tok_ref, load.at[1]),
             pltpu.make_async_copy(cot_hbm.at[mine], cot_ref, load.at[2]),
         ]
@@ -890,6 +965,8 @@
             copy.wait()
         late.start()
         pair = 2 * units
+        for m in range(parts):
+            wr_ref[m, :, wr_hbm.shape[2] :] = wa_ref[m, :, 256 - units % 128 :]
 
         def keep(what, m, made):
             if what == "gu":
@@ -899,10 +976,11 @@
             elif what == "out":
                 wr_ref[m, :, 3 * width : 4 * width] = made
             else:
-                wr_ref[m, :, 4 * width + 1 : 4 * width + 2] = made
+                put(1, made)
 
         middle(
-            len_ref, me, tok_ref, cot_ref, heads_ref, inv_ref, wr_ref, units, own_ref.at[1], mcot_ref, do_ref, keep,
+            len_ref, me, tok_ref, cot_ref, heads_ref, inv_ref, wr_ref, wa_ref[0, :, three + 1 : three + 2].astype(F32), units,
+            own_ref.at[1], mcot_ref, do_ref, keep,
             lambda: out_share.begin(0), lambda: rest.begin(2, 3),
         )
         va_ref[HDIM:] = jnp.full((AUG - HDIM, rows), -1.0, BF16)
@@ -911,17 +989,15 @@
         late.wait()
 
     def collect(head):
-        made = fold.end(head)
-        at = lax.rem(head, per) * HDIM
-        pc_ref[pl.ds(pl.multiple_of(width + at, HDIM), HDIM)] = made[:HDIM]
-        pc_ref[pl.ds(pl.multiple_of(2 * width + at, HDIM), HDIM)] = made[HDIM:]
+        at = lax.rem(head, per) * three
+        pc_ref[pl.ds(pl.multiple_of(at + HDIM, HDIM), 2 * HDIM)] = fold.end(head)
 
     def close(part):
         for i in range(per):
-            pc_ref[i * HDIM : (i + 1) * HDIM] = qc_ref[lax.rem(part, 3), i * HDIM : (i + 1) * HDIM]
+            pc_ref[i * three : i * three + HDIM] = qc_ref[lax.rem(part, 3), i * HDIM : (i + 1) * HDIM]
         made = dot(n1_ref[...], pc_ref[...], NT)
         wr_ref[part, :, : 3 * width] = made.astype(BF16)
-        weights = w_ref[part, :, : 3 * width]
+        weights = jnp.concatenate([wa_ref[part, :, :three], wb_ref[part]], axis=1)
         gc_ref[...] += jnp.sum(made * weights.astype(F32), axis=1, keepdims=True)
         acc_ref[...] += dot(weights, pc_ref[...], NN)
 
@@ -955,7 +1031,7 @@
         def _():
             close((step - LAG) // per)
 
-    sums = {"rest": rest, "low": low, "high": high, "out": out_share}
+    sums = {"rest": rest, "low": low, "high": high, "out": out_share, "gains": gains}
     for at, which, name, *d in SUM_STEPS:
         pl.when(step == at)(functools.partial(getattr(sums[which], name), *d))
 
@@ -966,11 +1042,10 @@
             collect(step - back)
             if (heads - 1 - back) % per == per - 1:
                 close((step - back) // per)
-        gain = w_ref[0, :, 3 * width :].astype(F32)
-        gain_cot = (gc_ref[...] / gain).astype(BF16)
-        for m in range(2, parts):
-            wr_ref[m, :, 4 * width : 4 * width + 1] = gain_cot
         high.begin(2, 3, 1, 0)
+        gain = wa_ref[0, :, three : three + 1].astype(F32)
+        put(0, gc_ref[...] / gain)
+        gains.begin()
         own_ref[0] = finish(tok_ref[...], gain, acc_ref[...], mcot_ref[...])
         in_share.begin(0)
         for which, name, *d in LAST_STEPS:
@@ -978,10 +1053,19 @@
         in_share.on(0)
         for which in (rest, low, high):
             which.along()
+        gains.hop(4)
         for which in (rest, low, high):
             which.end()
         out_share.end()
         in_share.end()
+        made = gains.end()
+        dp = lax.axis_index("dp")
+        for row in range(2):
+            for i in range(shards):
+
+                @pl.when(dp == i)
+                def _():
+                    gains_ref[row : row + 1] = made[row * shards + i : row * shards + i + 1, : features // shards]
 
 
 SUM_STEPS = (
@@ -1020,22 +1104,26 @@
     ("high", "cross", 2),
     ("high", "cross", 3),
     ("low", "over", 0),
+    ("gains", "hop", 0),
     ("high", "over", 2),
     ("high", "cross", 1),
     ("high", "cross", 0),
+    ("gains", "hop", 1),
     ("high", "over", 3),
+    ("gains", "hop", 2),
     ("high", "over", 1),
+    ("gains", "hop", 3),
     ("high", "over", 0),
 )
 
 
-def backward(nz, lengths, q, k, v, p, cos, sin, n1, heads_out, inv, tokens, out_grad, w_qkv, w_rest, units):
+def backward(nz, lengths, q, k, v, p, cos, sin, n1, heads_out, inv, tokens, out_grad, w_a, w_b, w_rest, units):
     (features, own), rows = q.shape, k.shape[1]
-    n_mp = w_qkv.shape[0]
+    n_mp = w_a.shape[0]
     heads = features // HDIM
     width = features // n_mp
     depth = features // (2 * nz)
-    columns = lanes(4 * width + 2), 3 * units
+    columns = 4 * width, 3 * units
     hbm = pl.BlockSpec(memory_space=pl.ANY)
     vm = pl.BlockSpec(memory_space=pltpu.VMEM)
     row = lambda h: (jnp.maximum(h - 1, 0), 0)
@@ -1051,18 +1139,19 @@
             pl.BlockSpec((HDIM, rows), row),
             pl.BlockSpec((1, rows, own), cube),
         ]
-        + [vm] * 5
+        + [vm] * 6
         + [hbm] * 4,
-        out_specs=[vm, vm, hbm, hbm],
+        out_specs=[vm, vm, vm, hbm, hbm],
         out_shape=[
             jax.ShapeDtypeStruct((depth, columns[0]), F32),
             jax.ShapeDtypeStruct((depth, columns[1]), F32),
+            jax.ShapeDtypeStruct((2, depth), F32),
             jax.ShapeDtypeStruct((rows, features), BF16),
             jax.ShapeDtypeStruct((rows, features), BF16),
         ],
         scratch_shapes=[
-            pltpu.VMEM(w_qkv.shape, BF16),
-            pltpu.VMEM(w_rest.shape, BF16),
+            pltpu.VMEM(w_b.shape, BF16),
+            pltpu.VMEM((n_mp, features, width + 3 * units), BF16),
             pltpu.VMEM((n_mp, features, 3 * units), BF16),
             pltpu.VMEM((heads, AUG, own), BF16),
             pltpu.VMEM((features, own), F32),
@@ -1081,28 +1170,27 @@
         + Scatter.scratch(nz, (1,), depth, columns[0])
         + Fold.scratch(n_mp, own, SLOTS)
         + Share.sems(1)
-        + Share.sems(1),
+        + Share.sems(1)
+        + Everyone.scratch(nz, 4 * nz),
         compiler_params=pltpu.CompilerParams(
             dimension_semantics=("arbitrary",), collective_id=3, has_side_effects=True, vmem_limit_bytes=VMEM_BYTES
         ),
         name="backward",
-    )(lengths, q, k, v, p, cos, sin, n1, heads_out, inv, tokens, out_grad, w_qkv, w_rest)
-
-
-def lanes(columns):
-    return (columns + 127) // 128 * 128
-
-
-def deliver_kernel(units, in_ref, out_ref, dq_ref, dr_ref, grad_ref, to_ref, gq_ref, go_ref, gg_ref, gd_ref, one_ref, two_ref):
+    )(lengths, q, k, v, p, cos, sin, n1, heads_out, inv, w_a, tokens, out_grad, w_b, w_rest)
+
+
+def deliver_kernel(units, in_ref, out_ref, dq_ref, dr_ref, gains_ref, grad_ref, to_ref, gq_ref, go_ref, gg_ref, gd_ref, one_ref, two_ref):
     @pl.when(pl.program_id(0) == 0)
     def _():
         width = go_ref.shape[0]
         pair = 2 * units
-        for i in range(3):
-            gq_ref[i] = dq_ref[:, i * width : (i + 1) * width]
+        for r in range(width // HDIM):
+            for i in range(3):
+                at = (3 * r + i) * HDIM
+                gq_ref[i, :, r * HDIM : (r + 1) * HDIM] = dq_ref[:, at : at + HDIM]
         go_ref[...] = dq_ref[:, 3 * width : 4 * width].T
-        one_ref[...] = dq_ref[:, 4 * width : 4 * width + 1].T
-        two_ref[...] = dq_ref[:, 4 * width + 1 : 4 * width + 2].T
+        one_ref[...] = gains_ref[0:1]
+        two_ref[...] = gains_ref[1:2]
         for i in range(2):
             gg_ref[:, i, :] = dr_ref[:, i * units : (i + 1) * units]
         gd_ref[...] = dr_ref[:, pair : pair + units].T
@@ -1111,7 +1199,7 @@
     to_ref[...] = out_ref[...]
 
 
-def deliver(layer_out, input_grad, d_qkv, d_rest, width, units):
+def deliver(layer_out, input_grad, d_qkv, d_rest, gains, width, units):
     rows, features = input_grad.shape
     depth = d_qkv.shape[0]
     shape = lambda *s: jax.ShapeDtypeStruct(s, F32)
@@ -1121,12 +1209,12 @@
     return pl.pallas_call(
         functools.partial(deliver_kernel, units),
         grid=(steps,),
-        in_specs=[slab, slab, whole(*d_qkv.shape), whole(*d_rest.shape)],
+        in_specs=[slab, slab, whole(*d_qkv.shape), whole(*d_rest.shape), whole(*gains.shape)],
         out_specs=[slab, slab] + [whole(*s) for s in shapes],
         out_shape=[shape(rows, features), jax.ShapeDtypeStruct((rows, features), BF16)] + [shape(*s) for s in shapes],
         compiler_params=params("arbitrary"),
         name="deliver",
-    )(input_grad, layer_out, d_qkv, d_rest)
+    )(input_grad, layer_out, d_qkv, d_rest, gains)
 
 
 def per_device(n_dp, n_mp, tokens, out_grad, w_qkv, w_out, w_gu, w_down, gain_attn, gain_mlp, lengths):
@@ -1136,47 +1224,56 @@
     everyone = ("mp", "dp")
     linked = n_mp == 4 and n_dp == 8 and depth % 32 == 0 and features // HDIM == 12
     nz = n_dp // 2 if linked else 0
-    columns = 3 * width + 1, 3 * units + width + 1
+    three = 3 * HDIM
+    loose = units % 128
+    columns = 256, 3 * width - three, 3 * units + width - loose
     wq = w_qkv.transpose(1, 0, 2)
     if linked:
         weights = wq, w_gu, w_out, w_down, gain_attn[None], gain_mlp[None]
-        n1, q, k, v, cos, sin, heads_out, probs, inv, full_qkv, full_rest = forward(
-            nz, n_mp, lengths, tokens, weights, columns
+        n1, q, k, v, cos, sin, heads_out, probs, inv, w_a, w_b, w_c = forward(
+            nz, n_mp, units, lengths, tokens, weights, columns
         )
-        d_qkv, d_rest, in_full, layer_out = backward(
-            nz, lengths, q, k, v, probs, cos, sin, n1, heads_out, inv, tokens, out_grad, full_qkv, full_rest, units
+        d_qkv, d_rest, gains, in_full, layer_out = backward(
+            nz, lengths, q, k, v, probs, cos, sin, n1, heads_out, inv, tokens, out_grad, w_a, w_b, w_c, units
         )
     else:
+        by_head = w_qkv.reshape(depth, 3, width // HDIM, HDIM).transpose(0, 2, 1, 3).reshape(depth, 3 * width)
+        blank = jnp.zeros((depth, columns[0] - three - 2), BF16)
         shards = [
-            jnp.concatenate([*wq, gain_attn[:, None]], axis=1),
-            jnp.concatenate([w_gu.reshape(depth, -1), w_out.T, w_down.T, gain_mlp[:, None]], axis=1),
+            jnp.concatenate([by_head[:, :three], gain_attn[:, None], gain_mlp[:, None], blank], axis=1),
+            by_head[:, three:],
+            jnp.concatenate([w_gu.reshape(depth, -1), w_out.T, w_down.T], axis=1),
         ]
-        full_qkv, full_rest = (
+        w_a, w_b, w_c = (
             lax.all_gather(s, everyone, axis=0, tiled=True).reshape(n_mp, features, s.shape[1]) for s in shards
         )
-        n1, q, k, v, cos, sin, heads_out, probs, inv = forward(nz, n_mp, lengths, tokens, [full_qkv], columns)
-        layer_out, middle_cot, do, g_rest, g_out = mid(
-            n_mp, lengths, tokens, out_grad, heads_out, inv, full_rest, units
+        n1, q, k, v, cos, sin, heads_out, probs, inv = forward(nz, n_mp, units, lengths, tokens, [w_a, w_b], columns)
+        layer_out, middle_cot, do, g_rest, g_out, gain_two = mid(
+            n_mp, lengths, tokens, out_grad, heads_out, inv, w_a[0, :, three + 1 : three + 2], w_c, units
         )
         own = middle_cot.shape[1]
-        g_qkv, nc = last(q, k, v, do, probs, cos, sin, lax.all_gather(n1, "mp", axis=1, tiled=True), full_qkv)
-        gain_one = full_qkv[0, :, 3 * width :].astype(F32)
+        swap = lambda g, a, b: g.reshape(n_mp, features, a, b, HDIM).swapaxes(2, 3).reshape(n_mp, features, 3 * width)
+        natural = jnp.concatenate([w_a[..., :three], w_b], axis=2)
+        natural = jnp.concatenate([swap(natural, width // HDIM, 3), w_a[..., three : three + 1]], axis=2)
+        g_qkv, nc = last(q, k, v, do, probs, cos, sin, lax.all_gather(n1, "mp", axis=1, tiled=True), natural)
+        gain_one = w_a[0, :, three : three + 1].astype(F32)
         tok = lax.dynamic_slice_in_dim(tokens, lax.axis_index("mp") * own, own, 0)
         nc_own = lax.psum_scatter(nc, "mp", scatter_dimension=0, tiled=True)[0]
         in_own = finish(tok, gain_one, nc_own.astype(F32), middle_cot)
         layer_out, in_full = (lax.all_gather(v, "mp", axis=0, tiled=True) for v in (layer_out, in_own))
-        g_qkv = jnp.concatenate(
-            [g_qkv[..., : 3 * width], g_out[..., :width], g_qkv[..., 3 * width :], g_out[..., width:]], axis=2
-        )
+        both = jnp.stack([g_qkv[0, :, -1].astype(F32), gain_two[:, 0]])
+        both = lax.psum(both, everyone)
+        gains = lax.dynamic_slice_in_dim(both, lax.axis_index("dp") * depth, depth, 1)
+        g_qkv = jnp.concatenate([swap(g_qkv[..., : 3 * width], 3, width // HDIM), g_out], axis=2)
         d_qkv, d_rest = (
             lax.psum_scatter(
                 g.reshape(n_mp * features, -1), everyone, scatter_dimension=0, tiled=True
             ).astype(F32)
             for g in (g_qkv, g_rest)
         )
-    input_grad, layer_out, g_q, g_o, g_g, g_d, one, two = deliver(layer_out, in_full, d_qkv, d_rest, width, units)
-    if not linked:
-        one, two = (lax.all_gather(g, "mp")[0] for g in (one, two))
+    input_grad, layer_out, g_q, g_o, g_g, g_d, one, two = deliver(
+        layer_out, in_full, d_qkv, d_rest, gains, width, units
+    )
     return layer_out, input_grad, g_q.transpose(1, 0, 2), g_o, g_g, g_d, one[0], two[0]
 
 

time: 202 us -> 191 us (0.946)
  Pallas kernels: 201 us -> 190 us
    pallas_call x1, Pallas kernels: 79.6 us -> 72.1 us  [forward(): pl.pallas_call(functools.partial(forward_kernel, nz, units), grid=(heads,...]
    pallas_call x1, Pallas kernels: 114 us -> 110 us  [backward(): pl.pallas_call(functools.partial(backward_kernel, nz, units), grid=(heads...]
where the time goes in v6:
time: 191 us
  Pallas kernels  190 us (99%)
    pallas_call x1, Pallas kernels, backward(): pl.pallas_call(functools.partial(backward_kernel, nz, units), grid=(heads...  110 us
    pallas_call x1, Pallas kernels, forward(): pl.pallas_call(functools.partial(forward_kernel, nz, units), grid=(heads,...  72.1 us
    pallas_call x1, Pallas kernels, deliver(): pl.pallas_call(functools.partial(deliver_kernel, units), grid=(steps,), i...  7.54 us

profile of v6, /device:TPU:0, one launch (start us, length us, event | category | flops | bytes accessed | tf_op | source)
XLA Modules:
  0.0 190.6 jit_solution(259804376171859481)
XLA Ops:
  0.6 72.1 %forward.1 = (bf16[768,512]{1,0:T(8,128)(2,1)}, bf16[768,512]{1,0:T(8,128)(2,1)}, bf16[768,2048]{1,0:T(8,128)(2,1)}, bf16[768,2048]{1,0:T(8,128)(2,1)}, f32[32,2...) custom-call(s32[1,8]{1,0:T(1,128)} %refs_0_.1, ...), custom_call_target="tpu_custom_call" | custom-call | tf_op jit(solution)/shard_map/forward/pallas_call | solution.py:737
  72.8 110.1 %backward.1 = (f32[96,768]{1,0:T(8,128)}, f32[96,864]{1,0:T(8,128)}, f32[2,96]{1,0:T(2,128)}, bf16[2048,768]{1,0:T(8,128)(2,1)}, bf16[2048,768]{1,0:T(8,128)(2,1)}) custom-call(s32[1,8]{1,0:T(1,128)} %refs_0_.1, bf16[768,512]{1,0:T(8,128)(2,1)} %get-tuple-element.33.refs_1_, bf16[768,2048]{1,0:T(8,128)(2,1)} %get-tuple-element.34.refs_2_, ...), custom_call_target="tpu_custom_call" | custom-call | tf_op jit(solution)/shard_map/backward/pallas_call | solution.py:1132
  182.9 7.5 %deliver.1 = (f32[2048,768]{1,0:T(8,128)}, bf16[2048,768]{1,0:T(8,128)(2,1)}, f32[3,96,192]{2,1,0:T(8,128)}, f32[192,96]{1,0:T(8,128)}, f32[96,2,288]{2,1,0:T(2,...) custom-call(bf16[2048,768]{1,0:T(8,128)(2,1)} %get-tuple-element.45.in_ref, ...), custom_call_target="tpu_custom_call" | custom-call | tf_op jit(solution)/shard_map/deliver/pallas_call | solution.py:1209

commit v7 on v6

--- a/solution.py
+++ b/solution.py
@@ -258,6 +258,9 @@
             self.start(kind, 0)
         self.own().start()
 
+    def push(self, d):
+        self.start("Z", d)
+
     def all_along(self):
         for d in range(1, self.nz):
             self.along(d)
@@ -273,8 +276,6 @@
 
     def along(self, d):
         self.arrived("Z", d)
-        if d + 1 < self.nz and not self.eager:
-            self.start("Z", d + 1)
         for kind in ("X", "Y", "S"):
             self.start(kind, d)
 
@@ -419,16 +420,14 @@
         for side in range(2):
             rows = self.rows(d, side)
             for u, up in enumerate(self.ups):
-                made = self.part[2 * up + c, rows].astype(F32) + self.core[u, rows].astype(F32)
-                self.core[u, rows] = made.astype(BF16)
+                self.core[u, rows] = self.part[2 * up + c, rows] + self.core[u, rows]
 
     def over(self, d):
         _, x, _, _ = place()
         self.message("X", d).wait_recv()
         rows, lane = self.rows(d, x), self.lane(d)
         for u in range(len(self.ups)):
-            made = self.core[u, rows].astype(F32) + self.side[u, lane].astype(F32)
-            self.side[u, lane] = made.astype(BF16)
+            self.side[u, lane] = self.core[u, rows] + self.side[u, lane]
         if d:
             self.message("Z", d).start()
 
@@ -539,8 +538,7 @@
         _, _, y, c = place()
         slot = lax.rem(head, self.slots)
         self.message("far", head).wait_recv()
-        made = self.part[slot, 2 * (1 - y) + c].astype(F32) + self.near[slot, 1 - y].astype(F32)
-        self.near[slot, 1 - y] = made.astype(BF16)
+        self.near[slot, 1 - y] = self.part[slot, 2 * (1 - y) + c] + self.near[slot, 1 - y]
         self.message("Y", head).start()
 
     def end(self, head):
@@ -703,20 +701,22 @@
     (0, "two", "along", 1),
     (0, "two", "along", 2),
     (0, "two", "along", 3),
+    (0, "last", "push", 2),
     (1, "two", "over", 0),
     (1, "two", "over", 1),
     (2, "two", "over", 2),
     (2, "two", "over", 3),
+    (2, "last", "push", 3),
     (3, "last", "along", 1),
     (3, "last", "over", 0),
+    (4, "last", "along", 2),
     (5, "last", "over", 1),
-    (5, "last", "along", 2),
     (6, "last", "corner", 0),
+    (6, "last", "along", 3),
     (7, "last", "over", 2),
     (8, "last", "corner", 1),
-    (8, "last", "along", 3),
-    (10, "last", "corner", 2),
-    (10, "last", "over", 3),
+    (9, "last", "over", 3),
+    (11, "last", "corner", 2),
 )
 
 
@@ -787,7 +787,7 @@
     )(lengths, tokens, *weights)
 
 
-def middle(len_ref, me, tok_ref, cot_ref, heads_ref, inv_ref, w_ref, gain, units, out_ref, mcot_ref, do_ref, keep, sent, done):
+def middle(len_ref, me, tok_ref, cot_ref, heads_ref, inv_ref, w_ref, gain, units, out_ref, mcot_ref, do_ref, keep, sent, done, later):
     own, features = tok_ref.shape
     parts = w_ref.shape[0]
     width = features // parts
@@ -849,6 +849,7 @@
             high = inner.astype(BF16).astype(F32)
             pad = jnp.zeros((AUG - HDIM - 2, own), F32)
             do_ref[head] = jnp.concatenate([cot, high, inner - high, pad], axis=0).astype(BF16)
+    later()
     for m in range(parts):
         keep("out", m, dot(attn_cot, heads_ref[m * width : (m + 1) * width], NT).astype(BF16))
 
@@ -884,7 +885,7 @@
     nothing = lambda: None
     middle(
         len_ref, me, tok_ref, cot_ref, heads_ref, inv_ref, w_ref, two_ref[...].astype(F32), units, out_ref, mcot_ref, do_ref,
-        keep, nothing, nothing,
+        keep, nothing, nothing, nothing,
     )
 
 
@@ -918,6 +919,7 @@
 
 SLOTS = 7
 LAG = 4
+PIECES = 4
 
 
 def backward_kernel(nz, units, *refs):
@@ -930,7 +932,7 @@
     low = Scatter(nz, (0,), gq_ref, gq_ref, dq_ref, *refs[6:12])
     high = Scatter(nz, (1,), gq_ref, gq_ref, dq_ref, *refs[12:18])
     fold = Fold(*refs[18:23])
-    in_share = Share(own_ref.at[0], in_full, *refs[23:26])
+    in_share = Share(own_ref.at[0], in_full, *refs[23:26], PIECES)
     out_share = Share(own_ref.at[1], out_full, *refs[26:29])
     gains = Everyone(*refs[29:33])
     step, heads = pl.program_id(0) - 1, pl.num_programs(0) - 1
@@ -965,6 +967,11 @@
             copy.wait()
         late.start()
         pair = 2 * units
+
+        def first():
+            rest.chip(2)
+            rest.cross(2)
+
         for m in range(parts):
             wr_ref[m, :, wr_hbm.shape[2] :] = wa_ref[m, :, 256 - units % 128 :]
 
@@ -981,7 +988,7 @@
         middle(
             len_ref, me, tok_ref, cot_ref, heads_ref, inv_ref, wr_ref, wa_ref[0, :, three + 1 : three + 2].astype(F32), units,
             own_ref.at[1], mcot_ref, do_ref, keep,
-            lambda: out_share.begin(0), lambda: rest.begin(2, 3),
+            lambda: out_share.begin(0), lambda: rest.begin(2, 3), first,
         )
         va_ref[HDIM:] = jnp.full((AUG - HDIM, rows), -1.0, BF16)
         acc_ref[...] = jnp.zeros_like(acc_ref)
@@ -1031,28 +1038,31 @@
         def _():
             close((step - LAG) // per)
 
-    sums = {"rest": rest, "low": low, "high": high, "out": out_share, "gains": gains}
+    sums = {"rest": rest, "low": low, "high": high, "out": out_share, "in": in_share, "gains": gains}
     for at, which, name, *d in SUM_STEPS:
         pl.when(step == at)(functools.partial(getattr(sums[which], name), *d))
 
     @pl.when(step == heads - 1)
     def _():
         fold.chip(step)
+        for which, name, *d in FLUSH_STEPS:
+            getattr(sums[which], name)(*d)
         for back in range(LAG - 1, -1, -1):
             collect(step - back)
-            if (heads - 1 - back) % per == per - 1:
+            if (features // HDIM - 1 - back) % per == per - 1:
                 close((step - back) // per)
         high.begin(2, 3, 1, 0)
         gain = wa_ref[0, :, three : three + 1].astype(F32)
+        size = own // PIECES
+        for i in range(PIECES):
+            at = slice(i * size, (i + 1) * size)
+            own_ref[0, at] = finish(tok_ref[at], gain, acc_ref[:, at], mcot_ref[:, at])
+            in_share.begin(i)
         put(0, gc_ref[...] / gain)
         gains.begin()
-        own_ref[0] = finish(tok_ref[...], gain, acc_ref[...], mcot_ref[...])
-        in_share.begin(0)
         for which, name, *d in LAST_STEPS:
             getattr(sums[which], name)(*d)
-        in_share.on(0)
-        for which in (rest, low, high):
-            which.along()
+        high.along()
         gains.hop(4)
         for which in (rest, low, high):
             which.end()
@@ -1069,51 +1079,57 @@
 
 
 SUM_STEPS = (
-    (-1, "rest", "chip", 2),
-    (-1, "rest", "cross", 2),
     (-1, "rest", "begin", 1, 0),
     (-1, "rest", "chip", 3),
-    (1, "rest", "chip", 1),
-    (1, "rest", "chip", 0),
+    (0, "rest", "cross", 3),
+    (0, "rest", "chip", 1),
+    (0, "rest", "chip", 0),
+    (1, "rest", "over", 2),
     (1, "out", "on", 0),
-    (2, "rest", "over", 2),
-    (2, "rest", "cross", 3),
-    (5, "rest", "over", 3),
-    (5, "rest", "cross", 1),
-    (8, "rest", "over", 1),
-    (8, "rest", "cross", 0),
+    (3, "rest", "cross", 1),
+    (4, "rest", "over", 3),
+    (6, "rest", "cross", 0),
+    (7, "rest", "over", 1),
     (9, "low", "begin", 2, 3, 1, 0),
     (10, "low", "chip", 2),
     (10, "low", "chip", 3),
     (10, "low", "chip", 1),
     (10, "low", "chip", 0),
-    (11, "rest", "over", 0),
-    (11, "low", "cross", 2),
-    (11, "low", "cross", 3),
+    (10, "low", "cross", 2),
+    (10, "low", "cross", 3),
+    (10, "low", "cross", 1),
+    (10, "low", "cross", 0),
+    (9, "rest", "over", 0),
+)
+FLUSH_STEPS = (
+    ("rest", "along"),
+    ("low", "over", 2),
+    ("low", "over", 3),
 )
 LAST_STEPS = (
     ("high", "chip", 2),
+    ("high", "cross", 2),
     ("high", "chip", 3),
+    ("high", "cross", 3),
     ("high", "chip", 1),
+    ("high", "cross", 1),
     ("high", "chip", 0),
-    ("low", "over", 2),
-    ("low", "cross", 1),
-    ("low", "over", 3),
-    ("low", "cross", 0),
+    ("high", "cross", 0),
     ("low", "over", 1),
-    ("high", "cross", 2),
-    ("high", "cross", 3),
     ("low", "over", 0),
     ("gains", "hop", 0),
     ("high", "over", 2),
-    ("high", "cross", 1),
-    ("high", "cross", 0),
+    ("in", "on", 0),
     ("gains", "hop", 1),
     ("high", "over", 3),
+    ("in", "on", 1),
     ("gains", "hop", 2),
     ("high", "over", 1),
+    ("low", "along"),
     ("gains", "hop", 3),
     ("high", "over", 0),
+    ("in", "on", 2),
+    ("in", "on", 3),
 )
 
 
@@ -1169,7 +1185,7 @@
         + Scatter.scratch(nz, (0,), depth, columns[0])
         + Scatter.scratch(nz, (1,), depth, columns[0])
         + Fold.scratch(n_mp, own, SLOTS)
-        + Share.sems(1)
+        + Share.sems(PIECES)
         + Share.sems(1)
         + Everyone.scratch(nz, 4 * nz),
         compiler_params=pltpu.CompilerParams(
@@ -1204,7 +1220,7 @@
     depth = d_qkv.shape[0]
     shape = lambda *s: jax.ShapeDtypeStruct(s, F32)
     shapes = [(3, depth, width), (width, depth), (depth, 2, units), (units, depth), (1, depth), (1, depth)]
-    steps = 4
+    steps = 2
     slab = pl.BlockSpec((rows // steps, features), lambda i: (i, 0))
     return pl.pallas_call(
         functools.partial(deliver_kernel, units),

time: 191 us -> 182 us (0.953)
  Pallas kernels: 190 us -> 181 us
    pallas_call x1, Pallas kernels: 110 us -> 102 us  [backward(): pl.pallas_call(functools.partial(backward_kernel, nz, units), grid=(heads...]
where the time goes in v7:
time: 182 us
  Pallas kernels  181 us (99%)
    pallas_call x1, Pallas kernels, backward(): pl.pallas_call(functools.partial(backward_kernel, nz, units), grid=(heads...  102 us
    pallas_call x1, Pallas kernels, forward(): pl.pallas_call(functools.partial(forward_kernel, nz, units), grid=(heads,...  72 us
    pallas_call x1, Pallas kernels, deliver(): pl.pallas_call(functools.partial(deliver_kernel, units), grid=(steps,), i...  6.58 us

profile of v7, /device:TPU:0, one launch (start us, length us, event | category | flops | bytes accessed | tf_op | source)
XLA Modules:
  0.0 181.8 jit_solution(4115269727916532695)
XLA Ops:
  0.6 72.0 %forward.1 = (bf16[768,512]{1,0:T(8,128)(2,1)}, bf16[768,512]{1,0:T(8,128)(2,1)}, bf16[768,2048]{1,0:T(8,128)(2,1)}, bf16[768,2048]{1,0:T(8,128)(2,1)}, f32[32,2...) custom-call(s32[1,8]{1,0:T(1,128)} %refs_0_.1, ...), custom_call_target="tpu_custom_call" | custom-call | tf_op jit(solution)/shard_map/forward/pallas_call | solution.py:737
  72.7 102.4 %backward.1 = (f32[96,768]{1,0:T(8,128)}, f32[96,864]{1,0:T(8,128)}, f32[2,96]{1,0:T(2,128)}, bf16[2048,768]{1,0:T(8,128)(2,1)}, bf16[2048,768]{1,0:T(8,128)(2,1)}) custom-call(s32[1,8]{1,0:T(1,128)} %refs_0_.1, bf16[768,512]{1,0:T(8,128)(2,1)} %get-tuple-element.33.refs_1_, bf16[768,2048]{1,0:T(8,128)(2,1)} %get-tuple-element.34.refs_2_, ...), custom_call_target="tpu_custom_call" | custom-call | tf_op jit(solution)/shard_map/backward/pallas_call | solution.py:1148
  175.0 6.6 %deliver.1 = (f32[2048,768]{1,0:T(8,128)}, bf16[2048,768]{1,0:T(8,128)(2,1)}, f32[3,96,192]{2,1,0:T(8,128)}, f32[192,96]{1,0:T(8,128)}, f32[96,2,288]{2,1,0:T(2,...) custom-call(bf16[2048,768]{1,0:T(8,128)(2,1)} %get-tuple-element.45.in_ref, ...), custom_call_target="tpu_custom_call" | custom-call | tf_op jit(solution)/shard_map/deliver/pallas_call | solution.py:1225

commit v8 on v7

--- a/solution.py
+++ b/solution.py
@@ -469,39 +469,63 @@
 
 
 class Everyone:
-    def __init__(self, held, got, send, recv):
-        self.held, self.got, self.send, self.recv = held, got, send, recv
-        self.hops = got.shape[0]
+    def __init__(self, held, near, full, far, send, recv):
+        self.held, self.near, self.full, self.far, self.send, self.recv = held, near, full, far, send, recv
+        self.group, self.owners = near.shape[0], far.shape[0]
 
     @staticmethod
-    def scratch(nz, rows):
-        hops = 3 + nz.bit_length() - 1
+    def scratch(n_mp, n_dp):
         dma = pltpu.SemaphoreType.DMA
-        return [pltpu.VMEM((hops + 1, rows, 128), F32), pltpu.VMEM((hops, rows, 128), F32), dma((hops,)), dma((hops,))]
-
-    def message(self, i):
-        z, x, y, c = place()
-        target = (
-            device(z, x, y, 1 - c) if i == 0
-            else device(z, x, 1 - y, c) if i == 1
-            else device(z, 1 - x, y, c) if i == 2
-            else device(lax.bitwise_xor(z, 1 << (i - 3)), x, y, c)
-        )
-        return remote(self.held.at[i], self.got.at[i], self.send.at[i], self.recv.at[i], target)
+        blocks = pltpu.VMEM((n_dp, 8, 128), F32)
+        count = n_mp + n_dp
+        return [blocks, pltpu.VMEM((n_mp, n_dp, 8, 128), F32), blocks, blocks, dma((count,)), dma((count,))]
+
+    @staticmethod
+    def peers(n_mp, n_dp):
+        dp, mp = lax.axis_index("dp"), lax.axis_index("mp")
+        return [(dp, lax.bitwise_xor(mp, k)) for k in range(1, n_mp)] + [
+            (lax.bitwise_xor(dp, k), mp) for k in range(1, n_dp)
+        ]
+
+    def within(self, k):
+        dp, mp = lax.axis_index("dp"), lax.axis_index("mp")
+        sems = self.send.at[k], self.recv.at[k]
+        return remote(self.held, self.near.at[mp], *sems, (dp, lax.bitwise_xor(mp, k)))
+
+    def owner(self, k):
+        dp, mp = lax.axis_index("dp"), lax.axis_index("mp")
+        other = lax.bitwise_xor(dp, k)
+        sems = self.send.at[self.group + k], self.recv.at[self.group + k]
+        return remote(self.full.at[other], self.far.at[dp], *sems, (other, mp))
 
     def begin(self):
-        self.message(0).start()
-
-    def hop(self, i):
-        self.message(i).wait_recv()
-        self.held[i + 1] = self.held[i] + self.got[i]
-        if i + 1 < self.hops:
-            self.message(i + 1).start()
+        for k in range(1, self.group):
+            self.within(k).start()
+        self.near[lax.axis_index("mp")] = self.held[...]
+
+    def pass_on(self):
+        for k in range(1, self.group):
+            self.within(k).wait_recv()
+        made = self.near[0]
+        for i in range(1, self.group):
+            made += self.near[i]
+        self.full[...] = made
+        for k in range(1, self.owners):
+            self.owner(k).start()
+        dp = lax.axis_index("dp")
+        self.far[dp] = self.full[dp]
 
     def end(self):
-        for i in range(self.hops):
-            self.message(i).wait_send()
-        return self.held[self.hops]
+        for k in range(1, self.owners):
+            self.owner(k).wait_recv()
+        made = self.far[0]
+        for i in range(1, self.owners):
+            made += self.far[i]
+        for k in range(1, self.group):
+            self.within(k).wait_send()
+        for k in range(1, self.owners):
+            self.owner(k).wait_send()
+        return made
 
 
 class Fold:
@@ -934,7 +958,7 @@
     fold = Fold(*refs[18:23])
     in_share = Share(own_ref.at[0], in_full, *refs[23:26], PIECES)
     out_share = Share(own_ref.at[1], out_full, *refs[26:29])
-    gains = Everyone(*refs[29:33])
+    gains = Everyone(*refs[29:35])
     step, heads = pl.program_id(0) - 1, pl.num_programs(0) - 1
     parts = wa_ref.shape[0]
     features, own = n1_ref.shape
@@ -945,12 +969,12 @@
     mine = pl.ds(pl.multiple_of(me * own, own), own)
     late = pltpu.make_async_copy(wb_hbm, wb_ref, load.at[3])
     three = 3 * HDIM
-    shards = features // gains_ref.shape[1]
+    depth = gains_ref.shape[1]
+    shards = features // depth
 
     def put(row, column):
         for i in range(shards):
-            at = row * shards + i
-            gains.held[0, at : at + 1, : features // shards] = column[i * (features // shards) : (i + 1) * (features // shards)].T
+            gains.held[i, row : row + 1, :depth] = column[i * depth : (i + 1) * depth].T
 
     @pl.when(step < 0)
     def _():
@@ -962,7 +986,7 @@
         ]
         for copy in loads:
             copy.start()
-        greet(peers(nz))
+        greet(Everyone.peers(parts, 2 * nz))
         for copy in loads:
             copy.wait()
         late.start()
@@ -1053,29 +1077,21 @@
                 close((step - back) // per)
         high.begin(2, 3, 1, 0)
         gain = wa_ref[0, :, three : three + 1].astype(F32)
+        put(0, gc_ref[...] / gain)
+        gains.begin()
         size = own // PIECES
         for i in range(PIECES):
             at = slice(i * size, (i + 1) * size)
             own_ref[0, at] = finish(tok_ref[at], gain, acc_ref[:, at], mcot_ref[:, at])
             in_share.begin(i)
-        put(0, gc_ref[...] / gain)
-        gains.begin()
         for which, name, *d in LAST_STEPS:
             getattr(sums[which], name)(*d)
         high.along()
-        gains.hop(4)
         for which in (rest, low, high):
             which.end()
         out_share.end()
         in_share.end()
-        made = gains.end()
-        dp = lax.axis_index("dp")
-        for row in range(2):
-            for i in range(shards):
-
-                @pl.when(dp == i)
-                def _():
-                    gains_ref[row : row + 1] = made[row * shards + i : row * shards + i + 1, : features // shards]
+        gains_ref[...] = gains.end()[:2, :depth]
 
 
 SUM_STEPS = (
@@ -1117,16 +1133,13 @@
     ("high", "cross", 0),
     ("low", "over", 1),
     ("low", "over", 0),
-    ("gains", "hop", 0),
+    ("gains", "pass_on"),
     ("high", "over", 2),
     ("in", "on", 0),
-    ("gains", "hop", 1),
     ("high", "over", 3),
     ("in", "on", 1),
-    ("gains", "hop", 2),
     ("high", "over", 1),
     ("low", "along"),
-    ("gains", "hop", 3),
     ("high", "over", 0),
     ("in", "on", 2),
     ("in", "on", 3),
@@ -1187,7 +1200,7 @@
         + Fold.scratch(n_mp, own, SLOTS)
         + Share.sems(PIECES)
         + Share.sems(1)
-        + Everyone.scratch(nz, 4 * nz),
+        + Everyone.scratch(n_mp, 2 * nz),
         compiler_params=pltpu.CompilerParams(
             dimension_semantics=("arbitrary",), collective_id=3, has_side_effects=True, vmem_limit_bytes=VMEM_BYTES
         ),

time: 182 us -> 177 us (0.973)
  Pallas kernels: 181 us -> 176 us
    pallas_call x1, Pallas kernels: 102 us -> 97.6 us  [backward(): pl.pallas_call(functools.partial(backward_kernel, nz, units), grid=(heads...]
where the time goes in v8:
time: 177 us
  Pallas kernels  176 us (99%)
    pallas_call x1, Pallas kernels, backward(): pl.pallas_call(functools.partial(backward_kernel, nz, units), grid=(heads...  97.6 us
    pallas_call x1, Pallas kernels, forward(): pl.pallas_call(functools.partial(forward_kernel, nz, units), grid=(heads,...  72 us
    pallas_call x1, Pallas kernels, deliver(): pl.pallas_call(functools.partial(deliver_kernel, units), grid=(steps,), i...  6.58 us

profile of v8, /device:TPU:0, one launch (start us, length us, event | category | flops | bytes accessed | tf_op | source)
XLA Modules:
  0.0 177.0 jit_solution(4399305970841286521)
XLA Ops:
  0.6 72.0 %forward.1 = (bf16[768,512]{1,0:T(8,128)(2,1)}, bf16[768,512]{1,0:T(8,128)(2,1)}, bf16[768,2048]{1,0:T(8,128)(2,1)}, bf16[768,2048]{1,0:T(8,128)(2,1)}, f32[32,2...) custom-call(s32[1,8]{1,0:T(1,128)} %refs_0_.1, ...), custom_call_target="tpu_custom_call" | custom-call | tf_op jit(solution)/shard_map/forward/pallas_call | solution.py:761
  72.7 97.6 %backward.1 = (f32[96,768]{1,0:T(8,128)}, f32[96,864]{1,0:T(8,128)}, f32[2,96]{1,0:T(2,128)}, bf16[2048,768]{1,0:T(8,128)(2,1)}, bf16[2048,768]{1,0:T(8,128)(2,1)}) custom-call(s32[1,8]{1,0:T(1,128)} %refs_0_.1, bf16[768,512]{1,0:T(8,128)(2,1)} %get-tuple-element.33.refs_1_, bf16[768,2048]{1,0:T(8,128)(2,1)} %get-tuple-element.34.refs_2_, ...), custom_call_target="tpu_custom_call" | custom-call | tf_op jit(solution)/shard_map/backward/pallas_call | solution.py:1161
  170.3 6.6 %deliver.1 = (f32[2048,768]{1,0:T(8,128)}, bf16[2048,768]{1,0:T(8,128)(2,1)}, f32[3,96,192]{2,1,0:T(8,128)}, f32[192,96]{1,0:T(8,128)}, f32[96,2,288]{2,1,0:T(2,...) custom-call(bf16[2048,768]{1,0:T(8,128)(2,1)} %get-tuple-element.45.in_ref, ...), custom_call_target="tpu_custom_call" | custom-call | tf_op jit(solution)/shard_map/deliver/pallas_call | solution.py:1238

commit v9 on v8

--- a/solution.py
+++ b/solution.py
@@ -576,13 +576,13 @@
         return made.astype(BF16)
 
 
-def forward_kernel(nz, units, len_ref, tok_ref, *refs):
+def forward_kernel(nz, units, len_ref, tok_hbm, *refs):
     linked = nz > 0
     given, refs = refs[: 6 if linked else 2], refs[6 if linked else 2 :]
     mine_ref, q_ref, k_ref, v_ref, cos_ref, sin_ref, o_ref, p_ref, inv_ref = refs[:9]
     full_refs, refs = refs[9 : 12 if linked else 9], refs[12 if linked else 9 :]
-    wa_ref, wb_ref, w_ref, n1_ref, ka_ref, qa_ref, va_ref, stat_ref, load = refs[:9]
-    refs = refs[9:]
+    wa_ref, wb_ref, w_ref, n1_ref, ka_ref, qa_ref, va_ref, stat_ref, tok_ref, load = refs[:10]
+    refs = refs[10:]
     rows, features = tok_ref.shape
     own = q_ref.shape[1]
     docs = len_ref.shape[1]
@@ -605,6 +605,8 @@
 
     @pl.when(step == 0)
     def _():
+        bring = pltpu.make_async_copy(tok_hbm, tok_ref, load.at[2])
+        bring.start()
         if linked:
             wq_ref, wg_ref, wo_ref, wd_ref, one_ref, two_ref = given
             for i in range(3):
@@ -652,6 +654,7 @@
 
         if linked:
             one.all_along()
+        bring.wait()
         lax.fori_loop(0, rows // own, measure, 0)
         if linked:
             one.all_over()
@@ -761,7 +764,7 @@
     return pl.pallas_call(
         functools.partial(forward_kernel, nz, units),
         grid=(heads,),
-        in_specs=[pl.BlockSpec(memory_space=pltpu.SMEM), vm] + ([vm] * 6 if linked else [hbm] * 2),
+        in_specs=[pl.BlockSpec(memory_space=pltpu.SMEM), hbm] + ([vm] * 6 if linked else [hbm] * 2),
         out_specs=[
             whole(features, own),
             pl.BlockSpec((HDIM, own), row),
@@ -795,7 +798,8 @@
             pltpu.VMEM((AUG, own), BF16),
             pltpu.VMEM((AUG, rows), BF16),
             pltpu.VMEM((8, rows), F32),
-            dma((2,)),
+            pltpu.VMEM((rows, features), BF16),
+            dma((3,)),
         ]
         + (
             [pltpu.VMEM((depth, c), BF16) for c in columns] + [dma((n,)), dma((n,)), dma] * 3

time: 177 us -> 176 us (level)
  no operation moved by 1% of the time
where the time goes in v9:
time: 176 us
  Pallas kernels  175 us (99%)
    pallas_call x1, Pallas kernels, backward(): pl.pallas_call(functools.partial(backward_kernel, nz, units), grid=(heads...  97.6 us
    pallas_call x1, Pallas kernels, forward(): pl.pallas_call(functools.partial(forward_kernel, nz, units), grid=(heads,...  71 us
    pallas_call x1, Pallas kernels, deliver(): pl.pallas_call(functools.partial(deliver_kernel, units), grid=(steps,), i...  6.58 us

profile of v9, /device:TPU:0, one launch (start us, length us, event | category | flops | bytes accessed | tf_op | source)
XLA Modules:
  0.0 176.0 jit_solution(33021328962404803)
XLA Ops:
  0.6 71.0 %forward.1 = (bf16[768,512]{1,0:T(8,128)(2,1)}, bf16[768,512]{1,0:T(8,128)(2,1)}, bf16[768,2048]{1,0:T(8,128)(2,1)}, bf16[768,2048]{1,0:T(8,128)(2,1)}, f32[32,2...) custom-call(s32[1,8]{1,0:T(1,128)} %refs_0_.1, ...), custom_call_target="tpu_custom_call" | custom-call | tf_op jit(solution)/shard_map/forward/pallas_call | solution.py:764
  71.7 97.6 %backward.1 = (f32[96,768]{1,0:T(8,128)}, f32[96,864]{1,0:T(8,128)}, f32[2,96]{1,0:T(2,128)}, bf16[2048,768]{1,0:T(8,128)(2,1)}, bf16[2048,768]{1,0:T(8,128)(2,1)}) custom-call(s32[1,8]{1,0:T(1,128)} %refs_0_.1, bf16[768,512]{1,0:T(8,128)(2,1)} %get-tuple-element.33.refs_1_, bf16[768,2048]{1,0:T(8,128)(2,1)} %get-tuple-element.34.refs_2_, ...), custom_call_target="tpu_custom_call" | custom-call | tf_op jit(solution)/shard_map/backward/pallas_call | solution.py:1165
  169.3 6.6 %deliver.1 = (f32[2048,768]{1,0:T(8,128)}, bf16[2048,768]{1,0:T(8,128)(2,1)}, f32[3,96,192]{2,1,0:T(8,128)}, f32[192,96]{1,0:T(8,128)}, f32[96,2,288]{2,1,0:T(2,...) custom-call(bf16[2048,768]{1,0:T(8,128)(2,1)} %get-tuple-element.45.in_ref, ...), custom_call_target="tpu_custom_call" | custom-call | tf_op jit(solution)/shard_map/deliver/pallas_call | solution.py:1242

commit v10 on v9

--- a/solution.py
+++ b/solution.py
@@ -189,11 +189,15 @@
     )
 
 
-def greet(targets):
+def hail(targets):
     barrier = pltpu.get_barrier_semaphore()
     for target in targets:
         pl.semaphore_signal(barrier, inc=1, device_id=target, device_id_type=pl.DeviceIdType.MESH)
-    pl.semaphore_wait(barrier, len(targets))
+
+
+def greet(targets):
+    hail(targets)
+    pl.semaphore_wait(pltpu.get_barrier_semaphore(), len(targets))
 
 
 def peers(nz):
@@ -609,13 +613,14 @@
         bring.start()
         if linked:
             wq_ref, wg_ref, wo_ref, wd_ref, one_ref, two_ref = given
+            hail(peers(nz))
             for i in range(3):
                 srcs[0][:, i * HDIM : (i + 1) * HDIM] = wq_ref[i, :, :HDIM]
             srcs[0][:, three : three + 1] = one_ref[...].astype(F32).T.astype(BF16)
             srcs[0][:, three + 1 : three + 2] = two_ref[...].astype(F32).T.astype(BF16)
             down = wd_ref[...].T
             srcs[0][:, 256 - units % 128 :] = down[:, units - units % 128 :]
-            greet(peers(nz))
+            pl.semaphore_wait(pltpu.get_barrier_semaphore(), len(peers(nz)))
             one.begin()
             for r in range(1, wq_ref.shape[2] // HDIM):
                 for i in range(3):

time: 176 us -> 176 us (level)
  no operation moved by 1% of the time
where the time goes in v10:
time: 176 us
  Pallas kernels  175 us (99%)
    pallas_call x1, Pallas kernels, backward(): pl.pallas_call(functools.partial(backward_kernel, nz, units), grid=(heads...  97.6 us
    pallas_call x1, Pallas kernels, forward(): pl.pallas_call(functools.partial(forward_kernel, nz, units), grid=(heads,...  70.8 us
    pallas_call x1, Pallas kernels, deliver(): pl.pallas_call(functools.partial(deliver_kernel, units), grid=(steps,), i...  6.58 us

profile of v10, /device:TPU:0, one launch (start us, length us, event | category | flops | bytes accessed | tf_op | source)
XLA Modules:
  0.0 175.8 jit_solution(17265985119427811329)
XLA Ops:
  0.6 70.8 %forward.1 = (bf16[768,512]{1,0:T(8,128)(2,1)}, bf16[768,512]{1,0:T(8,128)(2,1)}, bf16[768,2048]{1,0:T(8,128)(2,1)}, bf16[768,2048]{1,0:T(8,128)(2,1)}, f32[32,2...) custom-call(s32[1,8]{1,0:T(1,128)} %refs_0_.1, ...), custom_call_target="tpu_custom_call" | custom-call | tf_op jit(solution)/shard_map/forward/pallas_call | solution.py:769
  71.5 97.6 %backward.1 = (f32[96,768]{1,0:T(8,128)}, f32[96,864]{1,0:T(8,128)}, f32[2,96]{1,0:T(2,128)}, bf16[2048,768]{1,0:T(8,128)(2,1)}, bf16[2048,768]{1,0:T(8,128)(2,1)}) custom-call(s32[1,8]{1,0:T(1,128)} %refs_0_.1, bf16[768,512]{1,0:T(8,128)(2,1)} %get-tuple-element.33.refs_1_, bf16[768,2048]{1,0:T(8,128)(2,1)} %get-tuple-element.34.refs_2_, ...), custom_call_target="tpu_custom_call" | custom-call | tf_op jit(solution)/shard_map/backward/pallas_call | solution.py:1170
  169.1 6.6 %deliver.1 = (f32[2048,768]{1,0:T(8,128)}, bf16[2048,768]{1,0:T(8,128)(2,1)}, f32[3,96,192]{2,1,0:T(8,128)}, f32[192,96]{1,0:T(8,128)}, f32[96,2,288]{2,1,0:T(2,...) custom-call(bf16[2048,768]{1,0:T(8,128)(2,1)} %get-tuple-element.45.in_ref, ...), custom_call_target="tpu_custom_call" | custom-call | tf_op jit(solution)/shard_map/deliver/pallas_call | solution.py:1247
